TPU v7x, 512 devices: a whole 4x8x8 slice. The times are simulated.
512 devices in a mesh: tensor: 4 (over y_hi, core), fsdp: 8 (over z), replica: 16 (over y_lo, x).
Axes of the slice: x: 4, y: 8 (y_hi: 2, y_lo: 4; y = y_hi * 4 + y_lo), z: 8, core: 2. Of those that a mesh axis runs over, the one named last changes fastest.
Arguments:
- activations: bfloat16 [16, 1536, 8192], P('replica', 'fsdp', 'tensor'), may hold values from -6 to 6
- cotangents: bfloat16 [16, 1536, 2, 1024], P('replica', 'fsdp', None, 'tensor'), may hold values from -0.15234375 to 0.15234375
- inner_drift: float32 [16, 8192, 2, 1024], P('replica', ('tensor', 'fsdp')), may hold values from -6 to 6
- drift_flags: int32 [16, 2], P('replica'), may hold values 0 or 1
- master_weights: float32 [8192, 2, 1024], P(('tensor', 'fsdp', 'replica')), may hold values from -3 to 3
- outer_momentum: float32 [8192, 2, 1024], P(('tensor', 'fsdp', 'replica')), may hold values from -3 to 3
Outputs:
- new_master: float32 [8192, 2, 1024], P(('tensor', 'fsdp', 'replica'))
- new_momentum: float32 [8192, 2, 1024], P(('tensor', 'fsdp', 'replica'))
- fresh_copy: bfloat16 [8192, 2, 1024], P(('tensor', 'fsdp'))
All inputs are finite; a program needn't handle non-finite values. No bound on the sum of `drift_flags` on one device may be relied on, other than what follows from the above.
Results may differ from a plain program's by a relative error of at most 0.001.
Values may be sent and summed in bfloat16 or wider, within the bound.
No kernel may reach another device: no remote copies, remote signals or barrier semaphores. Data moves between devices by JAX's collectives and lax.ppermute only.
A program may use at most 64 MiB of HBM per device.

v0:
```python
import jax
import jax.numpy as jnp
from jax import lax
from jax.sharding import PartitionSpec as P

inner_rate = 0.8
momentum_decay = 0.9
outer_rate = 0.7


def body(activations, cotangents, inner_drift, drift_flags, master_weights, outer_momentum):
    replicas = lax.axis_size("replica")
    own_rows = master_weights.shape[0]
    weighting = drift_flags[0].astype(jnp.float32)[None, :, None]
    columns = lax.all_to_all(activations, "fsdp", split_axis=2, concat_axis=1, tiled=True)[0]
    all_heads = lax.all_gather(cotangents, "tensor", axis=3, tiled=True)[0]
    width = all_heads.shape[1] * all_heads.shape[2]
    portion = lax.all_gather(all_heads, "fsdp", axis=0, tiled=True)
    count = portion.shape[0]
    summed = lax.dot_general(
        columns,
        portion.reshape(count, width),
        (((0,), (0,)), ((), ())),
        preferred_element_type=jnp.float32,
    )
    whole_sum = lax.psum(
        weighting
        * (
            inner_drift[0]
            + inner_rate * summed.reshape(columns.shape[1], all_heads.shape[1], all_heads.shape[2])
        ),
        "replica",
    )
    drift_sum = lax.dynamic_slice_in_dim(
        whole_sum, lax.axis_index("replica") * own_rows, own_rows, 0
    )
    delta = drift_sum / replicas
    new_momentum = momentum_decay * outer_momentum + delta
    new_master = master_weights - outer_rate * (delta + momentum_decay * new_momentum)
    fresh_copy = lax.all_gather(new_master.astype(jnp.bfloat16), "replica", axis=0, tiled=True)
    return (new_master, new_momentum, fresh_copy)


def solution(mesh):
    return jax.shard_map(
        body,
        mesh=mesh,
        in_specs=(
            P("replica", "fsdp", "tensor"),
            P("replica", "fsdp", None, "tensor"),
            P("replica", ("tensor", "fsdp"), None, None),
            P("replica", None),
            P(("tensor", "fsdp", "replica"), None, None),
            P(("tensor", "fsdp", "replica"), None, None),
        ),
        out_specs=(
            P(("tensor", "fsdp", "replica"), None, None),
            P(("tensor", "fsdp", "replica"), None, None),
            P(("tensor", "fsdp"), None, None),
        ),
        check_vma=False,
    )
```

profile of v0, /device:TPU:2, one launch (start us, length us, event | category | flops | bytes accessed | tf_op | source)
XLA Modules:
  0.0 412.5 jit_solution(7104150623678873050)
XLA Ops:
  7.2 0.0 all-gather.6.cloned.1.call-start
  7.2 19.1 %all_gather.9 = bf16[1,192,2,1024]{3,2,0,1:T(2,128)(2,1)} all-gather(bf16[1,192,2,256]{3,2,0,1:T(2,128)(2,1)} %bitcast.35), channel_id=1, replica_groups=mesh['tensor'=4,'fsdp'=8,'replica'=16] {'tensor'}, dimensions={3}, use_global_device_ids=true | all-gather | bytes 983040 | tf_op jit(solution)/shard_map/all_gather | solution.py:16
  26.4 1.7 copy.35
  28.1 0.5 broadcast.9
  28.6 11.6 %reduce = bf16[2048,192]{1,0:T(8,128)(2,1)S(1)} reduce(bf16[2048,1,192]{2,1,0:T(2,128)(2,1)S(1)} %bitcast.30, bf16[]{:T(256)} %broadcast.9), dimensions={1}, to_apply=%bitcast.26.reduce_sub_computation | reduce | bytes 1572866
  40.2 2.1 reshape.22
  42.3 10.3 %all-to-all-start = ((bf16[8,2,24576]{2,1,0:T(2,128)(2,1)}), bf16[8,2,24576]{2,1,0:T(2,128)(2,1)S(1)}, u32[]{:S(2)}, u32[]{:S(2)}) async-start(bf16[8,2,24576]{2,1,0:T(2,128)(2,1)} %reshape.22), calls=%async_computation | async-start | bytes 1572864 | tf_op jit(solution)/shard_map/all_to_all | solution.py:15
  52.6 0.0 all-reduce.2.cloned.1.call-start
  52.7 32.3 %all-to-all-done = bf16[8,2,24576]{2,1,0:T(2,128)(2,1)S(1)} async-done(((bf16[8,2,24576]{2,1,0:T(2,128)(2,1)}), bf16[8,2,24576]{2,1,0:T(2,128)(2,1)S(1)}, u32[]{:S(2)}, u32[]{:S(2)}) %all-to-all-start) | async-done | bytes 786464 | tf_op jit(solution)/shard_map/all_to_all | solution.py:15
  85.0 1.5 reshape.23
  86.5 1.2 copy.36
  87.7 0.2 copy.49
  87.9 0.1 bitcast_bitcast_fusion
  88.0 0.2 copy.37
  88.1 35.8 %all-gather.6.cloned.1.call-done = bf16[1,1536,2,1024]{3,2,0,1:T(2,128)(2,1)} async-done(((bf16[1,192,2,1024]{3,2,0,1:T(2,128)(2,1)}), bf16[1,1536,2,1024]{3,2,0,1:T(2,128)(2,1)}) %all-gather.6.cloned.1.call-update) | async-done | bytes 6291472 | tf_op jit(solution)/shard_map/all_gather | solution.py:18
  124.0 16.2 %copy.48 = bf16[1,1536,2,1024]{1,3,2,0:T(8,128)(2,1)} copy(bf16[1,1536,2,1024]{3,2,0,1:T(2,128)(2,1)} %all-gather.6.cloned.1.call-done) | data formatting | bytes 12582912 | tf_op jit(solution)/shard_map/reshape | solution.py:22
  140.1 6.7 %fusion.2 = f32[256,2,1024]{2,0,1:T(8,128)} fusion(f32[1,256,2,1024]{3,2,1,0:T(2,128)S(1)} %copy-done.3, bf16[1536,256,1]{1,0,2:T(8,128)(2,1)S(1)} %bitcast.34, bf16[1,1536,2,1024]{1,3,2,0:T(8,128)(2,1)} %copy.48, f32[2]{0:T(128)S(1)} %convert_bitcast_fusion), kind=kOutput, calls=%fused_computation.3 | convolution fusion | flops 1612185600 | bytes 11272200 | tf_op jit(solution)/shard_map/dot_general | solution.py:20
  146.9 0.0 all-gather.4.cloned.1.call-start
  147.0 170.7 %all-reduce.2.cloned.1.call-done = f32[256,2,1024]{2,0,1:T(8,128)} async-done(((f32[256,2,1024]{2,0,1:T(8,128)}), f32[256,2,1024]{2,0,1:T(8,128)}) %all-reduce.2.cloned.1.call-update) | async-done | bytes 2097168 | tf_op jit(solution)/shard_map/psum | solution.py:26
  317.6 1.6 fusion.6
  319.3 0.8 copy.43
  320.1 0.8 copy.44
  320.8 81.9 %all-gather.4.cloned.1.call-done = bf16[256,2,1024]{2,0,1:T(8,128)(2,1)} async-done(((bf16[16,2,1024]{2,0,1:T(8,128)(2,1)}), bf16[256,2,1024]{2,0,1:T(8,128)(2,1)}) %all-gather.4.cloned.1.call-update) | async-done | bytes 1048592 | tf_op jit(solution)/shard_map/all_gather | solution.py:40
  402.7 3.3 copy.45
  (14 shorter events, 0.1 us)
Async XLA Ops:
  7.2 19.2 %copy-start = (bf16[1,192,2048]{2,1,0:T(8,128)(2,1)S(1)}, bf16[1,192,2048]{2,1,0:T(8,128)(2,1)}, u32[]{:S(2)}) copy-start(bf16[1,192,2048]{2,1,0:T(8,128)(2,1)} %param.6) | copy-start | bytes 2359300
  7.2 116.8 %all-gather.6.cloned.1.call-start = ((), (), s32[]{:S(2)}) async-start(), calls=%async_computation.3 | async-start | bytes 7077888 | tf_op jit(solution)/shard_map/all_gather | solution.py:18
  40.2 12.4 %copy-start.4 = (s32[1,2]{1,0:T(1,128)S(1)}, s32[1,2]{1,0:T(1,128)}, u32[]{:S(2)}) copy-start(s32[1,2]{1,0:T(1,128)} %param.9) | copy-start | bytes 28
  42.3 42.7 %all-to-all-start = ((bf16[8,2,24576]{2,1,0:T(2,128)(2,1)}), bf16[8,2,24576]{2,1,0:T(2,128)(2,1)S(1)}, u32[]{:S(2)}, u32[]{:S(2)}) async-start(bf16[8,2,24576]{2,1,0:T(2,128)(2,1)} %reshape.22), calls=%async_computation | async-start | bytes 1572864 | tf_op jit(solution)/shard_map/all_to_all | solution.py:15
  52.6 265.0 %all-reduce.2.cloned.1.call-start = ((), (), s32[]{:S(2)}) async-start(), calls=%async_computation.1 | async-start | bytes 4194304 | tf_op jit(solution)/shard_map/psum | solution.py:26
  88.1 52.0 %copy-start.3 = (f32[1,256,2,1024]{3,2,1,0:T(2,128)S(1)}, f32[1,256,2,1024]{3,2,1,0:T(2,128)}, u32[]{:S(2)}) copy-start(f32[1,256,2,1024]{3,2,1,0:T(2,128)} %param.8) | copy-start | bytes 6291460
  146.9 170.8 %copy-start.1 = (f32[16,2,1024]{2,1,0:T(2,128)S(1)}, f32[16,2,1024]{2,1,0:T(2,128)}, u32[]{:S(2)}) copy-start(f32[16,2,1024]{2,1,0:T(2,128)} %param.10) | copy-start | bytes 393220
  146.9 170.8 %copy-start.2 = (f32[16,2,1024]{2,1,0:T(2,128)S(1)}, f32[16,2,1024]{2,1,0:T(2,128)}, u32[]{:S(2)}) copy-start(f32[16,2,1024]{2,1,0:T(2,128)} %param.11) | copy-start | bytes 393220
  146.9 255.8 %all-gather.4.cloned.1.call-start = ((), (), s32[]{:S(2)}) async-start(), calls=%async_computation.2 | async-start | bytes 1114112 | tf_op jit(solution)/shard_map/all_gather | solution.py:40
Sparse Core Ops, SparseCore 0:
  26.5 97.4 all-gather.5
  147.0 170.5 all-reduce.1
  320.3 82.3 all-gather.3
where the time goes:
time: 413 us; the launch traced here: 412 us
  waiting for transfers between devices  321 us (78%)
  local copies, waits for them, and re-layouts  28.3 us (7%)
  blocking collectives  19.1 us (5%)
  between operations  13.9 us (3%)
  other arithmetic  13.3 us (3%)
  starting transfers between devices  10.4 us (3%)
  matrix products  6.75 us (2%)
    psum x1, waiting for transfers between devices, body(): lax.psum(weighting * (inner_drift[0] + inner_rate * summed.reshape(column...  171 us
    all_gather x1, waiting for transfers between devices, body(): lax.all_gather(new_master.astype(jnp.bfloat16), 'replica', axis=0, tiled=...  81.9 us
    all_gather x1, waiting for transfers between devices, body(): portion = lax.all_gather(all_heads, 'fsdp', axis=0, tiled=True)  35.8 us
    all_to_all x1, waiting for transfers between devices, body(): lax.all_to_all(activations, 'fsdp', split_axis=2, concat_axis=1, tiled=True)  32.3 us
    all_gather x1, blocking collectives, body(): all_heads = lax.all_gather(cotangents, 'tensor', axis=3, tiled=True)[0]  19.1 us
    reshape x1, local copies, waits for them, and re-layouts, body(): portion.reshape(count, width)  16.2 us
    unnamed x1, other arithmetic  11.6 us
    unnamed x18, local copies, waits for them, and re-layouts  10.7 us
  transfers between devices with their start and end apart: 4, of which 4 were waited for; matrix products, arithmetic and copies ran while one was open for 5% of the time, Pallas kernels for 0%

commit v1 on v0

v1 whole, which is shorter than its diff:
```python
import jax
import jax.numpy as jnp
from jax import lax
from jax.sharding import Mesh, PartitionSpec as P

inner_rate = 0.8
momentum_decay = 0.9
outer_rate = 0.7

f32, f16, bf16 = jnp.float32, jnp.float16, jnp.bfloat16


def body(activations, cotangents, inner_drift, drift_flags, master_weights, outer_momentum):
    n_yh, n_core, n_z, n_yl, n_x = (lax.axis_size(a) for a in ("yh", "core", "z", "yl", "x"))
    replicas = n_yl * n_x
    core = lax.axis_index("core")
    tokens, width = activations.shape[1], activations.shape[2]
    heads = cotangents.shape[3]
    own_rows = master_weights.shape[0]
    rows, kvw = inner_drift.shape[1], inner_drift.shape[3]

    by_k = cotangents[0].swapaxes(0, 1)[None]
    by_k = jnp.broadcast_to(by_k, (n_yh, 2, tokens, heads)).reshape(n_yh * 2, tokens, heads)
    parts = lax.all_to_all(by_k, ("yh", "core"), 0, 0, tiled=True)
    mine = parts.swapaxes(0, 1).reshape(tokens, kvw)
    mine, acts, drift = lax.optimization_barrier((mine, activations[0], inner_drift[0]))
    portion = lax.all_gather(mine, "z", axis=0, tiled=True)

    acts = acts.reshape(tokens, n_z, rows).swapaxes(0, 1)
    acts = lax.all_to_all(acts, "z", 0, 0, tiled=True).reshape(n_z * tokens, rows)
    acts_pair = lax.all_to_all(jnp.broadcast_to(acts[None], (n_core,) + acts.shape), "core", 0, 0, tiled=True)

    drift_pair = lax.all_to_all(drift.swapaxes(0, 1), "core", 0, 0, tiled=True)

    flag = lax.dynamic_index_in_dim(drift_flags[0], core, 0, keepdims=False).astype(f32)
    grads = lax.dot_general(acts_pair, portion, (((1,), (0,)), ((), ())), preferred_element_type=f32)
    term = flag * (drift_pair + inner_rate * grads)

    sent = term.astype(f16).reshape(n_core, n_yl, n_x, own_rows, kvw).transpose(2, 0, 1, 3, 4)
    got = lax.all_to_all(sent, "x", 0, 0, tiled=True)
    half = got.astype(f32).sum(0).astype(f16).reshape(n_core * n_yl, own_rows, kvw)
    got = lax.all_to_all(half, ("core", "yl"), 0, 0, tiled=True)
    drift_sum = got.astype(f32).reshape(2, n_yl, own_rows, kvw).sum(1).swapaxes(0, 1)

    delta = drift_sum / replicas
    new_momentum = momentum_decay * outer_momentum + delta
    new_master = master_weights - outer_rate * (delta + momentum_decay * new_momentum)

    fresh = new_master.astype(bf16)
    fresh = jnp.broadcast_to(fresh[None], (n_yl, own_rows, 2, kvw))
    fresh = lax.all_to_all(fresh, "yl", 0, 0, tiled=True)
    fresh = jnp.broadcast_to(fresh[None], (n_x, n_yl, own_rows, 2, kvw))
    fresh = lax.all_to_all(fresh, "x", 0, 0, tiled=True)
    fresh_copy = fresh.swapaxes(0, 1).reshape(rows, 2, kvw)
    return (new_master, new_momentum, fresh_copy)


def solution(mesh):
    split = Mesh(mesh.devices.reshape(2, 2, 8, 4, 4), ("yh", "core", "z", "yl", "x"))
    tensor, replica = ("yh", "core"), ("yl", "x")
    return jax.shard_map(
        body,
        mesh=split,
        in_specs=(
            P(replica, "z", tensor),
            P(replica, "z", None, tensor),
            P(replica, tensor + ("z",), None, None),
            P(replica, None),
            P(tensor + ("z",) + replica, None, None),
            P(tensor + ("z",) + replica, None, None),
        ),
        out_specs=(
            P(tensor + ("z",) + replica, None, None),
            P(tensor + ("z",) + replica, None, None),
            P(tensor + ("z",), None, None),
        ),
        check_vma=False,
    )
```

time: 413 us -> 171 us (0.41)
  waiting for transfers between devices: 321 us -> 60.5 us
  blocking collectives: 19.1 us -> 48.6 us
  starting transfers between devices: 10.4 us -> 27.2 us
  local copies, waits for them, and re-layouts: 28.3 us -> 13.9 us
  other arithmetic: 13.3 us -> 1.02 us
    psum x1 -> x0, waiting for transfers between devices: 171 us -> none  [body(): lax.psum(weighting * (inner_drift[0] + inner_rate * summed.reshape(column...]
    all_gather x2 -> x1, waiting for transfers between devices: 118 us -> 7.95 us  [body(): portion = lax.all_gather(mine, 'z', axis=0, tiled=True)]
    all_to_all x0 -> x4, blocking collectives: none -> 48.6 us  [the longest x1 18 us: body(): got = lax.all_to_all(sent, 'x', 0, 0, tiled=True)]
    all_to_all x1 -> x4, waiting for transfers between devices: 32.3 us -> 52.5 us  [the longest x1 28.7 us: body(): lax.all_to_all(acts, 'z', 0, 0, tiled=True).reshape(n_z * tokens, rows)]
    all_gather x1 -> x0, blocking collectives: 19.1 us -> none  [body(): all_heads = lax.all_gather(cotangents, 'tensor', axis=3, tiled=True)[0]]
    all_to_all x1 -> x4, starting transfers between devices: 10.3 us -> 27.2 us  [the longest x1 10.3 us: body(): lax.all_to_all(acts, 'z', 0, 0, tiled=True).reshape(n_z * tokens, rows)]
    reshape x1 -> x2, local copies, waits for them, and re-layouts: 16.2 us -> 1.04 us  [the longest x1 0.78 us: body(): mine = parts.swapaxes(0, 1).reshape(tokens, kvw)]
    unnamed x1 -> x0, other arithmetic: 11.6 us -> none
  transfers between devices with their start and end apart: 4 -> 5, of which waited for: 4 -> 5; matrix products, arithmetic and copies ran while one was open for 5% -> 4% of each run, Pallas kernels for 0% -> 0%
where the time goes in v1:
time: 171 us; the launch traced here: 170 us
  waiting for transfers between devices  60.5 us (35%)
  blocking collectives  48.6 us (28%)
  starting transfers between devices  27.2 us (16%)
  between operations  14.2 us (8%)
  local copies, waits for them, and re-layouts  13.9 us (8%)
  matrix products  5.01 us (3%)
    all_to_all x1, waiting for transfers between devices, body(): lax.all_to_all(acts, 'z', 0, 0, tiled=True).reshape(n_z * tokens, rows)  28.7 us
    all_to_all x1, blocking collectives, body(): got = lax.all_to_all(sent, 'x', 0, 0, tiled=True)  18 us
    all_to_all x1, blocking collectives, body(): got = lax.all_to_all(half, ('core', 'yl'), 0, 0, tiled=True)  13.8 us
    all_to_all x1, blocking collectives, body(): fresh = lax.all_to_all(fresh, 'yl', 0, 0, tiled=True)  11.9 us
    all_to_all x1, waiting for transfers between devices, body(): fresh = lax.all_to_all(fresh, 'x', 0, 0, tiled=True)  11.6 us
    all_to_all x1, starting transfers between devices, body(): lax.all_to_all(acts, 'z', 0, 0, tiled=True).reshape(n_z * tokens, rows)  10.3 us
    all_to_all x1, waiting for transfers between devices, body(): parts = lax.all_to_all(by_k, ('yh', 'core'), 0, 0, tiled=True)  9.54 us
    all_gather x1, waiting for transfers between devices, body(): portion = lax.all_gather(mine, 'z', axis=0, tiled=True)  7.95 us
  transfers between devices with their start and end apart: 5, of which 5 were waited for; matrix products, arithmetic and copies ran while one was open for 4% of the time, Pallas kernels for 0%

profile of v1, /device:TPU:2, one launch (start us, length us, event | category | flops | bytes accessed | tf_op | source)
XLA Modules:
  0.0 170.4 jit_solution(8981948798312991612)
XLA Ops:
  7.2 0.9 copy.30
  8.1 0.8 broadcast_in_dim.10
  8.9 7.1 %all-to-all-start = ((bf16[4,192,256]{2,1,0:T(8,128)(2,1)}), bf16[4,192,256]{2,1,0:T(8,128)(2,1)S(1)}, u32[]{:S(2)}, u32[]{:S(2)}) async-start(bf16[4,192,256]{2,1,0:T(8,128)(2,1)} %bitcast.3), calls=%async_computation | async-start | bytes 786432 | tf_op jit(solution)/shard_map/all_to_all | solution.py:24
  16.0 3.7 %copy.55 = f32[1,256,2,1024]{3,1,2,0:T(8,128)} copy(f32[1,256,2,1024]{3,2,1,0:T(2,128)} %param.8) | data formatting | bytes 4194304 | tf_op args[2]
  19.7 9.5 %all-to-all-done = bf16[4,192,256]{2,1,0:T(8,128)(2,1)S(1)} async-done(((bf16[4,192,256]{2,1,0:T(8,128)(2,1)}), bf16[4,192,256]{2,1,0:T(8,128)(2,1)S(1)}, u32[]{:S(2)}, u32[]{:S(2)}) %all-to-all-start) | async-done | bytes 393248 | tf_op jit(solution)/shard_map/all_to_all | solution.py:24
  29.2 0.8 copy.43
  30.2 1.0 copy.33
  31.3 10.3 %all-to-all-start.2 = ((bf16[8,192,256]{2,1,0:T(8,128)(2,1)}), bf16[8,192,256]{2,1,0:T(8,128)(2,1)S(1)}, u32[]{:S(2)}, u32[]{:S(2)}) async-start(bf16[8,192,256]{2,1,0:T(8,128)(2,1)} %copy.33), calls=%async_computation.2 | async-start | bytes 1572864 | tf_op jit(solution)/shard_map/all_to_all | solution.py:30
  41.6 0.6 fusion.8
  42.2 28.7 %all-to-all-done.2 = bf16[8,192,256]{2,1,0:T(8,128)(2,1)S(1)} async-done(((bf16[8,192,256]{2,1,0:T(8,128)(2,1)}), bf16[8,192,256]{2,1,0:T(8,128)(2,1)S(1)}, u32[]{:S(2)}, u32[]{:S(2)}) %all-to-all-start.2) | async-done | bytes 786464 | tf_op jit(solution)/shard_map/all_to_all | solution.py:30
  70.9 4.8 %all-to-all-start.1 = ((f32[2,256,1024]{2,1,0:T(8,128)}), f32[2,256,1024]{2,1,0:T(8,128)}, u32[]{:S(2)}, u32[]{:S(2)}) async-start(f32[2,256,1024]{2,1,0:T(8,128)} %bitcast.7), calls=%async_computation.1 | async-start | bytes 4194304 | tf_op jit(solution)/shard_map/all_to_all | solution.py:33
  76.0 2.7 %all-to-all-done.1 = f32[2,256,1024]{2,1,0:T(8,128)} async-done(((f32[2,256,1024]{2,1,0:T(8,128)}), f32[2,256,1024]{2,1,0:T(8,128)}, u32[]{:S(2)}, u32[]{:S(2)}) %all-to-all-start.1) | async-done | bytes 2097184 | tf_op jit(solution)/shard_map/all_to_all | solution.py:33
  78.8 5.0 %all_to_all.40 = bf16[2,1536,256]{1,2,0:T(8,128)(2,1)S(1)} all-to-all(bf16[2,1536,256]{1,2,0:T(8,128)(2,1)S(1)} %broadcast_in_dim.12), channel_id=1, replica_groups=mesh['yh'=2,'core'=2,'z'=8,'yl'=4,'x'=4] {'core'}, dimensions={0} | all-to-all | bytes 3145728 | tf_op jit(solution)/shard_map/all_to_all | solution.py:31
  83.8 7.9 %all-gather.2.cloned.1.call-done = bf16[1536,1024]{1,0:T(8,128)(2,1)} async-done(((bf16[192,1024]{1,0:T(8,128)(2,1)}), bf16[1536,1024]{1,0:T(8,128)(2,1)}) %all-gather.2.cloned.1.call-update) | async-done | bytes 3145744 | tf_op jit(solution)/shard_map/all_gather | solution.py:27
  91.8 5.0 %multiply_convert_fusion = f16[2,256,1024]{2,1,0:T(8,128)(2,1)S(1)} fusion(f32[2,256,1024]{2,1,0:T(8,128)} %all-to-all-done.1, bf16[2,1536,256]{1,2,0:T(8,128)(2,1)S(1)} %all_to_all.40, bf16[1536,1024]{1,0:T(8,128)(2,1)} %all-gather.2.cloned.1.call-done, f32[]{:T(128)} %bitcast), kind=kOutput, calls=%fused_computation.4 | convolution fusion | flops 1612709888 | bytes 7864324 | tf_op jit(solution)/shard_map/dot_general | solution.py:36
  97.1 18.0 %all_to_all.41 = f16[4,2,4,16,1024]{4,3,2,1,0:T(8,128)(2,1)S(1)} all-to-all(f16[4,2,4,16,1024]{4,3,2,1,0:T(8,128)(2,1)S(1)} %bitcast.45), channel_id=1, replica_groups=mesh['yh'=2,'core'=2,'z'=8,'yl'=4,'x'=4] {'x'}, dimensions={0} | all-to-all | bytes 2097152 | tf_op jit(solution)/shard_map/all_to_all | solution.py:40
  115.3 13.8 %all_to_all.42 = f16[8,16,1024]{2,1,0:T(8,128)(2,1)S(1)} all-to-all(f16[8,16,1024]{2,1,0:T(8,128)(2,1)S(1)} %bitcast.51), channel_id=1, replica_groups=mesh['yh'=2,'core'=2,'z'=8,'yl'=4,'x'=4] {'core','yl'}, dimensions={0} | all-to-all | bytes 524288 | tf_op jit(solution)/shard_map/all_to_all | solution.py:42
  129.5 11.9 %all_to_all.43 = bf16[4,16,2,1024]{3,2,1,0:T(2,128)(2,1)S(1)} all-to-all(bf16[4,16,2,1024]{3,2,1,0:T(2,128)(2,1)S(1)} %broadcast_in_dim.13), channel_id=1, replica_groups=mesh['yh'=2,'core'=2,'z'=8,'yl'=4,'x'=4] {'yl'}, dimensions={0} | all-to-all | bytes 524288 | tf_op jit(solution)/shard_map/all_to_all | solution.py:51
  141.4 1.8 %broadcast_in_dim.14 = bf16[4,4,16,2,1024]{4,3,2,1,0:T(2,128)(2,1)} broadcast(bf16[4,16,2,1024]{3,2,1,0:T(2,128)(2,1)S(1)} %all_to_all.43), dimensions={1,2,3,4} | broadcast | bytes 1310720 | tf_op jit(solution)/shard_map/broadcast_in_dim | solution.py:52
  143.2 4.9 %all-to-all-start.7 = ((bf16[4,4,16,2,1024]{4,3,2,1,0:T(2,128)(2,1)}), bf16[4,4,16,2,1024]{4,3,2,1,0:T(2,128)(2,1)S(1)}, u32[]{:S(2)}, u32[]{:S(2)}) async-start(bf16[4,4,16,2,1024]{4,3,2,1,0:T(2,128)(2,1)} %broadcast_in_dim.14), calls=%async_computation.7 | async-start | bytes 2097152 | tf_op jit(solution)/shard_map/all_to_all | solution.py:53
  148.1 0.8 copy.40
  148.9 0.8 copy.41
  149.6 11.6 %all-to-all-done.7 = bf16[4,4,16,2,1024]{4,3,2,1,0:T(2,128)(2,1)S(1)} async-done(((bf16[4,4,16,2,1024]{4,3,2,1,0:T(2,128)(2,1)}), bf16[4,4,16,2,1024]{4,3,2,1,0:T(2,128)(2,1)S(1)}, u32[]{:S(2)}, u32[]{:S(2)}) %all-to-all-start.7) | async-done | bytes 1048608 | tf_op jit(solution)/shard_map/all_to_all | solution.py:53
  161.5 2.1 %copy.42 = bf16[256,2,1024]{2,1,0:T(2,128)(2,1)} copy(bf16[256,2,1024]{2,0,1:T(8,128)(2,1)S(1)} %bitcast.46) | data formatting | bytes 2097152
  (21 shorter events, 1.8 us)
Async XLA Ops:
  8.9 20.3 %all-to-all-start = ((bf16[4,192,256]{2,1,0:T(8,128)(2,1)}), bf16[4,192,256]{2,1,0:T(8,128)(2,1)S(1)}, u32[]{:S(2)}, u32[]{:S(2)}) async-start(bf16[4,192,256]{2,1,0:T(8,128)(2,1)} %bitcast.3), calls=%async_computation | async-start | bytes 786432 | tf_op jit(solution)/shard_map/all_to_all | solution.py:24
  16.0 14.0 %copy-start = (bf16[1,192,2048]{2,1,0:T(8,128)(2,1)S(1)}, bf16[1,192,2048]{2,1,0:T(8,128)(2,1)}, u32[]{:S(2)}) copy-start(bf16[1,192,2048]{2,1,0:T(8,128)(2,1)} %param.6) | copy-start | bytes 2359300
  16.0 75.8 %all-gather.2.cloned.1.call-start = ((), (), s32[]{:S(2)}) async-start(), calls=%async_computation.8 | async-start | bytes 3538944 | tf_op jit(solution)/shard_map/all_gather | solution.py:27
  30.0 11.6 %copy-start.3 = (s32[1,2]{1,0:T(1,128)S(1)}, s32[1,2]{1,0:T(1,128)}, u32[]{:S(2)}) copy-start(s32[1,2]{1,0:T(1,128)} %param.9) | copy-start | bytes 28
  31.3 39.6 %all-to-all-start.2 = ((bf16[8,192,256]{2,1,0:T(8,128)(2,1)}), bf16[8,192,256]{2,1,0:T(8,128)(2,1)S(1)}, u32[]{:S(2)}, u32[]{:S(2)}) async-start(bf16[8,192,256]{2,1,0:T(8,128)(2,1)} %copy.33), calls=%async_computation.2 | async-start | bytes 1572864 | tf_op jit(solution)/shard_map/all_to_all | solution.py:30
  70.9 7.8 %all-to-all-start.1 = ((f32[2,256,1024]{2,1,0:T(8,128)}), f32[2,256,1024]{2,1,0:T(8,128)}, u32[]{:S(2)}, u32[]{:S(2)}) async-start(f32[2,256,1024]{2,1,0:T(8,128)} %bitcast.7), calls=%async_computation.1 | async-start | bytes 4194304 | tf_op jit(solution)/shard_map/all_to_all | solution.py:33
  115.0 14.1 %copy-start.1 = (f32[16,2,1024]{2,1,0:T(2,128)S(1)}, f32[16,2,1024]{2,1,0:T(2,128)}, u32[]{:S(2)}) copy-start(f32[16,2,1024]{2,1,0:T(2,128)} %param.11) | copy-start | bytes 393220
  115.0 14.1 %copy-start.2 = (f32[16,2,1024]{2,1,0:T(2,128)S(1)}, f32[16,2,1024]{2,1,0:T(2,128)}, u32[]{:S(2)}) copy-start(f32[16,2,1024]{2,1,0:T(2,128)} %param.10) | copy-start | bytes 393220
  143.2 18.0 %all-to-all-start.7 = ((bf16[4,4,16,2,1024]{4,3,2,1,0:T(2,128)(2,1)}), bf16[4,4,16,2,1024]{4,3,2,1,0:T(2,128)(2,1)S(1)}, u32[]{:S(2)}, u32[]{:S(2)}) async-start(bf16[4,4,16,2,1024]{4,3,2,1,0:T(2,128)(2,1)} %broadcast_in_dim.14), calls=%async_computation.7 | async-start | bytes 2097152 | tf_op jit(solution)/shard_map/all_to_all | solution.py:53
Sparse Core Ops, SparseCore 0:
  30.1 61.6 all-gather.1

commit v2 on v1

v2 whole, which is shorter than its diff:
```python
import jax
import jax.numpy as jnp
from jax import lax
from jax.sharding import Mesh, PartitionSpec as P

inner_rate = 0.8
momentum_decay = 0.9
outer_rate = 0.7

f32, f16, bf16 = jnp.float32, jnp.float16, jnp.bfloat16


def body(activations, cotangents, inner_drift, drift_flags, master_weights, outer_momentum):
    n_z, replicas = lax.axis_size("z"), lax.axis_size("yl") * lax.axis_size("x")
    first_core = lax.axis_index("core") == 0
    low_half = lax.axis_index("yh") == 0
    z = lax.axis_index("z")
    tokens = activations.shape[1]
    part = tokens // 2
    own_rows = master_weights.shape[0]
    rows, kvw = inner_drift.shape[1], inner_drift.shape[3]
    half = kvw // 2

    def swap(value, axis):
        return lax.ppermute(value, axis, [(0, 1), (1, 0)])

    ways = [(i, (i + 1) % n_z) for i in range(n_z)] + [(n_z + i, n_z + (i - 1) % n_z) for i in range(n_z)]

    def step(value):
        return lax.ppermute(value, ("core", "z"), ways)

    def cut(block, first):
        return jnp.where(first, block[:part], block[part:])

    def chip(mine, other):
        low, high = jnp.where(first_core, mine, other), jnp.where(first_core, other, mine)
        return jnp.concatenate([low[0], high[0], low[1], high[1]], axis=1)

    def ring(block):
        held = [cut(block, first_core)]
        for _ in range(n_z // 2 - 1):
            block = step(block)
            held.append(block)
        held.append(step(cut(block, first_core)))
        return jnp.concatenate(held, axis=0)

    cots = cotangents[0].swapaxes(0, 1)
    far = swap(cots, "yh")
    near_columns = ring(chip(cots, swap(cots, "core")))
    far_columns = ring(chip(far, swap(far, "core")))

    acts = activations[0].reshape(tokens, n_z, rows).swapaxes(0, 1)
    acts = lax.all_to_all(acts, "z", 0, 0, tiled=True)

    def in_order(first):
        sign = jnp.where(first, -1, 1)
        blocks = [lax.dynamic_index_in_dim(acts, (z + n_z + sign * s) % n_z, 0, keepdims=False) for s in range(n_z // 2 + 1)]
        return jnp.concatenate([cut(blocks[0], first)] + blocks[1:-1] + [cut(blocks[-1], first)], axis=0)

    acts_mine = in_order(first_core)
    acts_other = swap(in_order(~first_core), "core")

    def gradient(columns):
        dims = (((0,), (0,)), ((), ()))
        theirs = lax.dot_general(acts_other, columns, dims, preferred_element_type=f32)
        came = swap(theirs, "core")
        return lax.dot_general(acts_mine, columns, dims, preferred_element_type=f32) + came

    drift = inner_drift[0].swapaxes(0, 1)
    flags = drift_flags[0].astype(f32)

    def terms(columns, low):
        grads = gradient(columns)
        drifts = jnp.where(low, drift[:, :, :half], drift[:, :, half:])
        return jnp.concatenate(
            [flags[k] * (drifts[k] + inner_rate * grads[:, k * half : (k + 1) * half]) for k in range(2)], axis=1
        ).astype(f16)

    def reduced(term):
        got = lax.all_to_all(term.reshape(replicas, own_rows, -1), ("yl", "x"), 0, 0, tiled=True)
        return got.astype(f32).sum(0)

    total = reduced(jnp.concatenate([terms(near_columns, low_half), terms(far_columns, ~low_half)], axis=1))
    total = total.reshape(own_rows, 2, 2, half)
    low, high = jnp.where(low_half, total[:, 0], total[:, 1]), jnp.where(low_half, total[:, 1], total[:, 0])
    drift_sum = jnp.concatenate([low, high], axis=2)

    delta = drift_sum / replicas
    new_momentum = momentum_decay * outer_momentum + delta
    new_master = master_weights - outer_rate * (delta + momentum_decay * new_momentum)

    fresh = jnp.broadcast_to(new_master.astype(bf16)[None], (replicas, own_rows, 2, kvw))
    fresh_copy = lax.all_to_all(fresh, ("yl", "x"), 0, 0, tiled=True).reshape(rows, 2, kvw)
    return (new_master, new_momentum, fresh_copy)


def solution(mesh):
    split = Mesh(mesh.devices.reshape(2, 2, 8, 4, 4), ("yh", "core", "z", "yl", "x"))
    tensor, replica = ("yh", "core"), ("yl", "x")
    return jax.shard_map(
        body,
        mesh=split,
        in_specs=(
            P(replica, "z", tensor),
            P(replica, "z", None, tensor),
            P(replica, tensor + ("z",), None, None),
            P(replica, None),
            P(tensor + ("z",) + replica, None, None),
            P(tensor + ("z",) + replica, None, None),
        ),
        out_specs=(
            P(tensor + ("z",) + replica, None, None),
            P(tensor + ("z",) + replica, None, None),
            P(tensor + ("z",), None, None),
        ),
        check_vma=False,
    )
```

time: 171 us -> 175 us (1.023)
  the two profiles are of different devices: /device:TPU:2 before, /device:TPU:8 now
where the time goes in v2:
time: 175 us; the launch traced here: 173 us
  blocking collectives  62.8 us (36%)
  starting transfers between devices  48.9 us (28%)
  waiting for transfers between devices  27 us (15%)
  local copies, waits for them, and re-layouts  17.9 us (10%)
  other arithmetic  8.73 us (5%)
  matrix products  6.79 us (4%)
    all_to_all x1, blocking collectives, reduced(): lax.all_to_all(term.reshape(replicas, own_rows, -1), ('yl', 'x'), 0, 0, t...  32.6 us
    all_to_all x1, blocking collectives, body(): lax.all_to_all(fresh, ('yl', 'x'), 0, 0, tiled=True).reshape(rows, 2, kvw)  30.2 us
    ppermute x8, waiting for transfers between devices, step(): return lax.ppermute(value, ('core', 'z'), ways)  27 us
    ppermute x6, starting transfers between devices, swap(): return lax.ppermute(value, axis, [(0, 1), (1, 0)])  19.4 us
    ppermute x8, starting transfers between devices, step(): return lax.ppermute(value, ('core', 'z'), ways)  19.2 us
    unnamed x27, local copies, waits for them, and re-layouts  14.4 us
    all_to_all x1, starting transfers between devices, body(): acts = lax.all_to_all(acts, 'z', 0, 0, tiled=True)  10.3 us
    dot_general x2, matrix products, gradient(): lax.dot_general(acts_mine, columns, dims, preferred_element_type=f32) + came  3.63 us
  transfers between devices with their start and end apart: 15, of which 4 were waited for; matrix products, arithmetic and copies ran while one was open for 14% of the time, Pallas kernels for 0%

profile of v2, /device:TPU:8, one launch (start us, length us, event | category | flops | bytes accessed | tf_op | source)
XLA Modules:
  0.0 173.4 jit_solution(10681016051464757368)
XLA Ops:
  1.6 6.8 %collective-permute-start.7 = (bf16[2,192,256]{2,1,0:T(8,128)(2,1)S(1)}, bf16[2,192,256]{2,1,0:T(8,128)(2,1)S(1)}, u32[]{:S(2)}, u32[]{:S(2)}) collective-permute-start(bf16[2,192,256]{2,1,0:T(8,128)(2,1)S(1)} %bitcast.114), channel_id=1, source_target_pairs={{0,256},{256,0},{1,257},{257,1},{2,258},{258,2},{3,259},{259,3},{4... | collective-permute-start | bytes 589832 | tf_op jit(solution)/shard_map/ppermute | solution.py:25
  8.4 1.9 %collective-permute-start = (bf16[2,192,256]{2,1,0:T(8,128)(2,1)S(1)}, bf16[2,192,256]{2,1,0:T(8,128)(2,1)S(1)}, u32[]{:S(2)}, u32[]{:S(2)}) collective-permute-start(bf16[2,192,256]{2,1,0:T(8,128)(2,1)S(1)} %bitcast.115), channel_id=1, source_target_pairs={{0,128},{128,0},{1,129},{129,1},{2,130},{130,2},{3,131},{131,3},{4... | collective-permute-start | bytes 589832 | tf_op jit(solution)/shard_map/ppermute | solution.py:25
  12.7 10.3 %all-to-all-start = ((bf16[8,192,256]{2,1,0:T(8,128)(2,1)}), bf16[8,192,256]{2,1,0:T(8,128)(2,1)}, u32[]{:S(2)}, u32[]{:S(2)}) async-start(bf16[8,192,256]{2,1,0:T(8,128)(2,1)} %copy.31), calls=%async_computation | async-start | bytes 1572864 | tf_op jit(solution)/shard_map/all_to_all | solution.py:53
  23.1 2.1 %collective-permute-start.8 = (bf16[2,192,256]{2,1,0:T(8,128)(2,1)S(1)}, bf16[2,192,256]{2,1,0:T(8,128)(2,1)S(1)}, u32[]{:S(2)}, u32[]{:S(2)}) collective-permute-start(bf16[2,192,256]{2,1,0:T(8,128)(2,1)S(1)} %collective-permute-done.7), channel_id=1, source_target_pairs={{0,128},{128,0},{1,129},{129,1},{2,130},{130,2},{3,131},{131,3},{4... | collective-permute-start | bytes 589832 | tf_op jit(solution)/shard_map/ppermute | solution.py:25
  25.3 3.7 %collective-permute-start.1 = (bf16[192,1024]{1,0:T(8,128)(2,1)S(1)}, bf16[192,1024]{1,0:T(8,128)(2,1)S(1)}, u32[]{:S(2)}, u32[]{:S(2)}) collective-permute-start(bf16[192,1024]{1,0:T(8,128)(2,1)S(1)} %pad_maximum_fusion.1), channel_id=1, source_target_pairs={{0,16},{16,32},{32,48},{48,64},{64,80},{80,96},{96,112},{112,0},{1... | collective-permute-start | bytes 1179656 | tf_op jit(solution)/shard_map/ppermute | solution.py:30
  29.2 3.4 %collective-permute-start.9 = (bf16[192,1024]{1,0:T(8,128)(2,1)S(1)}, bf16[192,1024]{1,0:T(8,128)(2,1)}, u32[]{:S(2)}, u32[]{:S(2)}) collective-permute-start(bf16[192,1024]{1,0:T(8,128)(2,1)S(1)} %pad_maximum_fusion.2), channel_id=1, source_target_pairs={{0,16},{16,32},{32,48},{48,64},{64,80},{80,96},{96,112},{112,0},{1... | collective-permute-start | bytes 1179656 | tf_op jit(solution)/shard_map/ppermute | solution.py:30
  32.6 15.9 %collective-permute-done.1 = bf16[192,1024]{1,0:T(8,128)(2,1)S(1)} collective-permute-done((bf16[192,1024]{1,0:T(8,128)(2,1)S(1)}, bf16[192,1024]{1,0:T(8,128)(2,1)S(1)}, u32[]{:S(2)}, u32[]{:S(2)}) %collective-permute-start.1) | collective-permute-done | bytes 393248 | tf_op jit(solution)/shard_map/ppermute | solution.py:30
  48.5 1.9 %collective-permute-start.2 = (bf16[192,1024]{1,0:T(8,128)(2,1)S(1)}, bf16[192,1024]{1,0:T(8,128)(2,1)}, u32[]{:S(2)}, u32[]{:S(2)}) collective-permute-start(bf16[192,1024]{1,0:T(8,128)(2,1)S(1)} %collective-permute-done.1), channel_id=1, source_target_pairs={{0,16},{16,32},{32,48},{48,64},{64,80},{80,96},{96,112},{112,0},{1... | collective-permute-start | bytes 1179656 | tf_op jit(solution)/shard_map/ppermute | solution.py:30
  50.6 2.2 %collective-permute-done.9 = bf16[192,1024]{1,0:T(8,128)(2,1)} collective-permute-done((bf16[192,1024]{1,0:T(8,128)(2,1)S(1)}, bf16[192,1024]{1,0:T(8,128)(2,1)}, u32[]{:S(2)}, u32[]{:S(2)}) %collective-permute-start.9) | collective-permute-done | bytes 393248 | tf_op jit(solution)/shard_map/ppermute | solution.py:30
  52.8 1.9 %collective-permute-start.10 = (bf16[192,1024]{1,0:T(8,128)(2,1)}, bf16[192,1024]{1,0:T(8,128)(2,1)}, u32[]{:S(2)}, u32[]{:S(2)}) collective-permute-start(bf16[192,1024]{1,0:T(8,128)(2,1)} %collective-permute-done.9), channel_id=1, source_target_pairs={{0,16},{16,32},{32,48},{48,64},{64,80},{80,96},{96,112},{112,0},{1... | collective-permute-start | bytes 1179656 | tf_op jit(solution)/shard_map/ppermute | solution.py:30
  54.7 4.7 %collective-permute-done.2 = bf16[192,1024]{1,0:T(8,128)(2,1)} collective-permute-done((bf16[192,1024]{1,0:T(8,128)(2,1)S(1)}, bf16[192,1024]{1,0:T(8,128)(2,1)}, u32[]{:S(2)}, u32[]{:S(2)}) %collective-permute-start.2) | collective-permute-done | bytes 393248 | tf_op jit(solution)/shard_map/ppermute | solution.py:30
  59.5 1.9 %collective-permute-start.3 = (bf16[192,1024]{1,0:T(8,128)(2,1)}, bf16[192,1024]{1,0:T(8,128)(2,1)S(1)}, u32[]{:S(2)}, u32[]{:S(2)}) collective-permute-start(bf16[192,1024]{1,0:T(8,128)(2,1)} %collective-permute-done.2), channel_id=1, source_target_pairs={{0,16},{16,32},{32,48},{48,64},{64,80},{80,96},{96,112},{112,0},{1... | collective-permute-start | bytes 1179656 | tf_op jit(solution)/shard_map/ppermute | solution.py:30
  64.5 1.9 %collective-permute-start.11 = (bf16[192,1024]{1,0:T(8,128)(2,1)}, bf16[192,1024]{1,0:T(8,128)(2,1)}, u32[]{:S(2)}, u32[]{:S(2)}) collective-permute-start(bf16[192,1024]{1,0:T(8,128)(2,1)} %collective-permute-done.10), channel_id=1, source_target_pairs={{0,16},{16,32},{32,48},{48,64},{64,80},{80,96},{96,112},{112,0},{1... | collective-permute-start | bytes 1179656 | tf_op jit(solution)/shard_map/ppermute | solution.py:30
  66.5 4.1 %collective-permute-done.3 = bf16[192,1024]{1,0:T(8,128)(2,1)S(1)} collective-permute-done((bf16[192,1024]{1,0:T(8,128)(2,1)}, bf16[192,1024]{1,0:T(8,128)(2,1)S(1)}, u32[]{:S(2)}, u32[]{:S(2)}) %collective-permute-start.3) | collective-permute-done | bytes 393248 | tf_op jit(solution)/shard_map/ppermute | solution.py:30
  72.0 1.9 %collective-permute-start.4 = (bf16[96,1024]{1,0:T(8,128)(2,1)}, bf16[96,1024]{1,0:T(8,128)(2,1)}, u32[]{:S(2)}, u32[]{:S(2)}) collective-permute-start(bf16[96,1024]{1,0:T(8,128)(2,1)} %slice_select_fusion.4), channel_id=1, source_target_pairs={{0,16},{16,32},{32,48},{48,64},{64,80},{80,96},{96,112},{112,0},{1... | collective-permute-start | bytes 589832 | tf_op jit(solution)/shard_map/ppermute | solution.py:30
  78.7 1.9 %collective-permute-start.5 = (bf16[768,256]{1,0:T(8,128)(2,1)S(1)}, bf16[768,256]{1,0:T(8,128)(2,1)S(1)}, u32[]{:S(2)}, u32[]{:S(2)}) collective-permute-start(bf16[768,256]{1,0:T(8,128)(2,1)S(1)} %get-tuple-element.13), channel_id=1, source_target_pairs={{0,128},{128,0},{1,129},{129,1},{2,130},{130,2},{3,131},{131,3},{4... | collective-permute-start | bytes 1179656 | tf_op jit(solution)/shard_map/ppermute | solution.py:25
  81.7 2.6 %collective-permute-start.12 = (bf16[96,1024]{1,0:T(8,128)(2,1)S(1)}, bf16[96,1024]{1,0:T(8,128)(2,1)S(1)}, u32[]{:S(2)}, u32[]{:S(2)}) collective-permute-start(bf16[96,1024]{1,0:T(8,128)(2,1)S(1)} %slice_select_fusion.2), channel_id=1, source_target_pairs={{0,16},{16,32},{32,48},{48,64},{64,80},{80,96},{96,112},{112,0},{1... | collective-permute-start | bytes 589832 | tf_op jit(solution)/shard_map/ppermute | solution.py:30
  86.9 4.7 %collective-permute-start.6 = (f32[256,1024]{1,0:T(8,128)}, f32[256,1024]{1,0:T(8,128)}, u32[]{:S(2)}, u32[]{:S(2)}) collective-permute-start(f32[256,1024]{1,0:T(8,128)} %fusion.22), channel_id=1, source_target_pairs={{0,128},{128,0},{1,129},{129,1},{2,130},{130,2},{3,131},{131,3},{4... | collective-permute-start | bytes 3145736 | tf_op jit(solution)/shard_map/ppermute | solution.py:25
  95.2 1.9 %collective-permute-start.13 = (f32[256,1024]{1,0:T(8,128)}, f32[256,1024]{1,0:T(8,128)}, u32[]{:S(2)}, u32[]{:S(2)}) collective-permute-start(f32[256,1024]{1,0:T(8,128)} %fusion.23), channel_id=1, source_target_pairs={{0,128},{128,0},{1,129},{129,1},{2,130},{130,2},{3,131},{131,3},{4... | collective-permute-start | bytes 3145736 | tf_op jit(solution)/shard_map/ppermute | solution.py:25
  97.1 2.3 %copy.45 = f32[1,256,2,1024]{3,1,2,0:T(8,128)S(1)} copy(f32[1,256,2,1024]{3,2,1,0:T(2,128)} %param.8) | data formatting | bytes 4194304 | tf_op args[2]
  100.3 1.8 %convolution_add_fusion.1 = f32[256,1024]{1,0:T(8,128)S(1)} fusion(f32[256,1024]{1,0:T(8,128)} %collective-permute-done.6, bf16[768,256]{1,0:T(8,128)(2,1)S(1)} %get-tuple-element.12, bf16[768,1024]{1,0:T(8,128)(2,1)S(1)} %constant_dynamic-update-slice_fusion), kind=kOutput, calls=%fused_computation.3 | convolution fusion | flops 402915328 | bytes 4063232 | tf_op jit(solution)/shard_map/dot_general | solution.py:67
  103.7 1.8 %convolution_add_fusion = f32[256,1024]{1,0:T(8,128)S(1)} fusion(f32[256,1024]{1,0:T(8,128)} %collective-permute-done.13, bf16[768,256]{1,0:T(8,128)(2,1)S(1)} %get-tuple-element.12, bf16[768,1024]{1,0:T(8,128)(2,1)S(1)} %constant_dynamic-update-slice_fusion.4), kind=kOutput, calls=%fused_computation.2 | convolution fusion | flops 402915328 | bytes 4063232 | tf_op jit(solution)/shard_map/dot_general | solution.py:67
  107.5 32.6 %all_to_all.15 = f16[16,16,2048]{2,1,0:T(8,128)(2,1)S(1)} all-to-all(f16[16,16,2048]{2,1,0:T(8,128)(2,1)S(1)} %pad_maximum_fusion), channel_id=1, replica_groups=mesh['yh'=2,'core'=2,'z'=8,'yl'=4,'x'=4] {'yl','x'}, dimensions={0} | all-to-all | bytes 2097152 | tf_op jit(solution)/shard_map/all_to_all | solution.py:80
  142.2 30.2 %all_to_all.16 = bf16[16,16,2,1024]{3,2,1,0:T(2,128)(2,1)S(1)} all-to-all(bf16[16,16,2,1024]{3,2,1,0:T(2,128)(2,1)S(1)} %broadcast_in_dim.2), channel_id=1, replica_groups=mesh['yh'=2,'core'=2,'z'=8,'yl'=4,'x'=4] {'yl','x'}, dimensions={0} | all-to-all | bytes 2097152 | tf_op jit(solution)/shard_map/all_to_all | solution.py:93
  (66 shorter events, 27.6 us)
Async XLA Ops:
  1.6 21.5 %collective-permute-start.7 = (bf16[2,192,256]{2,1,0:T(8,128)(2,1)S(1)}, bf16[2,192,256]{2,1,0:T(8,128)(2,1)S(1)}, u32[]{:S(2)}, u32[]{:S(2)}) collective-permute-start(bf16[2,192,256]{2,1,0:T(8,128)(2,1)S(1)} %bitcast.114), channel_id=1, source_target_pairs={{0,256},{256,0},{1,257},{257,1},{2,258},{258,2},{3,259},{259,3},{4... | collective-permute-start | bytes 589832 | tf_op jit(solution)/shard_map/ppermute | solution.py:25
  8.4 16.8 %collective-permute-start = (bf16[2,192,256]{2,1,0:T(8,128)(2,1)S(1)}, bf16[2,192,256]{2,1,0:T(8,128)(2,1)S(1)}, u32[]{:S(2)}, u32[]{:S(2)}) collective-permute-start(bf16[2,192,256]{2,1,0:T(8,128)(2,1)S(1)} %bitcast.115), channel_id=1, source_target_pairs={{0,128},{128,0},{1,129},{129,1},{2,130},{130,2},{3,131},{131,3},{4... | collective-permute-start | bytes 589832 | tf_op jit(solution)/shard_map/ppermute | solution.py:25
  11.7 13.5 %copy-start.2 = (bf16[1,192,2,256]{3,2,1,0:T(2,128)(2,1)S(1)}, bf16[1,192,2,256]{3,2,1,0:T(2,128)(2,1)}, u32[]{:S(2)}) copy-start(bf16[1,192,2,256]{3,2,1,0:T(2,128)(2,1)} %param.7) | copy-start | bytes 589828
  12.7 61.2 %all-to-all-start = ((bf16[8,192,256]{2,1,0:T(8,128)(2,1)}), bf16[8,192,256]{2,1,0:T(8,128)(2,1)}, u32[]{:S(2)}, u32[]{:S(2)}) async-start(bf16[8,192,256]{2,1,0:T(8,128)(2,1)} %copy.31), calls=%async_computation | async-start | bytes 1572864 | tf_op jit(solution)/shard_map/all_to_all | solution.py:53
  23.1 6.0 %collective-permute-start.8 = (bf16[2,192,256]{2,1,0:T(8,128)(2,1)S(1)}, bf16[2,192,256]{2,1,0:T(8,128)(2,1)S(1)}, u32[]{:S(2)}, u32[]{:S(2)}) collective-permute-start(bf16[2,192,256]{2,1,0:T(8,128)(2,1)S(1)} %collective-permute-done.7), channel_id=1, source_target_pairs={{0,128},{128,0},{1,129},{129,1},{2,130},{130,2},{3,131},{131,3},{4... | collective-permute-start | bytes 589832 | tf_op jit(solution)/shard_map/ppermute | solution.py:25
  25.3 23.2 %collective-permute-start.1 = (bf16[192,1024]{1,0:T(8,128)(2,1)S(1)}, bf16[192,1024]{1,0:T(8,128)(2,1)S(1)}, u32[]{:S(2)}, u32[]{:S(2)}) collective-permute-start(bf16[192,1024]{1,0:T(8,128)(2,1)S(1)} %pad_maximum_fusion.1), channel_id=1, source_target_pairs={{0,16},{16,32},{32,48},{48,64},{64,80},{80,96},{96,112},{112,0},{1... | collective-permute-start | bytes 1179656 | tf_op jit(solution)/shard_map/ppermute | solution.py:30
  29.2 23.6 %collective-permute-start.9 = (bf16[192,1024]{1,0:T(8,128)(2,1)S(1)}, bf16[192,1024]{1,0:T(8,128)(2,1)}, u32[]{:S(2)}, u32[]{:S(2)}) collective-permute-start(bf16[192,1024]{1,0:T(8,128)(2,1)S(1)} %pad_maximum_fusion.2), channel_id=1, source_target_pairs={{0,16},{16,32},{32,48},{48,64},{64,80},{80,96},{96,112},{112,0},{1... | collective-permute-start | bytes 1179656 | tf_op jit(solution)/shard_map/ppermute | solution.py:30
  48.5 11.0 %copy-start.3 = (bf16[192,1024]{1,0:T(8,128)(2,1)}, bf16[192,1024]{1,0:T(8,128)(2,1)S(1)}, u32[]{:S(2)}) copy-start(bf16[192,1024]{1,0:T(8,128)(2,1)S(1)} %collective-permute-done.1) | copy-start | bytes 1179652
  48.5 11.0 %collective-permute-start.2 = (bf16[192,1024]{1,0:T(8,128)(2,1)S(1)}, bf16[192,1024]{1,0:T(8,128)(2,1)}, u32[]{:S(2)}, u32[]{:S(2)}) collective-permute-start(bf16[192,1024]{1,0:T(8,128)(2,1)S(1)} %collective-permute-done.1), channel_id=1, source_target_pairs={{0,16},{16,32},{32,48},{48,64},{64,80},{80,96},{96,112},{112,0},{1... | collective-permute-start | bytes 1179656 | tf_op jit(solution)/shard_map/ppermute | solution.py:30
  52.8 11.7 %collective-permute-start.10 = (bf16[192,1024]{1,0:T(8,128)(2,1)}, bf16[192,1024]{1,0:T(8,128)(2,1)}, u32[]{:S(2)}, u32[]{:S(2)}) collective-permute-start(bf16[192,1024]{1,0:T(8,128)(2,1)} %collective-permute-done.9), channel_id=1, source_target_pairs={{0,16},{16,32},{32,48},{48,64},{64,80},{80,96},{96,112},{112,0},{1... | collective-permute-start | bytes 1179656 | tf_op jit(solution)/shard_map/ppermute | solution.py:30
  59.5 11.1 %collective-permute-start.3 = (bf16[192,1024]{1,0:T(8,128)(2,1)}, bf16[192,1024]{1,0:T(8,128)(2,1)S(1)}, u32[]{:S(2)}, u32[]{:S(2)}) collective-permute-start(bf16[192,1024]{1,0:T(8,128)(2,1)} %collective-permute-done.2), channel_id=1, source_target_pairs={{0,16},{16,32},{32,48},{48,64},{64,80},{80,96},{96,112},{112,0},{1... | collective-permute-start | bytes 1179656 | tf_op jit(solution)/shard_map/ppermute | solution.py:30
  64.5 16.1 %collective-permute-start.11 = (bf16[192,1024]{1,0:T(8,128)(2,1)}, bf16[192,1024]{1,0:T(8,128)(2,1)}, u32[]{:S(2)}, u32[]{:S(2)}) collective-permute-start(bf16[192,1024]{1,0:T(8,128)(2,1)} %collective-permute-done.10), channel_id=1, source_target_pairs={{0,16},{16,32},{32,48},{48,64},{64,80},{80,96},{96,112},{112,0},{1... | collective-permute-start | bytes 1179656 | tf_op jit(solution)/shard_map/ppermute | solution.py:30
  70.6 0.8 copy-start
  72.0 12.3 %collective-permute-start.4 = (bf16[96,1024]{1,0:T(8,128)(2,1)}, bf16[96,1024]{1,0:T(8,128)(2,1)}, u32[]{:S(2)}, u32[]{:S(2)}) collective-permute-start(bf16[96,1024]{1,0:T(8,128)(2,1)} %slice_select_fusion.4), channel_id=1, source_target_pairs={{0,16},{16,32},{32,48},{48,64},{64,80},{80,96},{96,112},{112,0},{1... | collective-permute-start | bytes 589832 | tf_op jit(solution)/shard_map/ppermute | solution.py:30
  74.0 6.7 %copy-start.1 = (bf16[192,1024]{1,0:T(8,128)(2,1)S(1)}, bf16[192,1024]{1,0:T(8,128)(2,1)}, u32[]{:S(2)}) copy-start(bf16[192,1024]{1,0:T(8,128)(2,1)} %copy-done) | copy-start | bytes 1179652
  78.7 6.6 %collective-permute-start.5 = (bf16[768,256]{1,0:T(8,128)(2,1)S(1)}, bf16[768,256]{1,0:T(8,128)(2,1)S(1)}, u32[]{:S(2)}, u32[]{:S(2)}) collective-permute-start(bf16[768,256]{1,0:T(8,128)(2,1)S(1)} %get-tuple-element.13), channel_id=1, source_target_pairs={{0,128},{128,0},{1,129},{129,1},{2,130},{130,2},{3,131},{131,3},{4... | collective-permute-start | bytes 1179656 | tf_op jit(solution)/shard_map/ppermute | solution.py:25
  81.7 11.9 %collective-permute-start.12 = (bf16[96,1024]{1,0:T(8,128)(2,1)S(1)}, bf16[96,1024]{1,0:T(8,128)(2,1)S(1)}, u32[]{:S(2)}, u32[]{:S(2)}) collective-permute-start(bf16[96,1024]{1,0:T(8,128)(2,1)S(1)} %slice_select_fusion.2), channel_id=1, source_target_pairs={{0,16},{16,32},{32,48},{48,64},{64,80},{80,96},{96,112},{112,0},{1... | collective-permute-start | bytes 589832 | tf_op jit(solution)/shard_map/ppermute | solution.py:30
  86.9 13.5 %collective-permute-start.6 = (f32[256,1024]{1,0:T(8,128)}, f32[256,1024]{1,0:T(8,128)}, u32[]{:S(2)}, u32[]{:S(2)}) collective-permute-start(f32[256,1024]{1,0:T(8,128)} %fusion.22), channel_id=1, source_target_pairs={{0,128},{128,0},{1,129},{129,1},{2,130},{130,2},{3,131},{131,3},{4... | collective-permute-start | bytes 3145736 | tf_op jit(solution)/shard_map/ppermute | solution.py:25
  95.2 8.5 %collective-permute-start.13 = (f32[256,1024]{1,0:T(8,128)}, f32[256,1024]{1,0:T(8,128)}, u32[]{:S(2)}, u32[]{:S(2)}) collective-permute-start(f32[256,1024]{1,0:T(8,128)} %fusion.23), channel_id=1, source_target_pairs={{0,128},{128,0},{1,129},{129,1},{2,130},{130,2},{3,131},{131,3},{4... | collective-permute-start | bytes 3145736 | tf_op jit(solution)/shard_map/ppermute | solution.py:25
  97.1 2.3 %copy-start.6 = (s32[1,2]{1,0:T(1,128)S(1)}, s32[1,2]{1,0:T(1,128)}, u32[]{:S(2)}) copy-start(s32[1,2]{1,0:T(1,128)} %param.9) | copy-start | bytes 28
  107.5 33.0 %copy-start.4 = (f32[16,2,1024]{2,1,0:T(2,128)S(1)}, f32[16,2,1024]{2,1,0:T(2,128)}, u32[]{:S(2)}) copy-start(f32[16,2,1024]{2,1,0:T(2,128)} %param.10) | copy-start | bytes 393220
  107.5 33.0 %copy-start.5 = (f32[16,2,1024]{2,1,0:T(2,128)S(1)}, f32[16,2,1024]{2,1,0:T(2,128)}, u32[]{:S(2)}) copy-start(f32[16,2,1024]{2,1,0:T(2,128)} %param.11) | copy-start | bytes 393220

commit v3 on v2

--- a/solution.py
+++ b/solution.py
@@ -29,6 +29,9 @@
     def step(value):
         return lax.ppermute(value, ("core", "z"), ways)
 
+    def tied(*values):
+        return lax.optimization_barrier(values)
+
     def cut(block, first):
         return jnp.where(first, block[:part], block[part:])
 
@@ -36,20 +39,30 @@
         low, high = jnp.where(first_core, mine, other), jnp.where(first_core, other, mine)
         return jnp.concatenate([low[0], high[0], low[1], high[1]], axis=1)
 
-    def ring(block):
-        held = [cut(block, first_core)]
-        for _ in range(n_z // 2 - 1):
-            block = step(block)
-            held.append(block)
-        held.append(step(cut(block, first_core)))
-        return jnp.concatenate(held, axis=0)
+    cots = cotangents[0].swapaxes(0, 1)
+    near = chip(cots, swap(cots, "core"))
+    near, cots, own_acts, drift = lax.optimization_barrier((near, cots, activations[0], inner_drift[0]))
+    far = swap(cots, "yh")
 
-    cots = cotangents[0].swapaxes(0, 1)
-    far = swap(cots, "yh")
-    near_columns = ring(chip(cots, swap(cots, "core")))
-    far_columns = ring(chip(far, swap(far, "core")))
+    near_held = [cut(near, first_core)]
+    for _ in range(2):
+        near = step(near)
+        near_held.append(near)
+    far = chip(far, swap(far, "core"))
+    near, far = tied(near, far)
+    far_held = [cut(far, first_core)]
+    near, far = step(near), step(far)
+    near_held.append(near)
+    far_held.append(far)
+    near, far = tied(near, far)
+    near, far = step(cut(near, first_core)), step(far)
+    near_held.append(near)
+    far_held.append(far)
+    near, far = tied(near, far)
+    far = step(far)
+    far_held.append(far)
 
-    acts = activations[0].reshape(tokens, n_z, rows).swapaxes(0, 1)
+    acts = own_acts.reshape(tokens, n_z, rows).swapaxes(0, 1)
     acts = lax.all_to_all(acts, "z", 0, 0, tiled=True)
 
     def in_order(first):
@@ -60,29 +73,32 @@
     acts_mine = in_order(first_core)
     acts_other = swap(in_order(~first_core), "core")
 
-    def gradient(columns):
+    drift = drift.swapaxes(0, 1)
+    flags = drift_flags[0].astype(f32)
+    by_column = jnp.repeat(flags, half)[None]
+
+    def own_term(held, low, before=None):
+        columns = jnp.concatenate(held, axis=0)
+        drifts = jnp.where(low, drift[:, :, :half], drift[:, :, half:])
+        drifts = jnp.concatenate([drifts[0], drifts[1]], axis=1)
         dims = (((0,), (0,)), ((), ()))
         theirs = lax.dot_general(acts_other, columns, dims, preferred_element_type=f32)
         came = swap(theirs, "core")
-        return lax.dot_general(acts_mine, columns, dims, preferred_element_type=f32) + came
+        if before is not None:
+            before, came = tied(before, came)
+        grads = lax.dot_general(acts_mine, columns, dims, preferred_element_type=f32) + came
+        return (by_column * (drifts + inner_rate * grads)).astype(f16), before
 
-    drift = inner_drift[0].swapaxes(0, 1)
-    flags = drift_flags[0].astype(f32)
+    def summed(term):
+        got = lax.all_to_all(term.reshape(replicas, own_rows, 2 * half), ("yl", "x"), 0, 0, tiled=True)
+        return got.astype(f32).sum(0).reshape(own_rows, 2, half)
 
-    def terms(columns, low):
-        grads = gradient(columns)
-        drifts = jnp.where(low, drift[:, :, :half], drift[:, :, half:])
-        return jnp.concatenate(
-            [flags[k] * (drifts[k] + inner_rate * grads[:, k * half : (k + 1) * half]) for k in range(2)], axis=1
-        ).astype(f16)
-
-    def reduced(term):
-        got = lax.all_to_all(term.reshape(replicas, own_rows, -1), ("yl", "x"), 0, 0, tiled=True)
-        return got.astype(f32).sum(0)
-
-    total = reduced(jnp.concatenate([terms(near_columns, low_half), terms(far_columns, ~low_half)], axis=1))
-    total = total.reshape(own_rows, 2, 2, half)
-    low, high = jnp.where(low_half, total[:, 0], total[:, 1]), jnp.where(low_half, total[:, 1], total[:, 0])
+    near_term, far = tied(own_term(near_held, low_half)[0], cut(far, first_core))
+    near_sum = summed(near_term)
+    far_held.append(step(far))
+    far_term, near_sum = own_term(far_held, ~low_half, near_sum)
+    far_sum = summed(far_term)
+    low, high = jnp.where(low_half, near_sum, far_sum), jnp.where(low_half, far_sum, near_sum)
     drift_sum = jnp.concatenate([low, high], axis=2)
 
     delta = drift_sum / replicas

time: 175 us -> 189 us (1.080)
  waiting for transfers between devices: 27 us -> 50.1 us
  blocking collectives: 62.8 us -> 48.8 us
  starting transfers between devices: 48.9 us -> 56.6 us
  matrix products: 6.79 us -> 9.77 us
  other arithmetic: 8.73 us -> 6.02 us
  local copies, waits for them, and re-layouts: 17.9 us -> 15.8 us
    all_to_all x1, blocking collectives: 32.6 us -> 19 us  [summed(): lax.all_to_all(term.reshape(replicas, own_rows, 2 * half), ('yl', 'x'), 0...]
    ppermute x8, waiting for transfers between devices: 27 us -> 36.7 us  [step(): return lax.ppermute(value, ('core', 'z'), ways)]
    all_to_all x0 -> x1, waiting for transfers between devices: none -> 8.55 us  [summed(): lax.all_to_all(term.reshape(replicas, own_rows, 2 * half), ('yl', 'x'), 0...]
    all_to_all x0 -> x1, starting transfers between devices: none -> 8.36 us  [summed(): lax.all_to_all(term.reshape(replicas, own_rows, 2 * half), ('yl', 'x'), 0...]
    ppermute x6, waiting for transfers between devices: 0.02 us -> 4.8 us  [swap(): return lax.ppermute(value, axis, [(0, 1), (1, 0)])]
    unnamed x27 -> x33, local copies, waits for them, and re-layouts: 14.4 us -> 11 us
    another operation x2 -> x0, other arithmetic: 3.12 us -> none
    dot_general x4, matrix products: 6.79 us -> 9.77 us  [the longest x2 5.06 us: own_term(): lax.dot_general(acts_mine, columns, dims, preferred_element_type=f32) + came]
  transfers between devices with their start and end apart: 15 -> 16, of which waited for: 4 -> 8; matrix products, arithmetic and copies ran while one was open for 14% -> 12% of each run, Pallas kernels for 0% -> 0%
where the time goes in v3:
time: 189 us; the launch traced here: 188 us
  starting transfers between devices  56.6 us (30%)
  waiting for transfers between devices  50.1 us (27%)
  blocking collectives  48.8 us (26%)
  local copies, waits for them, and re-layouts  15.8 us (8%)
  matrix products  9.77 us (5%)
  other arithmetic  6.02 us (3%)
    ppermute x8, waiting for transfers between devices, step(): return lax.ppermute(value, ('core', 'z'), ways)  36.7 us
    all_to_all x1, blocking collectives, body(): lax.all_to_all(fresh, ('yl', 'x'), 0, 0, tiled=True).reshape(rows, 2, kvw)  29.7 us
    ppermute x8, starting transfers between devices, step(): return lax.ppermute(value, ('core', 'z'), ways)  21.1 us
    all_to_all x1, blocking collectives, summed(): lax.all_to_all(term.reshape(replicas, own_rows, 2 * half), ('yl', 'x'), 0...  19 us
    ppermute x6, starting transfers between devices, swap(): return lax.ppermute(value, axis, [(0, 1), (1, 0)])  18.6 us
    unnamed x33, local copies, waits for them, and re-layouts  11 us
    all_to_all x1, waiting for transfers between devices, summed(): lax.all_to_all(term.reshape(replicas, own_rows, 2 * half), ('yl', 'x'), 0...  8.55 us
    all_to_all x1, starting transfers between devices, body(): acts = lax.all_to_all(acts, 'z', 0, 0, tiled=True)  8.49 us
  transfers between devices with their start and end apart: 16, of which 8 were waited for; matrix products, arithmetic and copies ran while one was open for 12% of the time, Pallas kernels for 0%

profile of v3, /device:TPU:8, one launch (start us, length us, event | category | flops | bytes accessed | tf_op | source)
XLA Modules:
  0.0 188.2 jit_solution(8569782790761010965)
XLA Ops:
  3.5 2.3 %copy.33 = f32[1,256,2,1024]{3,1,2,0:T(8,128)S(1)} copy(f32[1,256,2,1024]{3,2,1,0:T(2,128)} %param.8) | data formatting | bytes 4194304 | tf_op args[2]
  6.0 7.0 %collective-permute-start.3 = (bf16[2,192,256]{2,1,0:T(8,128)(2,1)S(1)}, bf16[2,192,256]{2,1,0:T(8,128)(2,1)}, u32[]{:S(2)}, u32[]{:S(2)}) collective-permute-start(bf16[2,192,256]{2,1,0:T(8,128)(2,1)S(1)} %bitcast.97), channel_id=1, source_target_pairs={{0,256},{256,0},{1,257},{257,1},{2,258},{258,2},{3,259},{259,3},{4... | collective-permute-start | bytes 589832 | tf_op jit(solution)/shard_map/ppermute | solution.py:25
  13.0 4.3 %collective-permute-start.1 = (bf16[192,1024]{1,0:T(8,128)(2,1)S(1)}, bf16[192,1024]{1,0:T(8,128)(2,1)}, u32[]{:S(2)}, u32[]{:S(2)}) collective-permute-start(bf16[192,1024]{1,0:T(8,128)(2,1)S(1)} %pad_maximum_fusion), channel_id=1, source_target_pairs={{0,16},{16,32},{32,48},{48,64},{64,80},{80,96},{96,112},{112,0},{1... | collective-permute-start | bytes 1179656 | tf_op jit(solution)/shard_map/ppermute | solution.py:30
  17.3 4.8 %collective-permute-done.3 = bf16[2,192,256]{2,1,0:T(8,128)(2,1)} collective-permute-done((bf16[2,192,256]{2,1,0:T(8,128)(2,1)S(1)}, bf16[2,192,256]{2,1,0:T(8,128)(2,1)}, u32[]{:S(2)}, u32[]{:S(2)}) %collective-permute-start.3) | collective-permute-done | bytes 196640 | tf_op jit(solution)/shard_map/ppermute | solution.py:25
  22.1 3.7 %collective-permute-start.4 = (bf16[2,192,256]{2,1,0:T(8,128)(2,1)}, bf16[2,192,256]{2,1,0:T(8,128)(2,1)S(1)}, u32[]{:S(2)}, u32[]{:S(2)}) collective-permute-start(bf16[2,192,256]{2,1,0:T(8,128)(2,1)} %collective-permute-done.3), channel_id=1, source_target_pairs={{0,128},{128,0},{1,129},{129,1},{2,130},{130,2},{3,131},{131,3},{4... | collective-permute-start | bytes 589832 | tf_op jit(solution)/shard_map/ppermute | solution.py:25
  27.1 8.5 %all-to-all-start = ((bf16[8,192,256]{2,1,0:T(8,128)(2,1)}), bf16[8,192,256]{2,1,0:T(8,128)(2,1)S(1)}, u32[]{:S(2)}, u32[]{:S(2)}) async-start(bf16[8,192,256]{2,1,0:T(8,128)(2,1)} %copy.24), calls=%async_computation | async-start | bytes 1572864 | tf_op jit(solution)/shard_map/all_to_all | solution.py:66
  35.6 3.9 %collective-permute-start.2 = (bf16[192,1024]{1,0:T(8,128)(2,1)}, bf16[192,1024]{1,0:T(8,128)(2,1)}, u32[]{:S(2)}, u32[]{:S(2)}) collective-permute-start(bf16[192,1024]{1,0:T(8,128)(2,1)} %collective-permute-done.1), channel_id=1, source_target_pairs={{0,16},{16,32},{32,48},{48,64},{64,80},{80,96},{96,112},{112,0},{1... | collective-permute-start | bytes 1179656 | tf_op jit(solution)/shard_map/ppermute | solution.py:30
  40.6 20.4 %collective-permute-done.2 = bf16[192,1024]{1,0:T(8,128)(2,1)} collective-permute-done((bf16[192,1024]{1,0:T(8,128)(2,1)}, bf16[192,1024]{1,0:T(8,128)(2,1)}, u32[]{:S(2)}, u32[]{:S(2)}) %collective-permute-start.2) | collective-permute-done | bytes 393248 | tf_op jit(solution)/shard_map/ppermute | solution.py:30
  62.9 2.5 %collective-permute-start.6 = (bf16[192,1024]{1,0:T(8,128)(2,1)S(1)}, bf16[192,1024]{1,0:T(8,128)(2,1)}, u32[]{:S(2)}, u32[]{:S(2)}) collective-permute-start(bf16[192,1024]{1,0:T(8,128)(2,1)S(1)} %pad_maximum_fusion.1), channel_id=1, source_target_pairs={{0,16},{16,32},{32,48},{48,64},{64,80},{80,96},{96,112},{112,0},{1... | collective-permute-start | bytes 1179656 | tf_op jit(solution)/shard_map/ppermute | solution.py:30
  69.1 3.1 %collective-permute-done.5 = bf16[192,1024]{1,0:T(8,128)(2,1)} collective-permute-done((bf16[192,1024]{1,0:T(8,128)(2,1)}, bf16[192,1024]{1,0:T(8,128)(2,1)}, u32[]{:S(2)}, u32[]{:S(2)}) %collective-permute-start.5) | collective-permute-done | bytes 393248 | tf_op jit(solution)/shard_map/ppermute | solution.py:30
  72.2 4.2 %collective-permute-done.6 = bf16[192,1024]{1,0:T(8,128)(2,1)} collective-permute-done((bf16[192,1024]{1,0:T(8,128)(2,1)S(1)}, bf16[192,1024]{1,0:T(8,128)(2,1)}, u32[]{:S(2)}, u32[]{:S(2)}) %collective-permute-start.6) | collective-permute-done | bytes 393248 | tf_op jit(solution)/shard_map/ppermute | solution.py:30
  76.6 1.9 %collective-permute-start.8 = (bf16[768,256]{1,0:T(8,128)(2,1)S(1)}, bf16[768,256]{1,0:T(8,128)(2,1)S(1)}, u32[]{:S(2)}, u32[]{:S(2)}) collective-permute-start(bf16[768,256]{1,0:T(8,128)(2,1)S(1)} %get-tuple-element.39), channel_id=1, source_target_pairs={{0,128},{128,0},{1,129},{129,1},{2,130},{130,2},{3,131},{131,3},{4... | collective-permute-start | bytes 1179656 | tf_op jit(solution)/shard_map/ppermute | solution.py:25
  83.3 2.0 %collective-permute-start.10 = (bf16[192,1024]{1,0:T(8,128)(2,1)}, bf16[192,1024]{1,0:T(8,128)(2,1)S(1)}, u32[]{:S(2)}, u32[]{:S(2)}) collective-permute-start(bf16[192,1024]{1,0:T(8,128)(2,1)} %collective-permute-done.6), channel_id=1, source_target_pairs={{0,16},{16,32},{32,48},{48,64},{64,80},{80,96},{96,112},{112,0},{1... | collective-permute-start | bytes 1179656 | tf_op jit(solution)/shard_map/ppermute | solution.py:30
  89.0 2.1 %fusion.13 = f32[256,1024]{1,0:T(8,128)S(1)} fusion(bf16[768,256]{1,0:T(8,128)(2,1)S(1)} %collective-permute-done.8, bf16[768,1024]{1,0:T(8,128)(2,1)} %constant_dynamic-update-slice_fusion), kind=kOutput, calls=%fused_computation.68 | convolution fusion | flops 402653184 | bytes 3014656 | tf_op jit(solution)/shard_map/dot_general | solution.py:85
  91.2 2.2 %collective-permute-start.9 = (f32[256,1024]{1,0:T(8,128)S(1)}, f32[256,1024]{1,0:T(8,128)S(1)}, u32[]{:S(2)}, u32[]{:S(2)}) collective-permute-start(f32[256,1024]{1,0:T(8,128)S(1)} %fusion.13), channel_id=1, source_target_pairs={{0,128},{128,0},{1,129},{129,1},{2,130},{130,2},{3,131},{131,3},{4... | collective-permute-start | bytes 3145736 | tf_op jit(solution)/shard_map/ppermute | solution.py:25
  94.3 2.7 %collective-permute-start.11 = (bf16[192,1024]{1,0:T(8,128)(2,1)S(1)}, bf16[192,1024]{1,0:T(8,128)(2,1)S(1)}, u32[]{:S(2)}, u32[]{:S(2)}) collective-permute-start(bf16[192,1024]{1,0:T(8,128)(2,1)S(1)} %collective-permute-done.10), channel_id=1, source_target_pairs={{0,16},{16,32},{32,48},{48,64},{64,80},{80,96},{96,112},{112,0},{1... | collective-permute-start | bytes 1179656 | tf_op jit(solution)/shard_map/ppermute | solution.py:30
  98.2 7.0 %collective-permute-done.11 = bf16[192,1024]{1,0:T(8,128)(2,1)S(1)} collective-permute-done((bf16[192,1024]{1,0:T(8,128)(2,1)S(1)}, bf16[192,1024]{1,0:T(8,128)(2,1)S(1)}, u32[]{:S(2)}, u32[]{:S(2)}) %collective-permute-start.11) | collective-permute-done | bytes 393248 | tf_op jit(solution)/shard_map/ppermute | solution.py:30
  105.9 2.9 %fusion.6 = f16[256,1024]{1,0:T(8,128)(2,1)} fusion(f32[256,1024]{1,0:T(8,128)S(1)} %collective-permute-done.9, bf16[768,256]{1,0:T(8,128)(2,1)S(1)} %get-tuple-element.38, bf16[768,1024]{1,0:T(8,128)(2,1)} %constant_dynamic-update-slice_fusion, f32[256,512]{1,0:T(8,128)S(1)} %get-tuple-element.37, f32[256,512]{1,0:T(8,128)S(1)} %get-tuple-element.36, ...), kind=kOutput, calls=%fused_computation.9 | convolution fusion | flops 404226048 | bytes 4591616 | tf_op jit(solution)/shard_map/dot_general | solution.py:89
  110.8 8.4 %all-to-all-start.1 = ((f16[16,16,1024]{2,1,0:T(8,128)(2,1)}), f16[16,16,1024]{2,1,0:T(8,128)(2,1)S(1)}, u32[]{:S(2)}, u32[]{:S(2)}) async-start(f16[16,16,1024]{2,1,0:T(8,128)(2,1)} %bitcast.89), calls=%async_computation.1 | async-start | bytes 1048576 | tf_op jit(solution)/shard_map/all_to_all | solution.py:93
  120.1 2.6 %fusion.14 = f32[256,1024]{1,0:T(8,128)} fusion(bf16[768,256]{1,0:T(8,128)(2,1)} %copy-done.3, bf16[768,1024]{1,0:T(8,128)(2,1)S(1)} %constant_dynamic-update-slice_fusion.4), kind=kOutput, calls=%fused_computation.69 | convolution fusion | flops 402653184 | bytes 3014656 | tf_op jit(solution)/shard_map/dot_general | solution.py:85
  125.6 8.6 %all-to-all-done.1 = f16[16,16,1024]{2,1,0:T(8,128)(2,1)S(1)} async-done(((f16[16,16,1024]{2,1,0:T(8,128)(2,1)}), f16[16,16,1024]{2,1,0:T(8,128)(2,1)S(1)}, u32[]{:S(2)}, u32[]{:S(2)}) %all-to-all-start.1) | async-done | bytes 524320 | tf_op jit(solution)/shard_map/all_to_all | solution.py:93
  134.3 2.2 %fusion.7 = f16[256,1024]{1,0:T(8,128)(2,1)S(1)} fusion(f32[256,1024]{1,0:T(8,128)} %collective-permute-done.13, bf16[768,256]{1,0:T(8,128)(2,1)S(1)} %get-tuple-element.38, bf16[768,1024]{1,0:T(8,128)(2,1)S(1)} %constant_dynamic-update-slice_fusion.4, f32[256,512]{1,0:T(8,128)} %get-tuple-element.35, f32[256,512]{1,0:T(8,128)} %get-tuple-element.34, ...), kind=kOutput, calls=%fused_computation.10 | convolution fusion | flops 404226048 | bytes 4591616 | tf_op jit(solution)/shard_map/dot_general | solution.py:89
  136.5 19.0 %all_to_all.20 = f16[16,16,1024]{2,1,0:T(8,128)(2,1)S(1)} all-to-all(f16[16,16,1024]{2,1,0:T(8,128)(2,1)S(1)} %bitcast.90), channel_id=1, replica_groups=mesh['yh'=2,'core'=2,'z'=8,'yl'=4,'x'=4] {'yl','x'}, dimensions={0} | all-to-all | bytes 1048576 | tf_op jit(solution)/shard_map/all_to_all | solution.py:93
  157.5 29.7 %all_to_all.21 = bf16[16,16,2,1024]{3,2,1,0:T(2,128)(2,1)S(1)} all-to-all(bf16[16,16,2,1024]{3,2,1,0:T(2,128)(2,1)S(1)} %broadcast_in_dim.10), channel_id=1, replica_groups=mesh['yh'=2,'core'=2,'z'=8,'yl'=4,'x'=4] {'yl','x'}, dimensions={0} | all-to-all | bytes 2097152 | tf_op jit(solution)/shard_map/all_to_all | solution.py:109
  (74 shorter events, 31.1 us)
Async XLA Ops:
  1.6 4.3 %collective-permute-start = (bf16[2,192,256]{2,1,0:T(8,128)(2,1)S(1)}, bf16[2,192,256]{2,1,0:T(8,128)(2,1)S(1)}, u32[]{:S(2)}, u32[]{:S(2)}) collective-permute-start(bf16[2,192,256]{2,1,0:T(8,128)(2,1)S(1)} %bitcast.96), channel_id=1, source_target_pairs={{0,128},{128,0},{1,129},{129,1},{2,130},{130,2},{3,131},{131,3},{4... | collective-permute-start | bytes 589832 | tf_op jit(solution)/shard_map/ppermute | solution.py:25
  5.8 20.0 %copy-start.8 = (s32[1,2]{1,0:T(1,128)S(1)}, s32[1,2]{1,0:T(1,128)}, u32[]{:S(2)}) copy-start(s32[1,2]{1,0:T(1,128)} %param.9) | copy-start | bytes 28
  5.9 20.0 %copy-start.4 = (bf16[1,192,2048]{2,1,0:T(8,128)(2,1)S(1)}, bf16[1,192,2048]{2,1,0:T(8,128)(2,1)}, u32[]{:S(2)}) copy-start(bf16[1,192,2048]{2,1,0:T(8,128)(2,1)} %param.6) | copy-start | bytes 2359300
  6.0 21.1 %copy-start.2 = (bf16[192,1024]{1,0:T(8,128)(2,1)}, bf16[192,1024]{1,0:T(8,128)(2,1)S(1)}, u32[]{:S(2)}) copy-start(bf16[192,1024]{1,0:T(8,128)(2,1)S(1)} %pad_maximum_fusion) | copy-start | bytes 1179652
  6.0 16.1 %collective-permute-start.3 = (bf16[2,192,256]{2,1,0:T(8,128)(2,1)S(1)}, bf16[2,192,256]{2,1,0:T(8,128)(2,1)}, u32[]{:S(2)}, u32[]{:S(2)}) collective-permute-start(bf16[2,192,256]{2,1,0:T(8,128)(2,1)S(1)} %bitcast.97), channel_id=1, source_target_pairs={{0,256},{256,0},{1,257},{257,1},{2,258},{258,2},{3,259},{259,3},{4... | collective-permute-start | bytes 589832 | tf_op jit(solution)/shard_map/ppermute | solution.py:25
  13.0 22.6 %collective-permute-start.1 = (bf16[192,1024]{1,0:T(8,128)(2,1)S(1)}, bf16[192,1024]{1,0:T(8,128)(2,1)}, u32[]{:S(2)}, u32[]{:S(2)}) collective-permute-start(bf16[192,1024]{1,0:T(8,128)(2,1)S(1)} %pad_maximum_fusion), channel_id=1, source_target_pairs={{0,16},{16,32},{32,48},{48,64},{64,80},{80,96},{96,112},{112,0},{1... | collective-permute-start | bytes 1179656 | tf_op jit(solution)/shard_map/ppermute | solution.py:30
  22.1 17.4 %collective-permute-start.4 = (bf16[2,192,256]{2,1,0:T(8,128)(2,1)}, bf16[2,192,256]{2,1,0:T(8,128)(2,1)S(1)}, u32[]{:S(2)}, u32[]{:S(2)}) collective-permute-start(bf16[2,192,256]{2,1,0:T(8,128)(2,1)} %collective-permute-done.3), channel_id=1, source_target_pairs={{0,128},{128,0},{1,129},{129,1},{2,130},{130,2},{3,131},{131,3},{4... | collective-permute-start | bytes 589832 | tf_op jit(solution)/shard_map/ppermute | solution.py:25
  27.1 49.3 %all-to-all-start = ((bf16[8,192,256]{2,1,0:T(8,128)(2,1)}), bf16[8,192,256]{2,1,0:T(8,128)(2,1)S(1)}, u32[]{:S(2)}, u32[]{:S(2)}) async-start(bf16[8,192,256]{2,1,0:T(8,128)(2,1)} %copy.24), calls=%async_computation | async-start | bytes 1572864 | tf_op jit(solution)/shard_map/all_to_all | solution.py:66
  35.6 25.4 %collective-permute-start.2 = (bf16[192,1024]{1,0:T(8,128)(2,1)}, bf16[192,1024]{1,0:T(8,128)(2,1)}, u32[]{:S(2)}, u32[]{:S(2)}) collective-permute-start(bf16[192,1024]{1,0:T(8,128)(2,1)} %collective-permute-done.1), channel_id=1, source_target_pairs={{0,16},{16,32},{32,48},{48,64},{64,80},{80,96},{96,112},{112,0},{1... | collective-permute-start | bytes 1179656 | tf_op jit(solution)/shard_map/ppermute | solution.py:30
  40.6 35.8 %copy-start = (bf16[192,1024]{1,0:T(8,128)(2,1)}, bf16[192,1024]{1,0:T(8,128)(2,1)S(1)}, u32[]{:S(2)}) copy-start(bf16[192,1024]{1,0:T(8,128)(2,1)S(1)} %pad_maximum_fusion.1) | copy-start | bytes 1179652
  61.0 11.2 %collective-permute-start.5 = (bf16[192,1024]{1,0:T(8,128)(2,1)}, bf16[192,1024]{1,0:T(8,128)(2,1)}, u32[]{:S(2)}, u32[]{:S(2)}) collective-permute-start(bf16[192,1024]{1,0:T(8,128)(2,1)} %collective-permute-done.2), channel_id=1, source_target_pairs={{0,16},{16,32},{32,48},{48,64},{64,80},{80,96},{96,112},{112,0},{1... | collective-permute-start | bytes 1179656 | tf_op jit(solution)/shard_map/ppermute | solution.py:30
  62.9 13.5 %collective-permute-start.6 = (bf16[192,1024]{1,0:T(8,128)(2,1)S(1)}, bf16[192,1024]{1,0:T(8,128)(2,1)}, u32[]{:S(2)}, u32[]{:S(2)}) collective-permute-start(bf16[192,1024]{1,0:T(8,128)(2,1)S(1)} %pad_maximum_fusion.1), channel_id=1, source_target_pairs={{0,16},{16,32},{32,48},{48,64},{64,80},{80,96},{96,112},{112,0},{1... | collective-permute-start | bytes 1179656 | tf_op jit(solution)/shard_map/ppermute | solution.py:30
  76.6 12.4 %collective-permute-start.8 = (bf16[768,256]{1,0:T(8,128)(2,1)S(1)}, bf16[768,256]{1,0:T(8,128)(2,1)S(1)}, u32[]{:S(2)}, u32[]{:S(2)}) collective-permute-start(bf16[768,256]{1,0:T(8,128)(2,1)S(1)} %get-tuple-element.39), channel_id=1, source_target_pairs={{0,128},{128,0},{1,129},{129,1},{2,130},{130,2},{3,131},{131,3},{4... | collective-permute-start | bytes 1179656 | tf_op jit(solution)/shard_map/ppermute | solution.py:25
  79.5 8.8 %collective-permute-start.7 = (bf16[96,1024]{1,0:T(8,128)(2,1)S(1)}, bf16[96,1024]{1,0:T(8,128)(2,1)S(1)}, u32[]{:S(2)}, u32[]{:S(2)}) collective-permute-start(bf16[96,1024]{1,0:T(8,128)(2,1)S(1)} %slice_select_fusion.3), channel_id=1, source_target_pairs={{0,16},{16,32},{32,48},{48,64},{64,80},{80,96},{96,112},{112,0},{1... | collective-permute-start | bytes 589832 | tf_op jit(solution)/shard_map/ppermute | solution.py:30
  83.3 11.1 %collective-permute-start.10 = (bf16[192,1024]{1,0:T(8,128)(2,1)}, bf16[192,1024]{1,0:T(8,128)(2,1)S(1)}, u32[]{:S(2)}, u32[]{:S(2)}) collective-permute-start(bf16[192,1024]{1,0:T(8,128)(2,1)} %collective-permute-done.6), channel_id=1, source_target_pairs={{0,16},{16,32},{32,48},{48,64},{64,80},{80,96},{96,112},{112,0},{1... | collective-permute-start | bytes 1179656 | tf_op jit(solution)/shard_map/ppermute | solution.py:30
  89.0 4.3 %copy-start.3 = (bf16[768,256]{1,0:T(8,128)(2,1)}, bf16[768,256]{1,0:T(8,128)(2,1)S(1)}, u32[]{:S(2)}) copy-start(bf16[768,256]{1,0:T(8,128)(2,1)S(1)} %collective-permute-done.8) | copy-start | bytes 1179652
  91.2 14.7 %collective-permute-start.9 = (f32[256,1024]{1,0:T(8,128)S(1)}, f32[256,1024]{1,0:T(8,128)S(1)}, u32[]{:S(2)}, u32[]{:S(2)}) collective-permute-start(f32[256,1024]{1,0:T(8,128)S(1)} %fusion.13), channel_id=1, source_target_pairs={{0,128},{128,0},{1,129},{129,1},{2,130},{130,2},{3,131},{131,3},{4... | collective-permute-start | bytes 3145736 | tf_op jit(solution)/shard_map/ppermute | solution.py:25
  93.6 3.6 %copy-start.1 = (bf16[192,1024]{1,0:T(8,128)(2,1)S(1)}, bf16[192,1024]{1,0:T(8,128)(2,1)}, u32[]{:S(2)}) copy-start(bf16[192,1024]{1,0:T(8,128)(2,1)} %copy-done) | copy-start | bytes 1179652
  94.3 10.9 %collective-permute-start.11 = (bf16[192,1024]{1,0:T(8,128)(2,1)S(1)}, bf16[192,1024]{1,0:T(8,128)(2,1)S(1)}, u32[]{:S(2)}, u32[]{:S(2)}) collective-permute-start(bf16[192,1024]{1,0:T(8,128)(2,1)S(1)} %collective-permute-done.10), channel_id=1, source_target_pairs={{0,16},{16,32},{32,48},{48,64},{64,80},{80,96},{96,112},{112,0},{1... | collective-permute-start | bytes 1179656 | tf_op jit(solution)/shard_map/ppermute | solution.py:30
  108.8 10.3 %collective-permute-start.12 = (bf16[96,1024]{1,0:T(8,128)(2,1)}, bf16[96,1024]{1,0:T(8,128)(2,1)}, u32[]{:S(2)}, u32[]{:S(2)}) collective-permute-start(bf16[96,1024]{1,0:T(8,128)(2,1)} %slice_select_fusion.2), channel_id=1, source_target_pairs={{0,16},{16,32},{32,48},{48,64},{64,80},{80,96},{96,112},{112,0},{1... | collective-permute-start | bytes 589832 | tf_op jit(solution)/shard_map/ppermute | solution.py:30
  110.8 23.4 %all-to-all-start.1 = ((f16[16,16,1024]{2,1,0:T(8,128)(2,1)}), f16[16,16,1024]{2,1,0:T(8,128)(2,1)S(1)}, u32[]{:S(2)}, u32[]{:S(2)}) async-start(f16[16,16,1024]{2,1,0:T(8,128)(2,1)} %bitcast.89), calls=%async_computation.1 | async-start | bytes 1048576 | tf_op jit(solution)/shard_map/all_to_all | solution.py:93
  122.7 11.7 %collective-permute-start.13 = (f32[256,1024]{1,0:T(8,128)}, f32[256,1024]{1,0:T(8,128)}, u32[]{:S(2)}, u32[]{:S(2)}) collective-permute-start(f32[256,1024]{1,0:T(8,128)} %fusion.14), channel_id=1, source_target_pairs={{0,128},{128,0},{1,129},{129,1},{2,130},{130,2},{3,131},{131,3},{4... | collective-permute-start | bytes 3145736 | tf_op jit(solution)/shard_map/ppermute | solution.py:25
  136.5 19.2 %copy-start.6 = (f32[16,2,1024]{2,1,0:T(2,128)S(1)}, f32[16,2,1024]{2,1,0:T(2,128)}, u32[]{:S(2)}) copy-start(f32[16,2,1024]{2,1,0:T(2,128)} %param.10) | copy-start | bytes 393220
  136.5 19.2 %copy-start.7 = (f32[16,2,1024]{2,1,0:T(2,128)S(1)}, f32[16,2,1024]{2,1,0:T(2,128)}, u32[]{:S(2)}) copy-start(f32[16,2,1024]{2,1,0:T(2,128)} %param.11) | copy-start | bytes 393220
  (1 other events, 2.4 us)

commit v4 on v1

v4 whole, which is shorter than its diff:
```python
import jax
import jax.numpy as jnp
from jax import lax
from jax.sharding import Mesh, PartitionSpec as P

inner_rate = 0.8
momentum_decay = 0.9
outer_rate = 0.7

f32, f16, bf16 = jnp.float32, jnp.float16, jnp.bfloat16


def body(activations, cotangents, inner_drift, drift_flags, master_weights, outer_momentum):
    n_core, n_z, n_yl, n_x = (lax.axis_size(a) for a in ("core", "z", "yl", "x"))
    replicas = n_yl * n_x
    core = lax.axis_index("core")
    tokens, width = activations.shape[1], activations.shape[2]
    own_rows = master_weights.shape[0]
    rows, kvw = inner_drift.shape[1], inner_drift.shape[3]

    low_half = lax.axis_index("yh") == 0
    first_core = core == 0

    def swap(value, axis):
        return lax.ppermute(value, axis, [(0, 1), (1, 0)])

    def ordered(first, mine, other):
        return [jnp.where(first, mine, other), jnp.where(first, other, mine)]

    def of_core(pair):
        kept, sent = ordered(first_core, pair[0], pair[1])
        return jnp.concatenate(ordered(first_core, kept, swap(sent, "core")), axis=1)

    acts = activations[0].reshape(tokens, n_z, rows).swapaxes(0, 1)
    acts = lax.all_to_all(acts, "z", 0, 0, tiled=True).reshape(n_z * tokens, rows)
    cots = cotangents[0].swapaxes(0, 1)
    mine = jnp.concatenate(ordered(low_half, of_core(cots), of_core(swap(cots, "yh"))), axis=1)

    mine, acts, drift = lax.optimization_barrier((mine, acts, inner_drift[0]))
    portion = lax.all_gather(mine, "z", axis=0, tiled=True)

    acts_pair = lax.all_to_all(jnp.broadcast_to(acts[None], (n_core,) + acts.shape), "core", 0, 0, tiled=True)

    drift_pair = lax.all_to_all(drift.swapaxes(0, 1), "core", 0, 0, tiled=True)

    flag = lax.dynamic_index_in_dim(drift_flags[0], core, 0, keepdims=False).astype(f32)
    grads = lax.dot_general(acts_pair, portion, (((1,), (0,)), ((), ())), preferred_element_type=f32)
    term = flag * (drift_pair + inner_rate * grads)

    sent = term.astype(f16).reshape(n_core * replicas, own_rows, kvw)
    got = lax.all_to_all(sent, ("core", "yl", "x"), 0, 0, tiled=True)
    drift_sum = got.astype(f32).reshape(2, replicas, own_rows, kvw).sum(1).swapaxes(0, 1)

    delta = drift_sum / replicas
    new_momentum = momentum_decay * outer_momentum + delta
    new_master = master_weights - outer_rate * (delta + momentum_decay * new_momentum)

    fresh = jnp.broadcast_to(new_master.astype(bf16)[None], (replicas, own_rows, 2, kvw))
    fresh_copy = lax.all_to_all(fresh, ("yl", "x"), 0, 0, tiled=True).reshape(rows, 2, kvw)
    return (new_master, new_momentum, fresh_copy)


def solution(mesh):
    split = Mesh(mesh.devices.reshape(2, 2, 8, 4, 4), ("yh", "core", "z", "yl", "x"))
    tensor, replica = ("yh", "core"), ("yl", "x")
    return jax.shard_map(
        body,
        mesh=split,
        in_specs=(
            P(replica, "z", tensor),
            P(replica, "z", None, tensor),
            P(replica, tensor + ("z",), None, None),
            P(replica, None),
            P(tensor + ("z",) + replica, None, None),
            P(tensor + ("z",) + replica, None, None),
        ),
        out_specs=(
            P(tensor + ("z",) + replica, None, None),
            P(tensor + ("z",) + replica, None, None),
            P(tensor + ("z",), None, None),
        ),
        check_vma=False,
    )
```

time: 171 us -> 172 us (level)
  the two profiles are of different devices: /device:TPU:2 before, /device:TPU:8 now
where the time goes in v4:
time: 172 us; the launch traced here: 171 us
  waiting for transfers between devices  65.1 us (38%)
  blocking collectives  46.9 us (27%)
  starting transfers between devices  26 us (15%)
  between operations  14.2 us (8%)
  local copies, waits for them, and re-layouts  11.4 us (7%)
  matrix products  5.49 us (3%)
  other arithmetic  1.83 us (1%)
    all_to_all x1, blocking collectives, body(): got = lax.all_to_all(sent, ('core', 'yl', 'x'), 0, 0, tiled=True)  34.7 us
    all_gather x1, waiting for transfers between devices, body(): portion = lax.all_gather(mine, 'z', axis=0, tiled=True)  32 us
    all_to_all x1, waiting for transfers between devices, body(): lax.all_to_all(fresh, ('yl', 'x'), 0, 0, tiled=True).reshape(rows, 2, kvw)  24.1 us
    ppermute x3, starting transfers between devices, swap(): return lax.ppermute(value, axis, [(0, 1), (1, 0)])  10.7 us
    all_to_all x1, starting transfers between devices, body(): lax.all_to_all(acts, 'z', 0, 0, tiled=True).reshape(n_z * tokens, rows)  10.3 us
    all_to_all x1, blocking collectives, body(): drift_pair = lax.all_to_all(drift.swapaxes(0, 1), 'core', 0, 0, tiled=True)  6.31 us
    unnamed x14, local copies, waits for them, and re-layouts  6.16 us
    all_to_all x1, blocking collectives, body(): lax.all_to_all(jnp.broadcast_to(acts[None], (n_core,) + acts.shape), 'cor...  5.89 us
  transfers between devices with their start and end apart: 6, of which 5 were waited for; matrix products, arithmetic and copies ran while one was open for 5% of the time, Pallas kernels for 0%

profile of v4, /device:TPU:8, one launch (start us, length us, event | category | flops | bytes accessed | tf_op | source)
XLA Modules:
  0.0 171.0 jit_solution(13970429571375946496)
XLA Ops:
  7.2 1.4 copy.28
  8.5 1.0 copy.20
  9.6 10.3 %all-to-all-start = ((bf16[8,192,256]{2,1,0:T(8,128)(2,1)}), bf16[8,192,256]{2,1,0:T(8,128)(2,1)S(1)}, u32[]{:S(2)}, u32[]{:S(2)}) async-start(bf16[8,192,256]{2,1,0:T(8,128)(2,1)} %copy.20), calls=%async_computation | async-start | bytes 1572864 | tf_op jit(solution)/shard_map/all_to_all | solution.py:35
  20.0 6.8 %collective-permute-start.1 = (bf16[2,192,256]{2,1,0:T(8,128)(2,1)S(1)}, bf16[2,192,256]{2,1,0:T(8,128)(2,1)S(1)}, u32[]{:S(2)}, u32[]{:S(2)}) collective-permute-start(bf16[2,192,256]{2,1,0:T(8,128)(2,1)S(1)} %bitcast.51), channel_id=1, source_target_pairs={{0,256},{256,0},{1,257},{257,1},{2,258},{258,2},{3,259},{259,3},{4... | collective-permute-start | bytes 589832 | tf_op jit(solution)/shard_map/ppermute | solution.py:25
  26.9 1.9 %collective-permute-start = (bf16[192,256]{1,0:T(8,128)(2,1)S(1)}, bf16[192,256]{1,0:T(8,128)(2,1)S(1)}, u32[]{:S(2)}, u32[]{:S(2)}) collective-permute-start(bf16[192,256]{1,0:T(8,128)(2,1)S(1)} %select_bitcast_fusion.1), channel_id=1, source_target_pairs={{0,128},{128,0},{1,129},{129,1},{2,130},{130,2},{3,131},{131,3},{4... | collective-permute-start | bytes 294920 | tf_op jit(solution)/shard_map/ppermute | solution.py:25
  28.8 2.3 %copy.39 = f32[1,256,2,1024]{3,1,2,0:T(8,128)S(1)} copy(f32[1,256,2,1024]{3,2,1,0:T(2,128)} %param.8) | data formatting | bytes 4194304 | tf_op args[2]
  31.1 3.8 %collective-permute-done.1 = bf16[2,192,256]{2,1,0:T(8,128)(2,1)S(1)} collective-permute-done((bf16[2,192,256]{2,1,0:T(8,128)(2,1)S(1)}, bf16[2,192,256]{2,1,0:T(8,128)(2,1)S(1)}, u32[]{:S(2)}, u32[]{:S(2)}) %collective-permute-start.1) | collective-permute-done | bytes 196640 | tf_op jit(solution)/shard_map/ppermute | solution.py:25
  34.9 1.9 %collective-permute-start.2 = (bf16[192,256]{1,0:T(8,128)(2,1)S(1)}, bf16[192,256]{1,0:T(8,128)(2,1)S(1)}, u32[]{:S(2)}, u32[]{:S(2)}) collective-permute-start(bf16[192,256]{1,0:T(8,128)(2,1)S(1)} %select_bitcast_fusion), channel_id=1, source_target_pairs={{0,128},{128,0},{1,129},{129,1},{2,130},{130,2},{3,131},{131,3},{4... | collective-permute-start | bytes 294920 | tf_op jit(solution)/shard_map/ppermute | solution.py:25
  36.8 1.2 collective-permute-done.2
  38.2 0.8 pad_maximum_fusion
  39.0 4.0 %all-to-all-done = bf16[8,192,256]{2,1,0:T(8,128)(2,1)S(1)} async-done(((bf16[8,192,256]{2,1,0:T(8,128)(2,1)}), bf16[8,192,256]{2,1,0:T(8,128)(2,1)S(1)}, u32[]{:S(2)}, u32[]{:S(2)}) %all-to-all-start) | async-done | bytes 786464 | tf_op jit(solution)/shard_map/all_to_all | solution.py:35
  43.6 1.2 copy.22
  44.8 1.2 broadcast_in_dim.4
  46.0 5.9 %all_to_all.25 = bf16[2,1536,256]{1,2,0:T(8,128)(2,1)} all-to-all(bf16[2,1536,256]{1,2,0:T(8,128)(2,1)S(1)} %broadcast_in_dim.4), channel_id=1, replica_groups=mesh['yh'=2,'core'=2,'z'=8,'yl'=4,'x'=4] {'core'}, dimensions={0} | all-to-all | bytes 3145728 | tf_op jit(solution)/shard_map/all_to_all | solution.py:42
  51.9 6.3 %all_to_all.26 = f32[2,256,1024]{2,1,0:T(8,128)} all-to-all(f32[2,256,1024]{2,1,0:T(8,128)S(1)} %bitcast.47), channel_id=1, replica_groups=mesh['yh'=2,'core'=2,'z'=8,'yl'=4,'x'=4] {'core'}, dimensions={0} | all-to-all | bytes 4194304 | tf_op jit(solution)/shard_map/all_to_all | solution.py:44
  58.2 32.0 %all-gather.2.cloned.1.call-done = bf16[1536,1024]{1,0:T(8,128)(2,1)} async-done(((bf16[192,1024]{1,0:T(8,128)(2,1)}), bf16[1536,1024]{1,0:T(8,128)(2,1)}) %all-gather.2.cloned.1.call-update) | async-done | bytes 3145744 | tf_op jit(solution)/shard_map/all_gather | solution.py:40
  90.2 5.5 %multiply_convert_fusion = f16[2,256,1024]{2,1,0:T(8,128)(2,1)S(1)} fusion(f32[2,256,1024]{2,1,0:T(8,128)} %all_to_all.26, bf16[2,1536,256]{1,2,0:T(8,128)(2,1)} %all_to_all.25, bf16[1536,1024]{1,0:T(8,128)(2,1)} %all-gather.2.cloned.1.call-done, f32[]{:T(128)} %bitcast), kind=kOutput, calls=%fused_computation.4 | convolution fusion | flops 1612709888 | bytes 7864324 | tf_op jit(solution)/shard_map/dot_general | solution.py:47
  95.7 34.7 %all_to_all.27 = f16[32,16,1024]{2,1,0:T(8,128)(2,1)S(1)} all-to-all(f16[32,16,1024]{2,1,0:T(8,128)(2,1)S(1)} %bitcast.54), channel_id=1, replica_groups=mesh['yh'=2,'core'=2,'z'=8,'yl'=4,'x'=4] {'core','yl','x'}, dimensions={0} | all-to-all | bytes 2097152 | tf_op jit(solution)/shard_map/all_to_all | solution.py:51
  130.9 1.8 %broadcast_in_dim.5 = bf16[16,16,2,1024]{3,2,1,0:T(2,128)(2,1)} broadcast(bf16[16,2,1024]{2,1,0:T(2,128)(2,1)S(1)} %copy.25), dimensions={1,2,3} | broadcast | bytes 1114112 | tf_op jit(solution)/shard_map/broadcast_in_dim | solution.py:58
  132.6 5.0 %all-to-all-start.4 = ((bf16[16,16,2,1024]{3,2,1,0:T(2,128)(2,1)}), bf16[16,16,2,1024]{3,2,1,0:T(2,128)(2,1)S(1)}, u32[]{:S(2)}, u32[]{:S(2)}) async-start(bf16[16,16,2,1024]{3,2,1,0:T(2,128)(2,1)} %broadcast_in_dim.5), calls=%async_computation.4 | async-start | bytes 2097152 | tf_op jit(solution)/shard_map/all_to_all | solution.py:59
  137.6 0.8 copy.26
  138.4 0.8 copy.27
  139.1 24.1 %all-to-all-done.4 = bf16[16,16,2,1024]{3,2,1,0:T(2,128)(2,1)S(1)} async-done(((bf16[16,16,2,1024]{3,2,1,0:T(2,128)(2,1)}), bf16[16,16,2,1024]{3,2,1,0:T(2,128)(2,1)S(1)}, u32[]{:S(2)}, u32[]{:S(2)}) %all-to-all-start.4) | async-done | bytes 1048608 | tf_op jit(solution)/shard_map/all_to_all | solution.py:59
  163.2 1.0 copy.42
  (21 shorter events, 1.2 us)
Async XLA Ops:
  7.2 12.8 %copy-start = (bf16[1,192,2,256]{3,2,1,0:T(2,128)(2,1)S(1)}, bf16[1,192,2,256]{3,2,1,0:T(2,128)(2,1)}, u32[]{:S(2)}) copy-start(bf16[1,192,2,256]{3,2,1,0:T(2,128)(2,1)} %param.7) | copy-start | bytes 589828
  9.6 33.4 %all-to-all-start = ((bf16[8,192,256]{2,1,0:T(8,128)(2,1)}), bf16[8,192,256]{2,1,0:T(8,128)(2,1)S(1)}, u32[]{:S(2)}, u32[]{:S(2)}) async-start(bf16[8,192,256]{2,1,0:T(8,128)(2,1)} %copy.20), calls=%async_computation | async-start | bytes 1572864 | tf_op jit(solution)/shard_map/all_to_all | solution.py:35
  19.9 70.3 %all-gather.2.cloned.1.call-start = ((), (), s32[]{:S(2)}) async-start(), calls=%async_computation.5 | async-start | bytes 3538944 | tf_op jit(solution)/shard_map/all_gather | solution.py:40
  20.0 14.9 %collective-permute-start.1 = (bf16[2,192,256]{2,1,0:T(8,128)(2,1)S(1)}, bf16[2,192,256]{2,1,0:T(8,128)(2,1)S(1)}, u32[]{:S(2)}, u32[]{:S(2)}) collective-permute-start(bf16[2,192,256]{2,1,0:T(8,128)(2,1)S(1)} %bitcast.51), channel_id=1, source_target_pairs={{0,256},{256,0},{1,257},{257,1},{2,258},{258,2},{3,259},{259,3},{4... | collective-permute-start | bytes 589832 | tf_op jit(solution)/shard_map/ppermute | solution.py:25
  26.9 9.9 %collective-permute-start = (bf16[192,256]{1,0:T(8,128)(2,1)S(1)}, bf16[192,256]{1,0:T(8,128)(2,1)S(1)}, u32[]{:S(2)}, u32[]{:S(2)}) collective-permute-start(bf16[192,256]{1,0:T(8,128)(2,1)S(1)} %select_bitcast_fusion.1), channel_id=1, source_target_pairs={{0,128},{128,0},{1,129},{129,1},{2,130},{130,2},{3,131},{131,3},{4... | collective-permute-start | bytes 294920 | tf_op jit(solution)/shard_map/ppermute | solution.py:25
  31.1 12.0 %copy-start.3 = (s32[1,2]{1,0:T(1,128)S(1)}, s32[1,2]{1,0:T(1,128)}, u32[]{:S(2)}) copy-start(s32[1,2]{1,0:T(1,128)} %param.9) | copy-start | bytes 28
  34.9 3.2 %collective-permute-start.2 = (bf16[192,256]{1,0:T(8,128)(2,1)S(1)}, bf16[192,256]{1,0:T(8,128)(2,1)S(1)}, u32[]{:S(2)}, u32[]{:S(2)}) collective-permute-start(bf16[192,256]{1,0:T(8,128)(2,1)S(1)} %select_bitcast_fusion), channel_id=1, source_target_pairs={{0,128},{128,0},{1,129},{129,1},{2,130},{130,2},{3,131},{131,3},{4... | collective-permute-start | bytes 294920 | tf_op jit(solution)/shard_map/ppermute | solution.py:25
  95.7 35.0 %copy-start.1 = (f32[16,2,1024]{2,1,0:T(2,128)S(1)}, f32[16,2,1024]{2,1,0:T(2,128)}, u32[]{:S(2)}) copy-start(f32[16,2,1024]{2,1,0:T(2,128)} %param.11) | copy-start | bytes 393220
  95.7 35.0 %copy-start.2 = (f32[16,2,1024]{2,1,0:T(2,128)S(1)}, f32[16,2,1024]{2,1,0:T(2,128)}, u32[]{:S(2)}) copy-start(f32[16,2,1024]{2,1,0:T(2,128)} %param.10) | copy-start | bytes 393220
  132.6 30.6 %all-to-all-start.4 = ((bf16[16,16,2,1024]{3,2,1,0:T(2,128)(2,1)}), bf16[16,16,2,1024]{3,2,1,0:T(2,128)(2,1)S(1)}, u32[]{:S(2)}, u32[]{:S(2)}) async-start(bf16[16,16,2,1024]{3,2,1,0:T(2,128)(2,1)} %broadcast_in_dim.5), calls=%async_computation.4 | async-start | bytes 2097152 | tf_op jit(solution)/shard_map/all_to_all | solution.py:59
Sparse Core Ops, SparseCore 0:
  43.2 46.9 all-gather.1

commit v5 on v2

v5 whole, which is shorter than its diff:
```python
import functools

import jax
import jax.numpy as jnp
from jax import lax
from jax.experimental import pallas as pl
from jax.experimental.pallas import tpu as pltpu
from jax.sharding import Mesh, PartitionSpec as P

inner_rate = 0.8
momentum_decay = 0.9
outer_rate = 0.7

f32, f16, bf16 = jnp.float32, jnp.float16, jnp.bfloat16


def product_kernel(n, place, acts, *rest):
    blocks, out = rest[:n], rest[n]
    part = blocks[0].shape[0] // 2
    first, second = (pl.ds(pl.multiple_of(place[n + i], 32), part) for i in range(2))
    for i, block in enumerate(blocks):
        tokens = acts[place[i], first, :]
        if 0 < i < n - 1:
            tokens = jnp.concatenate([tokens, acts[place[i], second, :]], axis=0)
        value = block[...] if i > 0 else block[:part]
        product = lax.dot_general(tokens, value, (((0,), (0,)), ((), ())), preferred_element_type=f32)
        if i == 0:
            out[...] = product
        else:
            out[...] += product


def product(place, acts, blocks):
    rows, columns = acts.shape[2], blocks[0].shape[1]
    depth = acts.shape[0] * acts.shape[1] // 2
    return pl.pallas_call(
        functools.partial(product_kernel, len(blocks)),
        out_shape=jax.ShapeDtypeStruct((rows, columns), f32),
        in_specs=[pl.BlockSpec(memory_space=pltpu.SMEM)] + [pl.BlockSpec(memory_space=pltpu.VMEM)] * (1 + len(blocks)),
        out_specs=pl.BlockSpec(memory_space=pltpu.VMEM),
        compiler_params=pltpu.CompilerParams(vmem_limit_bytes=24 * 2**20),
        cost_estimate=pl.CostEstimate(
            flops=2 * depth * rows * columns, bytes_accessed=2 * depth * (rows + columns) + 4 * rows * columns, transcendentals=0
        ),
        name="token_half_product",
    )(place, acts, *blocks)


def body(activations, cotangents, inner_drift, drift_flags, master_weights, outer_momentum):
    n_z, replicas = lax.axis_size("z"), lax.axis_size("yl") * lax.axis_size("x")
    first_core = lax.axis_index("core") == 0
    low_half = lax.axis_index("yh") == 0
    z = lax.axis_index("z")
    tokens = activations.shape[1]
    part = tokens // 2
    own_rows = master_weights.shape[0]
    rows, kvw = inner_drift.shape[1], inner_drift.shape[3]
    half = kvw // 2

    def swap(value, axis):
        return lax.ppermute(value, axis, [(0, 1), (1, 0)])

    ways = [(i, (i + 1) % n_z) for i in range(n_z)] + [(n_z + i, n_z + (i - 1) % n_z) for i in range(n_z)]

    def step(value):
        return lax.ppermute(value, ("core", "z"), ways)

    def tied(*values):
        return lax.optimization_barrier(values)

    def chip(mine, other):
        mine, other = ([jnp.where(first_core, v, jnp.roll(v, part, axis=0)) for v in (w[0], w[1])] for w in (mine, other))
        pairs = [jnp.where(first_core, a, b) for k in range(2) for a, b in ((mine[k], other[k]), (other[k], mine[k]))]
        return jnp.concatenate(pairs, axis=1)

    def ring(block):
        held = [block]
        for _ in range(n_z // 2 - 1):
            block = step(block)
            held.append(block)
        held.append(step(block[:part]))
        return held

    acts = activations[0].reshape(tokens, n_z, rows).swapaxes(0, 1)
    acts = lax.all_to_all(acts, "z", 0, 0, tiled=True)
    acts_other = swap(acts, "core")
    sign = jnp.where(first_core, -1, 1)
    places = [(z + n_z + sign * s) % n_z for s in range(n_z // 2 + 1)]
    place = jnp.stack(places + [jnp.where(first_core, 0, part), jnp.where(first_core, part, 0)]).astype(jnp.int32)

    cots = cotangents[0].swapaxes(0, 1)
    far = swap(cots, "yh")
    near_held = ring(chip(cots, swap(cots, "core")))
    far_held = ring(chip(far, swap(far, "core")))

    flags = jnp.repeat(drift_flags[0].astype(f32), half)[None]
    drift = inner_drift[0].swapaxes(0, 1)

    def half_of(low):
        return jnp.concatenate(list(jnp.where(low, drift[:, :, :half], drift[:, :, half:])), axis=1)

    near_drift, far_drift, acts_other = tied(half_of(low_half), half_of(~low_half), acts_other)

    def term(held, drifts):
        came = swap(product(place, acts_other, held), "core")
        grads = product(place, acts, held) + came
        return (flags * (drifts + inner_rate * grads)).astype(f16)

    def reduced(value):
        got = lax.all_to_all(value.reshape(replicas, own_rows, -1), ("yl", "x"), 0, 0, tiled=True)
        return got.astype(f32).sum(0)

    near_term = term(near_held, near_drift)
    total = reduced(jnp.concatenate([near_term, term(far_held, far_drift)], axis=1))
    total = total.reshape(own_rows, 2, 2, half)
    low, high = jnp.where(low_half, total[:, 0], total[:, 1]), jnp.where(low_half, total[:, 1], total[:, 0])
    drift_sum = jnp.concatenate([low, high], axis=2)

    delta = drift_sum / replicas
    new_momentum = momentum_decay * outer_momentum + delta
    new_master = master_weights - outer_rate * (delta + momentum_decay * new_momentum)

    fresh = jnp.broadcast_to(new_master.astype(bf16)[None], (replicas, own_rows, 2, kvw))
    fresh_copy = lax.all_to_all(fresh, ("yl", "x"), 0, 0, tiled=True).reshape(rows, 2, kvw)
    return (new_master, new_momentum, fresh_copy)


def solution(mesh):
    split = Mesh(mesh.devices.reshape(2, 2, 8, 4, 4), ("yh", "core", "z", "yl", "x"))
    tensor, replica = ("yh", "core"), ("yl", "x")
    return jax.shard_map(
        body,
        mesh=split,
        in_specs=(
            P(replica, "z", tensor),
            P(replica, "z", None, tensor),
            P(replica, tensor + ("z",), None, None),
            P(replica, None),
            P(tensor + ("z",) + replica, None, None),
            P(tensor + ("z",) + replica, None, None),
        ),
        out_specs=(
            P(tensor + ("z",) + replica, None, None),
            P(tensor + ("z",) + replica, None, None),
            P(tensor + ("z",), None, None),
        ),
        check_vma=False,
    )
```

time: 175 us -> 161 us (0.920)
  Pallas kernels: 0 us -> 7.8 us
  matrix products: 6.79 us -> 0 us
  local copies, waits for them, and re-layouts: 17.9 us -> 11.6 us
  waiting for transfers between devices: 27 us -> 21 us
  other arithmetic: 8.73 us -> 6.67 us
    pallas_call x0 -> x4, Pallas kernels: none -> 7.8 us  [product(): pl.pallas_call(functools.partial(product_kernel, len(blocks)), out_shape=...]
    unnamed x27 -> x18, local copies, waits for them, and re-layouts: 14.4 us -> 6.97 us
    ppermute x8, waiting for transfers between devices: 27 us -> 20 us  [step(): return lax.ppermute(value, ('core', 'z'), ways)]
    dot_general x4 -> x0, matrix products: 6.79 us -> none  [the longest x2 3.63 us: gradient(): lax.dot_general(acts_mine, columns, dims, preferred_element_type=f32) + came]
    another operation x2 -> x0, other arithmetic: 3.12 us -> none
    another operation x0 -> x3, local copies, waits for them, and re-layouts: none -> 2.32 us  [the longest x1 1.2 us: half_of(): list(jnp.where(low, drift[:, :, :half], drift[:, :, half:]))]
    ppermute x8, starting transfers between devices: 19.2 us -> 21.2 us  [step(): return lax.ppermute(value, ('core', 'z'), ways)]
    ppermute x6, starting transfers between devices: 19.4 us -> 17.6 us  [swap(): return lax.ppermute(value, axis, [(0, 1), (1, 0)])]
  transfers between devices with their start and end apart: 15 -> 15, of which waited for: 4 -> 6; matrix products, arithmetic and copies ran while one was open for 14% -> 8% of each run, Pallas kernels for 0% -> 5%
where the time goes in v5:
time: 161 us; the launch traced here: 160 us
  blocking collectives  62.8 us (39%)
  starting transfers between devices  49 us (30%)
  waiting for transfers between devices  21 us (13%)
  local copies, waits for them, and re-layouts  11.6 us (7%)
  Pallas kernels  7.8 us (5%)
  other arithmetic  6.67 us (4%)
    all_to_all x1, blocking collectives, reduced(): lax.all_to_all(value.reshape(replicas, own_rows, -1), ('yl', 'x'), 0, 0,...  32.6 us
    all_to_all x1, blocking collectives, body(): lax.all_to_all(fresh, ('yl', 'x'), 0, 0, tiled=True).reshape(rows, 2, kvw)  30.2 us
    ppermute x8, starting transfers between devices, step(): return lax.ppermute(value, ('core', 'z'), ways)  21.2 us
    ppermute x8, waiting for transfers between devices, step(): return lax.ppermute(value, ('core', 'z'), ways)  20 us
    ppermute x6, starting transfers between devices, swap(): return lax.ppermute(value, axis, [(0, 1), (1, 0)])  17.6 us
    all_to_all x1, starting transfers between devices, body(): acts = lax.all_to_all(acts, 'z', 0, 0, tiled=True)  10.3 us
    pallas_call x4, Pallas kernels, product(): pl.pallas_call(functools.partial(product_kernel, len(blocks)), out_shape=...  7.8 us
    unnamed x18, local copies, waits for them, and re-layouts  6.97 us
  transfers between devices with their start and end apart: 15, of which 6 were waited for; matrix products, arithmetic and copies ran while one was open for 8% of the time, Pallas kernels for 5%

profile of v5, /device:TPU:8, one launch (start us, length us, event | category | flops | bytes accessed | tf_op | source)
XLA Modules:
  0.0 160.1 jit_solution(952347633325830328)
XLA Ops:
  1.6 1.9 %collective-permute-start.1 = (bf16[2,192,256]{2,1,0:T(8,128)(2,1)S(1)}, bf16[2,192,256]{2,1,0:T(8,128)(2,1)S(1)}, u32[]{:S(2)}, u32[]{:S(2)}) collective-permute-start(bf16[2,192,256]{2,1,0:T(8,128)(2,1)S(1)} %bitcast.154), channel_id=1, source_target_pairs={{0,128},{128,0},{1,129},{129,1},{2,130},{130,2},{3,131},{131,3},{4... | collective-permute-start | bytes 589832 | tf_op jit(solution)/shard_map/ppermute | solution.py:61
  3.5 6.8 %collective-permute-start.7 = (bf16[2,192,256]{2,1,0:T(8,128)(2,1)S(1)}, bf16[2,192,256]{2,1,0:T(8,128)(2,1)S(1)}, u32[]{:S(2)}, u32[]{:S(2)}) collective-permute-start(bf16[2,192,256]{2,1,0:T(8,128)(2,1)S(1)} %bitcast.155), channel_id=1, source_target_pairs={{0,256},{256,0},{1,257},{257,1},{2,258},{258,2},{3,259},{259,3},{4... | collective-permute-start | bytes 589832 | tf_op jit(solution)/shard_map/ppermute | solution.py:61
  12.7 10.3 %all-to-all-start = ((bf16[8,192,256]{2,1,0:T(8,128)(2,1)}), bf16[8,192,256]{2,1,0:T(8,128)(2,1)S(1)}, u32[]{:S(2)}, u32[]{:S(2)}) async-start(bf16[8,192,256]{2,1,0:T(8,128)(2,1)} %bitcast.148), calls=%async_computation | async-start | bytes 1572864 | tf_op jit(solution)/shard_map/all_to_all | solution.py:85
  23.3 3.9 %collective-permute-start.2 = (bf16[192,1024]{1,0:T(8,128)(2,1)S(1)}, bf16[192,1024]{1,0:T(8,128)(2,1)S(1)}, u32[]{:S(2)}, u32[]{:S(2)}) collective-permute-start(bf16[192,1024]{1,0:T(8,128)(2,1)S(1)} %pad_maximum_fusion.3.rest_0_), channel_id=1, source_target_pairs={{0,16},{16,32},{32,48},{48,64},{64,80},{80,96},{96,112},{112,0},{1... | collective-permute-start | bytes 1179656 | tf_op jit(solution)/shard_map/ppermute | solution.py:66
  27.2 2.5 %collective-permute-start.8 = (bf16[2,192,256]{2,1,0:T(8,128)(2,1)S(1)}, bf16[2,192,256]{2,1,0:T(8,128)(2,1)S(1)}, u32[]{:S(2)}, u32[]{:S(2)}) collective-permute-start(bf16[2,192,256]{2,1,0:T(8,128)(2,1)S(1)} %collective-permute-done.7), channel_id=1, source_target_pairs={{0,128},{128,0},{1,129},{129,1},{2,130},{130,2},{3,131},{131,3},{4... | collective-permute-start | bytes 589832 | tf_op jit(solution)/shard_map/ppermute | solution.py:61
  31.0 3.2 %collective-permute-start.9 = (bf16[192,1024]{1,0:T(8,128)(2,1)S(1)}, bf16[192,1024]{1,0:T(8,128)(2,1)S(1)}, u32[]{:S(2)}, u32[]{:S(2)}) collective-permute-start(bf16[192,1024]{1,0:T(8,128)(2,1)S(1)} %pad_maximum_fusion.4.rest_0_), channel_id=1, source_target_pairs={{0,16},{16,32},{32,48},{48,64},{64,80},{80,96},{96,112},{112,0},{1... | collective-permute-start | bytes 1179656 | tf_op jit(solution)/shard_map/ppermute | solution.py:66
  34.1 13.9 %collective-permute-done.2.rest_1_ = bf16[192,1024]{1,0:T(8,128)(2,1)S(1)} collective-permute-done((bf16[192,1024]{1,0:T(8,128)(2,1)S(1)}, bf16[192,1024]{1,0:T(8,128)(2,1)S(1)}, u32[]{:S(2)}, u32[]{:S(2)}) %collective-permute-start.2) | collective-permute-done | bytes 393248 | tf_op jit(solution)/shard_map/ppermute | solution.py:66
  48.1 1.9 %collective-permute-start.3 = (bf16[192,1024]{1,0:T(8,128)(2,1)S(1)}, bf16[192,1024]{1,0:T(8,128)(2,1)}, u32[]{:S(2)}, u32[]{:S(2)}) collective-permute-start(bf16[192,1024]{1,0:T(8,128)(2,1)S(1)} %collective-permute-done.2.rest_1_), channel_id=1, source_target_pairs={{0,16},{16,32},{32,48},{48,64},{64,80},{80,96},{96,112},{112,0},{1... | collective-permute-start | bytes 1179656 | tf_op jit(solution)/shard_map/ppermute | solution.py:66
  50.0 2.3 %collective-permute-done.9.rest_1_ = bf16[192,1024]{1,0:T(8,128)(2,1)S(1)} collective-permute-done((bf16[192,1024]{1,0:T(8,128)(2,1)S(1)}, bf16[192,1024]{1,0:T(8,128)(2,1)S(1)}, u32[]{:S(2)}, u32[]{:S(2)}) %collective-permute-start.9) | collective-permute-done | bytes 393248 | tf_op jit(solution)/shard_map/ppermute | solution.py:66
  52.3 1.9 %collective-permute-start.10 = (bf16[192,1024]{1,0:T(8,128)(2,1)S(1)}, bf16[192,1024]{1,0:T(8,128)(2,1)}, u32[]{:S(2)}, u32[]{:S(2)}) collective-permute-start(bf16[192,1024]{1,0:T(8,128)(2,1)S(1)} %collective-permute-done.9.rest_1_), channel_id=1, source_target_pairs={{0,16},{16,32},{32,48},{48,64},{64,80},{80,96},{96,112},{112,0},{1... | collective-permute-start | bytes 1179656 | tf_op jit(solution)/shard_map/ppermute | solution.py:66
  54.2 3.6 %copy.24 = f32[1,256,2,1024]{3,1,2,0:T(8,128)} copy(f32[1,256,2,1024]{3,2,1,0:T(2,128)} %param.8) | data formatting | bytes 4194304 | tf_op args[2]
  59.0 1.9 %collective-permute-start.4 = (bf16[192,1024]{1,0:T(8,128)(2,1)}, bf16[192,1024]{1,0:T(8,128)(2,1)S(1)}, u32[]{:S(2)}, u32[]{:S(2)}) collective-permute-start(bf16[192,1024]{1,0:T(8,128)(2,1)} %collective-permute-done.3.rest_2_), channel_id=1, source_target_pairs={{0,16},{16,32},{32,48},{48,64},{64,80},{80,96},{96,112},{112,0},{1... | collective-permute-start | bytes 1179656 | tf_op jit(solution)/shard_map/ppermute | solution.py:66
  60.9 2.3 %collective-permute-done.10.rest_2_ = bf16[192,1024]{1,0:T(8,128)(2,1)} collective-permute-done((bf16[192,1024]{1,0:T(8,128)(2,1)S(1)}, bf16[192,1024]{1,0:T(8,128)(2,1)}, u32[]{:S(2)}, u32[]{:S(2)}) %collective-permute-start.10) | collective-permute-done | bytes 393248 | tf_op jit(solution)/shard_map/ppermute | solution.py:66
  65.2 1.9 %collective-permute-start = (bf16[8,192,256]{2,1,0:T(8,128)(2,1)S(1)}, bf16[8,192,256]{2,1,0:T(8,128)(2,1)S(1)}, u32[]{:S(2)}, u32[]{:S(2)}) collective-permute-start(bf16[8,192,256]{2,1,0:T(8,128)(2,1)S(1)} %all-to-all-done.acts), channel_id=1, source_target_pairs={{0,128},{128,0},{1,129},{129,1},{2,130},{130,2},{3,131},{131,3},{4... | collective-permute-start | bytes 2359304 | tf_op jit(solution)/shard_map/ppermute | solution.py:61
  70.8 3.3 %collective-permute-start.5 = (bf16[96,1024]{1,0:T(8,128)(2,1)}, bf16[96,1024]{1,0:T(8,128)(2,1)}, u32[]{:S(2)}, u32[]{:S(2)}) collective-permute-start(bf16[96,1024]{1,0:T(8,128)(2,1)} %slice.220), channel_id=1, source_target_pairs={{0,16},{16,32},{32,48},{48,64},{64,80},{80,96},{96,112},{112,0},{1... | collective-permute-start | bytes 589832 | tf_op jit(solution)/shard_map/ppermute | solution.py:66
  75.0 3.1 %collective-permute-start.12 = (bf16[96,1024]{1,0:T(8,128)(2,1)}, bf16[96,1024]{1,0:T(8,128)(2,1)}, u32[]{:S(2)}, u32[]{:S(2)}) collective-permute-start(bf16[96,1024]{1,0:T(8,128)(2,1)} %slice.233), channel_id=1, source_target_pairs={{0,16},{16,32},{32,48},{48,64},{64,80},{80,96},{96,112},{112,0},{1... | collective-permute-start | bytes 589832 | tf_op jit(solution)/shard_map/ppermute | solution.py:66
  80.6 2.0 %token_half_product.5 = f32[256,1024]{1,0:T(8,128)S(1)} custom-call(s32[7]{0:T(128)S(1)} %stack.31.place, bf16[8,192,256]{2,1,0:T(8,128)(2,1)S(1)} %collective-permute-done.acts, bf16[192,1024]{1,0:T(8,128)(2,1)S(1)} %pad_maximum_fusion.3.rest_0_, bf16[192,1024]{1,0:T(8,128)(2,1)S(1)} %collective-permute-done.2.rest_1_, ...), custom_call_target="tpu_custom_call" | custom-call | flops 402653184 | bytes 3014656 | tf_op jit(solution)/shard_map/token_half_product/pallas_call | solution.py:36
  82.6 2.5 %collective-permute-start.6 = (f32[256,1024]{1,0:T(8,128)S(1)}, f32[256,1024]{1,0:T(8,128)S(1)}, u32[]{:S(2)}, u32[]{:S(2)}) collective-permute-start(f32[256,1024]{1,0:T(8,128)S(1)} %token_half_product.5), channel_id=1, source_target_pairs={{0,128},{128,0},{1,129},{129,1},{2,130},{130,2},{3,131},{131,3},{4... | collective-permute-start | bytes 3145736 | tf_op jit(solution)/shard_map/ppermute | solution.py:61
  85.1 1.9 %token_half_product.7 = f32[256,1024]{1,0:T(8,128)S(1)} custom-call(s32[7]{0:T(128)S(1)} %stack.31.place, bf16[8,192,256]{2,1,0:T(8,128)(2,1)S(1)} %collective-permute-done.acts, bf16[192,1024]{1,0:T(8,128)(2,1)S(1)} %pad_maximum_fusion.4.rest_0_, bf16[192,1024]{1,0:T(8,128)(2,1)S(1)} %copy-done.1, bf16[192,1024]{1,0:T(8,128)(2,1)} %collective-permute-done.10.rest_2_, ...), custom_call_target="tpu_custom_call" | custom-call | flops 402653184 | bytes 3014656 | tf_op jit(solution)/shard_map/token_half_product/pallas_call | solution.py:36
  87.0 1.9 %collective-permute-start.13 = (f32[256,1024]{1,0:T(8,128)S(1)}, f32[256,1024]{1,0:T(8,128)S(1)}, u32[]{:S(2)}, u32[]{:S(2)}) collective-permute-start(f32[256,1024]{1,0:T(8,128)S(1)} %token_half_product.7), channel_id=1, source_target_pairs={{0,128},{128,0},{1,129},{129,1},{2,130},{130,2},{3,131},{131,3},{4... | collective-permute-start | bytes 3145736 | tf_op jit(solution)/shard_map/ppermute | solution.py:61
  89.1 1.9 %token_half_product.4 = f32[256,1024]{1,0:T(8,128)S(1)} custom-call(s32[7]{0:T(128)S(1)} %stack.31.place, bf16[8,192,256]{2,1,0:T(8,128)(2,1)S(1)} %all-to-all-done.acts, bf16[192,1024]{1,0:T(8,128)(2,1)S(1)} %pad_maximum_fusion.3.rest_0_, bf16[192,1024]{1,0:T(8,128)(2,1)S(1)} %collective-permute-done.2.rest_1_, ...), custom_call_target="tpu_custom_call" | custom-call | flops 402653184 | bytes 3014656 | tf_op jit(solution)/shard_map/token_half_product/pallas_call | solution.py:36
  91.0 2.0 %token_half_product.6 = f32[256,1024]{1,0:T(8,128)S(1)} custom-call(s32[7]{0:T(128)S(1)} %stack.31.place, bf16[8,192,256]{2,1,0:T(8,128)(2,1)S(1)} %all-to-all-done.acts, bf16[192,1024]{1,0:T(8,128)(2,1)S(1)} %pad_maximum_fusion.4.rest_0_, bf16[192,1024]{1,0:T(8,128)(2,1)S(1)} %copy-done.1, bf16[192,1024]{1,0:T(8,128)(2,1)} %collective-permute-done.10.rest_2_, ...), custom_call_target="tpu_custom_call" | custom-call | flops 402653184 | bytes 3014656 | tf_op jit(solution)/shard_map/token_half_product/pallas_call | solution.py:36
  94.1 32.6 %all_to_all.15 = f16[16,16,2048]{2,1,0:T(8,128)(2,1)S(1)} all-to-all(f16[16,16,2048]{2,1,0:T(8,128)(2,1)S(1)} %bitcast.151), channel_id=1, replica_groups=mesh['yh'=2,'core'=2,'z'=8,'yl'=4,'x'=4] {'yl','x'}, dimensions={0} | all-to-all | bytes 2097152 | tf_op jit(solution)/shard_map/all_to_all | solution.py:110
  128.9 30.2 %all_to_all.16 = bf16[16,16,2,1024]{3,2,1,0:T(2,128)(2,1)S(1)} all-to-all(bf16[16,16,2,1024]{3,2,1,0:T(2,128)(2,1)S(1)} %broadcast_in_dim.10), channel_id=1, replica_groups=mesh['yh'=2,'core'=2,'z'=8,'yl'=4,'x'=4] {'yl','x'}, dimensions={0} | all-to-all | bytes 2097152 | tf_op jit(solution)/shard_map/all_to_all | solution.py:124
  (57 shorter events, 19.1 us)
Async XLA Ops:
  1.6 21.5 %collective-permute-start.1 = (bf16[2,192,256]{2,1,0:T(8,128)(2,1)S(1)}, bf16[2,192,256]{2,1,0:T(8,128)(2,1)S(1)}, u32[]{:S(2)}, u32[]{:S(2)}) collective-permute-start(bf16[2,192,256]{2,1,0:T(8,128)(2,1)S(1)} %bitcast.154), channel_id=1, source_target_pairs={{0,128},{128,0},{1,129},{129,1},{2,130},{130,2},{3,131},{131,3},{4... | collective-permute-start | bytes 589832 | tf_op jit(solution)/shard_map/ppermute | solution.py:61
  3.5 23.7 %collective-permute-start.7 = (bf16[2,192,256]{2,1,0:T(8,128)(2,1)S(1)}, bf16[2,192,256]{2,1,0:T(8,128)(2,1)S(1)}, u32[]{:S(2)}, u32[]{:S(2)}) collective-permute-start(bf16[2,192,256]{2,1,0:T(8,128)(2,1)S(1)} %bitcast.155), channel_id=1, source_target_pairs={{0,256},{256,0},{1,257},{257,1},{2,258},{258,2},{3,259},{259,3},{4... | collective-permute-start | bytes 589832 | tf_op jit(solution)/shard_map/ppermute | solution.py:61
  12.7 52.4 %all-to-all-start = ((bf16[8,192,256]{2,1,0:T(8,128)(2,1)}), bf16[8,192,256]{2,1,0:T(8,128)(2,1)S(1)}, u32[]{:S(2)}, u32[]{:S(2)}) async-start(bf16[8,192,256]{2,1,0:T(8,128)(2,1)} %bitcast.148), calls=%async_computation | async-start | bytes 1572864 | tf_op jit(solution)/shard_map/all_to_all | solution.py:85
  23.3 24.8 %collective-permute-start.2 = (bf16[192,1024]{1,0:T(8,128)(2,1)S(1)}, bf16[192,1024]{1,0:T(8,128)(2,1)S(1)}, u32[]{:S(2)}, u32[]{:S(2)}) collective-permute-start(bf16[192,1024]{1,0:T(8,128)(2,1)S(1)} %pad_maximum_fusion.3.rest_0_), channel_id=1, source_target_pairs={{0,16},{16,32},{32,48},{48,64},{64,80},{80,96},{96,112},{112,0},{1... | collective-permute-start | bytes 1179656 | tf_op jit(solution)/shard_map/ppermute | solution.py:66
  27.2 3.6 %collective-permute-start.8 = (bf16[2,192,256]{2,1,0:T(8,128)(2,1)S(1)}, bf16[2,192,256]{2,1,0:T(8,128)(2,1)S(1)}, u32[]{:S(2)}, u32[]{:S(2)}) collective-permute-start(bf16[2,192,256]{2,1,0:T(8,128)(2,1)S(1)} %collective-permute-done.7), channel_id=1, source_target_pairs={{0,128},{128,0},{1,129},{129,1},{2,130},{130,2},{3,131},{131,3},{4... | collective-permute-start | bytes 589832 | tf_op jit(solution)/shard_map/ppermute | solution.py:61
  31.0 21.3 %collective-permute-start.9 = (bf16[192,1024]{1,0:T(8,128)(2,1)S(1)}, bf16[192,1024]{1,0:T(8,128)(2,1)S(1)}, u32[]{:S(2)}, u32[]{:S(2)}) collective-permute-start(bf16[192,1024]{1,0:T(8,128)(2,1)S(1)} %pad_maximum_fusion.4.rest_0_), channel_id=1, source_target_pairs={{0,16},{16,32},{32,48},{48,64},{64,80},{80,96},{96,112},{112,0},{1... | collective-permute-start | bytes 1179656 | tf_op jit(solution)/shard_map/ppermute | solution.py:66
  48.1 11.0 %collective-permute-start.3 = (bf16[192,1024]{1,0:T(8,128)(2,1)S(1)}, bf16[192,1024]{1,0:T(8,128)(2,1)}, u32[]{:S(2)}, u32[]{:S(2)}) collective-permute-start(bf16[192,1024]{1,0:T(8,128)(2,1)S(1)} %collective-permute-done.2.rest_1_), channel_id=1, source_target_pairs={{0,16},{16,32},{32,48},{48,64},{64,80},{80,96},{96,112},{112,0},{1... | collective-permute-start | bytes 1179656 | tf_op jit(solution)/shard_map/ppermute | solution.py:66
  52.3 5.5 %copy-start = (bf16[192,1024]{1,0:T(8,128)(2,1)}, bf16[192,1024]{1,0:T(8,128)(2,1)S(1)}, u32[]{:S(2)}) copy-start(bf16[192,1024]{1,0:T(8,128)(2,1)S(1)} %collective-permute-done.9.rest_1_) | copy-start | bytes 1179652
  52.3 11.0 %collective-permute-start.10 = (bf16[192,1024]{1,0:T(8,128)(2,1)S(1)}, bf16[192,1024]{1,0:T(8,128)(2,1)}, u32[]{:S(2)}, u32[]{:S(2)}) collective-permute-start(bf16[192,1024]{1,0:T(8,128)(2,1)S(1)} %collective-permute-done.9.rest_1_), channel_id=1, source_target_pairs={{0,16},{16,32},{32,48},{48,64},{64,80},{80,96},{96,112},{112,0},{1... | collective-permute-start | bytes 1179656 | tf_op jit(solution)/shard_map/ppermute | solution.py:66
  59.0 11.1 %collective-permute-start.4 = (bf16[192,1024]{1,0:T(8,128)(2,1)}, bf16[192,1024]{1,0:T(8,128)(2,1)S(1)}, u32[]{:S(2)}, u32[]{:S(2)}) collective-permute-start(bf16[192,1024]{1,0:T(8,128)(2,1)} %collective-permute-done.3.rest_2_), channel_id=1, source_target_pairs={{0,16},{16,32},{32,48},{48,64},{64,80},{80,96},{96,112},{112,0},{1... | collective-permute-start | bytes 1179656 | tf_op jit(solution)/shard_map/ppermute | solution.py:66
  63.2 11.1 %collective-permute-start.11 = (bf16[192,1024]{1,0:T(8,128)(2,1)}, bf16[192,1024]{1,0:T(8,128)(2,1)S(1)}, u32[]{:S(2)}, u32[]{:S(2)}) collective-permute-start(bf16[192,1024]{1,0:T(8,128)(2,1)} %collective-permute-done.10.rest_2_), channel_id=1, source_target_pairs={{0,16},{16,32},{32,48},{48,64},{64,80},{80,96},{96,112},{112,0},{1... | collective-permute-start | bytes 1179656 | tf_op jit(solution)/shard_map/ppermute | solution.py:66
  65.2 15.5 %collective-permute-start = (bf16[8,192,256]{2,1,0:T(8,128)(2,1)S(1)}, bf16[8,192,256]{2,1,0:T(8,128)(2,1)S(1)}, u32[]{:S(2)}, u32[]{:S(2)}) collective-permute-start(bf16[8,192,256]{2,1,0:T(8,128)(2,1)S(1)} %all-to-all-done.acts), channel_id=1, source_target_pairs={{0,128},{128,0},{1,129},{129,1},{2,130},{130,2},{3,131},{131,3},{4... | collective-permute-start | bytes 2359304 | tf_op jit(solution)/shard_map/ppermute | solution.py:61
  70.8 9.8 %collective-permute-start.5 = (bf16[96,1024]{1,0:T(8,128)(2,1)}, bf16[96,1024]{1,0:T(8,128)(2,1)}, u32[]{:S(2)}, u32[]{:S(2)}) collective-permute-start(bf16[96,1024]{1,0:T(8,128)(2,1)} %slice.220), channel_id=1, source_target_pairs={{0,16},{16,32},{32,48},{48,64},{64,80},{80,96},{96,112},{112,0},{1... | collective-permute-start | bytes 589832 | tf_op jit(solution)/shard_map/ppermute | solution.py:66
  75.0 10.1 %collective-permute-start.12 = (bf16[96,1024]{1,0:T(8,128)(2,1)}, bf16[96,1024]{1,0:T(8,128)(2,1)}, u32[]{:S(2)}, u32[]{:S(2)}) collective-permute-start(bf16[96,1024]{1,0:T(8,128)(2,1)} %slice.233), channel_id=1, source_target_pairs={{0,16},{16,32},{32,48},{48,64},{64,80},{80,96},{96,112},{112,0},{1... | collective-permute-start | bytes 589832 | tf_op jit(solution)/shard_map/ppermute | solution.py:66
  80.6 4.5 %copy-start.1 = (bf16[192,1024]{1,0:T(8,128)(2,1)S(1)}, bf16[192,1024]{1,0:T(8,128)(2,1)}, u32[]{:S(2)}) copy-start(bf16[192,1024]{1,0:T(8,128)(2,1)} %copy-done) | copy-start | bytes 1179652
  82.6 6.4 %copy-start.5 = (s32[1,2]{1,0:T(1,128)S(1)}, s32[1,2]{1,0:T(1,128)}, u32[]{:S(2)}) copy-start(s32[1,2]{1,0:T(1,128)} %param.9) | copy-start | bytes 28
  82.6 10.4 %collective-permute-start.6 = (f32[256,1024]{1,0:T(8,128)S(1)}, f32[256,1024]{1,0:T(8,128)S(1)}, u32[]{:S(2)}, u32[]{:S(2)}) collective-permute-start(f32[256,1024]{1,0:T(8,128)S(1)} %token_half_product.5), channel_id=1, source_target_pairs={{0,128},{128,0},{1,129},{129,1},{2,130},{130,2},{3,131},{131,3},{4... | collective-permute-start | bytes 3145736 | tf_op jit(solution)/shard_map/ppermute | solution.py:61
  87.0 6.0 %collective-permute-start.13 = (f32[256,1024]{1,0:T(8,128)S(1)}, f32[256,1024]{1,0:T(8,128)S(1)}, u32[]{:S(2)}, u32[]{:S(2)}) collective-permute-start(f32[256,1024]{1,0:T(8,128)S(1)} %token_half_product.7), channel_id=1, source_target_pairs={{0,128},{128,0},{1,129},{129,1},{2,130},{130,2},{3,131},{131,3},{4... | collective-permute-start | bytes 3145736 | tf_op jit(solution)/shard_map/ppermute | solution.py:61
  91.0 2.0 %copy-start.2 = (f32[256,1024]{1,0:T(8,128)S(1)}, f32[256,1024]{1,0:T(8,128)}, u32[]{:S(2)}) copy-start(f32[256,1024]{1,0:T(8,128)} %pad_maximum_fusion) | copy-start | bytes 3145732
  94.1 33.0 %copy-start.3 = (f32[16,2,1024]{2,1,0:T(2,128)S(1)}, f32[16,2,1024]{2,1,0:T(2,128)}, u32[]{:S(2)}) copy-start(f32[16,2,1024]{2,1,0:T(2,128)} %param.10) | copy-start | bytes 393220
  94.1 33.0 %copy-start.4 = (f32[16,2,1024]{2,1,0:T(2,128)S(1)}, f32[16,2,1024]{2,1,0:T(2,128)}, u32[]{:S(2)}) copy-start(f32[16,2,1024]{2,1,0:T(2,128)} %param.11) | copy-start | bytes 393220

commit v6 on v5

--- a/solution.py
+++ b/solution.py
@@ -73,9 +73,9 @@
         pairs = [jnp.where(first_core, a, b) for k in range(2) for a, b in ((mine[k], other[k]), (other[k], mine[k]))]
         return jnp.concatenate(pairs, axis=1)
 
-    def ring(block):
-        held = [block]
-        for _ in range(n_z // 2 - 1):
+    def ring(first, block):
+        held = [first, block]
+        for _ in range(n_z // 2 - 2):
             block = step(block)
             held.append(block)
         held.append(step(block[:part]))
@@ -88,18 +88,20 @@
     places = [(z + n_z + sign * s) % n_z for s in range(n_z // 2 + 1)]
     place = jnp.stack(places + [jnp.where(first_core, 0, part), jnp.where(first_core, part, 0)]).astype(jnp.int32)
 
+    flags = jnp.repeat(drift_flags[0].astype(f32), half)[None]
     cots = cotangents[0].swapaxes(0, 1)
     far = swap(cots, "yh")
-    near_held = ring(chip(cots, swap(cots, "core")))
-    far_held = ring(chip(far, swap(far, "core")))
+    near = chip(cots, swap(cots, "core"))
+    far = chip(far, swap(far, "core"))
 
-    flags = jnp.repeat(drift_flags[0].astype(f32), half)[None]
-    drift = inner_drift[0].swapaxes(0, 1)
+    far, drift = tied(far, inner_drift[0])
+    drift = drift.swapaxes(0, 1)
 
     def half_of(low):
         return jnp.concatenate(list(jnp.where(low, drift[:, :, :half], drift[:, :, half:])), axis=1)
 
-    near_drift, far_drift, acts_other = tied(half_of(low_half), half_of(~low_half), acts_other)
+    near_next, far_next, near_drift, far_drift = tied(step(near), step(far), half_of(low_half), half_of(~low_half))
+    near_held, far_held = ring(near, near_next), ring(far, far_next)
 
     def term(held, drifts):
         came = swap(product(place, acts_other, held), "core")
@@ -120,8 +122,12 @@
     new_momentum = momentum_decay * outer_momentum + delta
     new_master = master_weights - outer_rate * (delta + momentum_decay * new_momentum)
 
-    fresh = jnp.broadcast_to(new_master.astype(bf16)[None], (replicas, own_rows, 2, kvw))
-    fresh_copy = lax.all_to_all(fresh, ("yl", "x"), 0, 0, tiled=True).reshape(rows, 2, kvw)
+    n_yl, n_x = lax.axis_size("yl"), lax.axis_size("x")
+    fresh = jnp.broadcast_to(new_master.astype(bf16)[None], (n_yl, own_rows, 2, kvw))
+    fresh = lax.all_to_all(fresh, "yl", 0, 0, tiled=True)
+    fresh = jnp.broadcast_to(fresh[None], (n_x, n_yl, own_rows, 2, kvw))
+    fresh = lax.all_to_all(fresh, "x", 0, 0, tiled=True)
+    fresh_copy = fresh.swapaxes(0, 1).reshape(rows, 2, kvw)
     return (new_master, new_momentum, fresh_copy)
 
 

time: 161 us -> 163 us (1.012)
  the two profiles are of different devices: /device:TPU:8 before, /device:TPU:24 now
where the time goes in v6:
time: 163 us; the launch traced here: 162 us
  blocking collectives  61.2 us (38%)
  starting transfers between devices  45.9 us (28%)
  waiting for transfers between devices  26.7 us (16%)
  local copies, waits for them, and re-layouts  12.3 us (8%)
  Pallas kernels  7.82 us (5%)
  other arithmetic  6.7 us (4%)
    all_to_all x1, blocking collectives, reduced(): lax.all_to_all(value.reshape(replicas, own_rows, -1), ('yl', 'x'), 0, 0,...  32.5 us
    ppermute x8, waiting for transfers between devices, step(): return lax.ppermute(value, ('core', 'z'), ways)  26.3 us
    ppermute x8, starting transfers between devices, step(): return lax.ppermute(value, ('core', 'z'), ways)  19.2 us
    all_to_all x1, blocking collectives, body(): fresh = lax.all_to_all(fresh, 'x', 0, 0, tiled=True)  17.3 us
    ppermute x6, starting transfers between devices, swap(): return lax.ppermute(value, axis, [(0, 1), (1, 0)])  16.3 us
    all_to_all x1, blocking collectives, body(): fresh = lax.all_to_all(fresh, 'yl', 0, 0, tiled=True)  11.3 us
    all_to_all x1, starting transfers between devices, body(): acts = lax.all_to_all(acts, 'z', 0, 0, tiled=True)  10.3 us
    pallas_call x4, Pallas kernels, product(): pl.pallas_call(functools.partial(product_kernel, len(blocks)), out_shape=...  7.82 us
  transfers between devices with their start and end apart: 15, of which 9 were waited for; matrix products, arithmetic and copies ran while one was open for 7% of the time, Pallas kernels for 5%

profile of v6, /device:TPU:24, one launch (start us, length us, event | category | flops | bytes accessed | tf_op | source)
XLA Modules:
  0.0 161.7 jit_solution(16630557355803163621)
XLA Ops:
  1.6 1.9 %collective-permute-start = (bf16[2,192,256]{2,1,0:T(8,128)(2,1)S(1)}, bf16[2,192,256]{2,1,0:T(8,128)(2,1)S(1)}, u32[]{:S(2)}, u32[]{:S(2)}) collective-permute-start(bf16[2,192,256]{2,1,0:T(8,128)(2,1)S(1)} %bitcast.155), channel_id=1, source_target_pairs={{0,128},{128,0},{1,129},{129,1},{2,130},{130,2},{3,131},{131,3},{4... | collective-permute-start | bytes 589832 | tf_op jit(solution)/shard_map/ppermute | solution.py:61
  3.5 5.0 %collective-permute-start.2 = (bf16[2,192,256]{2,1,0:T(8,128)(2,1)S(1)}, bf16[2,192,256]{2,1,0:T(8,128)(2,1)}, u32[]{:S(2)}, u32[]{:S(2)}) collective-permute-start(bf16[2,192,256]{2,1,0:T(8,128)(2,1)S(1)} %bitcast.156), channel_id=1, source_target_pairs={{0,256},{256,0},{1,257},{257,1},{2,258},{258,2},{3,259},{259,3},{4... | collective-permute-start | bytes 589832 | tf_op jit(solution)/shard_map/ppermute | solution.py:61
  11.1 10.3 %all-to-all-start = ((bf16[8,192,256]{2,1,0:T(8,128)(2,1)}), bf16[8,192,256]{2,1,0:T(8,128)(2,1)S(1)}, u32[]{:S(2)}, u32[]{:S(2)}) async-start(bf16[8,192,256]{2,1,0:T(8,128)(2,1)} %bitcast.149), calls=%async_computation | async-start | bytes 1572864 | tf_op jit(solution)/shard_map/all_to_all | solution.py:85
  21.4 2.0 %copy.40 = f32[1,256,2,1024]{3,1,2,0:T(8,128)} copy(f32[1,256,2,1024]{3,2,1,0:T(2,128)S(1)} %copy-done.5) | data formatting | bytes 4194304 | tf_op args[2]
  23.6 4.1 %collective-permute-start.1 = (bf16[192,1024]{1,0:T(8,128)(2,1)S(1)}, bf16[192,1024]{1,0:T(8,128)(2,1)S(1)}, u32[]{:S(2)}, u32[]{:S(2)}) collective-permute-start(bf16[192,1024]{1,0:T(8,128)(2,1)S(1)} %pad_maximum_fusion.3.rest_0_), channel_id=1, source_target_pairs={{0,16},{16,32},{32,48},{48,64},{64,80},{80,96},{96,112},{112,0},{1... | collective-permute-start | bytes 1179656 | tf_op jit(solution)/shard_map/ppermute | solution.py:66
  27.7 2.5 %collective-permute-start.3 = (bf16[2,192,256]{2,1,0:T(8,128)(2,1)}, bf16[2,192,256]{2,1,0:T(8,128)(2,1)S(1)}, u32[]{:S(2)}, u32[]{:S(2)}) collective-permute-start(bf16[2,192,256]{2,1,0:T(8,128)(2,1)} %collective-permute-done.2), channel_id=1, source_target_pairs={{0,128},{128,0},{1,129},{129,1},{2,130},{130,2},{3,131},{131,3},{4... | collective-permute-start | bytes 589832 | tf_op jit(solution)/shard_map/ppermute | solution.py:61
  33.5 3.2 %collective-permute-start.4 = (bf16[192,1024]{1,0:T(8,128)(2,1)S(1)}, bf16[192,1024]{1,0:T(8,128)(2,1)S(1)}, u32[]{:S(2)}, u32[]{:S(2)}) collective-permute-start(bf16[192,1024]{1,0:T(8,128)(2,1)S(1)} %pad_maximum_fusion.4.rest_0_), channel_id=1, source_target_pairs={{0,16},{16,32},{32,48},{48,64},{64,80},{80,96},{96,112},{112,0},{1... | collective-permute-start | bytes 1179656 | tf_op jit(solution)/shard_map/ppermute | solution.py:66
  39.2 7.2 %collective-permute-done.1.rest_1_ = bf16[192,1024]{1,0:T(8,128)(2,1)S(1)} collective-permute-done((bf16[192,1024]{1,0:T(8,128)(2,1)S(1)}, bf16[192,1024]{1,0:T(8,128)(2,1)S(1)}, u32[]{:S(2)}, u32[]{:S(2)}) %collective-permute-start.1) | collective-permute-done | bytes 393248 | tf_op jit(solution)/shard_map/ppermute | solution.py:66
  46.4 4.2 %collective-permute-done.4.rest_1_ = bf16[192,1024]{1,0:T(8,128)(2,1)S(1)} collective-permute-done((bf16[192,1024]{1,0:T(8,128)(2,1)S(1)}, bf16[192,1024]{1,0:T(8,128)(2,1)S(1)}, u32[]{:S(2)}, u32[]{:S(2)}) %collective-permute-start.4) | collective-permute-done | bytes 393248 | tf_op jit(solution)/shard_map/ppermute | solution.py:66
  52.5 2.5 %collective-permute-start.10 = (bf16[192,1024]{1,0:T(8,128)(2,1)S(1)}, bf16[192,1024]{1,0:T(8,128)(2,1)}, u32[]{:S(2)}, u32[]{:S(2)}) collective-permute-start(bf16[192,1024]{1,0:T(8,128)(2,1)S(1)} %collective-permute-done.4.rest_1_), channel_id=1, source_target_pairs={{0,16},{16,32},{32,48},{48,64},{64,80},{80,96},{96,112},{112,0},{1... | collective-permute-start | bytes 1179656 | tf_op jit(solution)/shard_map/ppermute | solution.py:66
  55.8 2.9 %collective-permute-start.8 = (bf16[8,192,256]{2,1,0:T(8,128)(2,1)S(1)}, bf16[8,192,256]{2,1,0:T(8,128)(2,1)S(1)}, u32[]{:S(2)}, u32[]{:S(2)}) collective-permute-start(bf16[8,192,256]{2,1,0:T(8,128)(2,1)S(1)} %all-to-all-done.acts), channel_id=1, source_target_pairs={{0,128},{128,0},{1,129},{129,1},{2,130},{130,2},{3,131},{131,3},{4... | collective-permute-start | bytes 2359304 | tf_op jit(solution)/shard_map/ppermute | solution.py:61
  58.7 2.9 %collective-permute-done.5.rest_2_ = bf16[192,1024]{1,0:T(8,128)(2,1)} collective-permute-done((bf16[192,1024]{1,0:T(8,128)(2,1)S(1)}, bf16[192,1024]{1,0:T(8,128)(2,1)}, u32[]{:S(2)}, u32[]{:S(2)}) %collective-permute-start.5) | collective-permute-done | bytes 393248 | tf_op jit(solution)/shard_map/ppermute | solution.py:66
  63.5 2.3 %collective-permute-done.10.rest_2_ = bf16[192,1024]{1,0:T(8,128)(2,1)} collective-permute-done((bf16[192,1024]{1,0:T(8,128)(2,1)S(1)}, bf16[192,1024]{1,0:T(8,128)(2,1)}, u32[]{:S(2)}, u32[]{:S(2)}) %collective-permute-start.10) | collective-permute-done | bytes 393248 | tf_op jit(solution)/shard_map/ppermute | solution.py:66
  67.7 5.0 %collective-permute-done.6.rest_3_ = bf16[192,1024]{1,0:T(8,128)(2,1)S(1)} collective-permute-done((bf16[192,1024]{1,0:T(8,128)(2,1)}, bf16[192,1024]{1,0:T(8,128)(2,1)S(1)}, u32[]{:S(2)}, u32[]{:S(2)}) %collective-permute-start.6) | collective-permute-done | bytes 393248 | tf_op jit(solution)/shard_map/ppermute | solution.py:66
  79.7 2.8 %collective-permute-done.7.rest_4_ = bf16[96,1024]{1,0:T(8,128)(2,1)} collective-permute-done((bf16[96,1024]{1,0:T(8,128)(2,1)}, bf16[96,1024]{1,0:T(8,128)(2,1)}, u32[]{:S(2)}, u32[]{:S(2)}) %collective-permute-start.7) | collective-permute-done | bytes 196640 | tf_op jit(solution)/shard_map/ppermute | solution.py:66
  84.4 1.9 %collective-permute-start.9 = (f32[256,1024]{1,0:T(8,128)S(1)}, f32[256,1024]{1,0:T(8,128)S(1)}, u32[]{:S(2)}, u32[]{:S(2)}) collective-permute-start(f32[256,1024]{1,0:T(8,128)S(1)} %token_half_product.5), channel_id=1, source_target_pairs={{0,128},{128,0},{1,129},{129,1},{2,130},{130,2},{3,131},{131,3},{4... | collective-permute-start | bytes 3145736 | tf_op jit(solution)/shard_map/ppermute | solution.py:61
  86.7 1.9 %token_half_product.7 = f32[256,1024]{1,0:T(8,128)S(1)} custom-call(s32[7]{0:T(128)S(1)} %stack.31.place, bf16[8,192,256]{2,1,0:T(8,128)(2,1)S(1)} %collective-permute-done.8.acts, bf16[192,1024]{1,0:T(8,128)(2,1)S(1)} %pad_maximum_fusion.4.rest_0_, bf16[192,1024]{1,0:T(8,128)(2,1)S(1)} %copy-done.1, bf16[192,1024]{1,0:T(8,128)(2,1)} %collective-permute-done.10.rest_2_, ...), custom_call_target="tpu_custom_call" | custom-call | flops 402653184 | bytes 3014656 | tf_op jit(solution)/shard_map/token_half_product/pallas_call | solution.py:36
  88.6 2.1 %collective-permute-start.13 = (f32[256,1024]{1,0:T(8,128)S(1)}, f32[256,1024]{1,0:T(8,128)S(1)}, u32[]{:S(2)}, u32[]{:S(2)}) collective-permute-start(f32[256,1024]{1,0:T(8,128)S(1)} %token_half_product.7), channel_id=1, source_target_pairs={{0,128},{128,0},{1,129},{129,1},{2,130},{130,2},{3,131},{131,3},{4... | collective-permute-start | bytes 3145736 | tf_op jit(solution)/shard_map/ppermute | solution.py:61
  90.8 1.9 %token_half_product.4 = f32[256,1024]{1,0:T(8,128)S(1)} custom-call(s32[7]{0:T(128)S(1)} %stack.31.place, bf16[8,192,256]{2,1,0:T(8,128)(2,1)S(1)} %all-to-all-done.acts, bf16[192,1024]{1,0:T(8,128)(2,1)S(1)} %pad_maximum_fusion.3.rest_0_, bf16[192,1024]{1,0:T(8,128)(2,1)S(1)} %collective-permute-done.1.rest_1_, ...), custom_call_target="tpu_custom_call" | custom-call | flops 402653184 | bytes 3014656 | tf_op jit(solution)/shard_map/token_half_product/pallas_call | solution.py:36
  92.7 2.1 %token_half_product.6 = f32[256,1024]{1,0:T(8,128)S(1)} custom-call(s32[7]{0:T(128)S(1)} %stack.31.place, bf16[8,192,256]{2,1,0:T(8,128)(2,1)S(1)} %all-to-all-done.acts, bf16[192,1024]{1,0:T(8,128)(2,1)S(1)} %pad_maximum_fusion.4.rest_0_, bf16[192,1024]{1,0:T(8,128)(2,1)S(1)} %copy-done.1, bf16[192,1024]{1,0:T(8,128)(2,1)} %collective-permute-done.10.rest_2_, ...), custom_call_target="tpu_custom_call" | custom-call | flops 402653184 | bytes 3014656 | tf_op jit(solution)/shard_map/token_half_product/pallas_call | solution.py:36
  95.9 32.5 %all_to_all.20 = f16[16,16,2048]{2,1,0:T(8,128)(2,1)S(1)} all-to-all(f16[16,16,2048]{2,1,0:T(8,128)(2,1)S(1)} %bitcast.152), channel_id=1, replica_groups=mesh['yh'=2,'core'=2,'z'=8,'yl'=4,'x'=4] {'yl','x'}, dimensions={0} | all-to-all | bytes 2097152 | tf_op jit(solution)/shard_map/all_to_all | solution.py:112
  129.9 11.3 %all_to_all.21 = bf16[4,16,2,1024]{3,2,1,0:T(2,128)(2,1)S(1)} all-to-all(bf16[4,16,2,1024]{3,2,1,0:T(2,128)(2,1)S(1)} %broadcast_in_dim.7), channel_id=1, replica_groups=mesh['yh'=2,'core'=2,'z'=8,'yl'=4,'x'=4] {'yl'}, dimensions={0} | all-to-all | bytes 524288 | tf_op jit(solution)/shard_map/all_to_all | solution.py:127
  142.0 17.3 %all_to_all.22 = bf16[4,4,16,2,1024]{4,3,2,1,0:T(2,128)(2,1)S(1)} all-to-all(bf16[4,4,16,2,1024]{4,3,2,1,0:T(2,128)(2,1)S(1)} %broadcast_in_dim.8), channel_id=1, replica_groups=mesh['yh'=2,'core'=2,'z'=8,'yl'=4,'x'=4] {'x'}, dimensions={0} | all-to-all | bytes 2097152 | tf_op jit(solution)/shard_map/all_to_all | solution.py:129
  159.6 2.1 %copy.33 = bf16[256,2,1024]{2,1,0:T(2,128)(2,1)} copy(bf16[256,2,1024]{2,0,1:T(8,128)(2,1)S(1)} %bitcast.153) | data formatting | bytes 2097152
  (66 shorter events, 28.8 us)
Async XLA Ops:
  1.6 21.8 %collective-permute-start = (bf16[2,192,256]{2,1,0:T(8,128)(2,1)S(1)}, bf16[2,192,256]{2,1,0:T(8,128)(2,1)S(1)}, u32[]{:S(2)}, u32[]{:S(2)}) collective-permute-start(bf16[2,192,256]{2,1,0:T(8,128)(2,1)S(1)} %bitcast.155), channel_id=1, source_target_pairs={{0,128},{128,0},{1,129},{129,1},{2,130},{130,2},{3,131},{131,3},{4... | collective-permute-start | bytes 589832 | tf_op jit(solution)/shard_map/ppermute | solution.py:61
  3.5 24.2 %collective-permute-start.2 = (bf16[2,192,256]{2,1,0:T(8,128)(2,1)S(1)}, bf16[2,192,256]{2,1,0:T(8,128)(2,1)}, u32[]{:S(2)}, u32[]{:S(2)}) collective-permute-start(bf16[2,192,256]{2,1,0:T(8,128)(2,1)S(1)} %bitcast.156), channel_id=1, source_target_pairs={{0,256},{256,0},{1,257},{257,1},{2,258},{258,2},{3,259},{259,3},{4... | collective-permute-start | bytes 589832 | tf_op jit(solution)/shard_map/ppermute | solution.py:61
  8.6 12.8 %copy-start.5 = (f32[1,256,2,1024]{3,2,1,0:T(2,128)S(1)}, f32[1,256,2,1024]{3,2,1,0:T(2,128)}, u32[]{:S(2)}) copy-start(f32[1,256,2,1024]{3,2,1,0:T(2,128)} %param.8) | copy-start | bytes 6291460
  11.1 44.7 %all-to-all-start = ((bf16[8,192,256]{2,1,0:T(8,128)(2,1)}), bf16[8,192,256]{2,1,0:T(8,128)(2,1)S(1)}, u32[]{:S(2)}, u32[]{:S(2)}) async-start(bf16[8,192,256]{2,1,0:T(8,128)(2,1)} %bitcast.149), calls=%async_computation | async-start | bytes 1572864 | tf_op jit(solution)/shard_map/all_to_all | solution.py:85
  23.5 13.1 %copy-start.2 = (f32[1,256,2,1024]{3,1,2,0:T(8,128)S(1)}, f32[1,256,2,1024]{3,1,2,0:T(8,128)}, u32[]{:S(2)}) copy-start(f32[1,256,2,1024]{3,1,2,0:T(8,128)} %copy.40) | copy-start | bytes 6291460
  23.6 22.8 %collective-permute-start.1 = (bf16[192,1024]{1,0:T(8,128)(2,1)S(1)}, bf16[192,1024]{1,0:T(8,128)(2,1)S(1)}, u32[]{:S(2)}, u32[]{:S(2)}) collective-permute-start(bf16[192,1024]{1,0:T(8,128)(2,1)S(1)} %pad_maximum_fusion.3.rest_0_), channel_id=1, source_target_pairs={{0,16},{16,32},{32,48},{48,64},{64,80},{80,96},{96,112},{112,0},{1... | collective-permute-start | bytes 1179656 | tf_op jit(solution)/shard_map/ppermute | solution.py:66
  27.7 3.8 %collective-permute-start.3 = (bf16[2,192,256]{2,1,0:T(8,128)(2,1)}, bf16[2,192,256]{2,1,0:T(8,128)(2,1)S(1)}, u32[]{:S(2)}, u32[]{:S(2)}) collective-permute-start(bf16[2,192,256]{2,1,0:T(8,128)(2,1)} %collective-permute-done.2), channel_id=1, source_target_pairs={{0,128},{128,0},{1,129},{129,1},{2,130},{130,2},{3,131},{131,3},{4... | collective-permute-start | bytes 589832 | tf_op jit(solution)/shard_map/ppermute | solution.py:61
  33.5 17.2 %collective-permute-start.4 = (bf16[192,1024]{1,0:T(8,128)(2,1)S(1)}, bf16[192,1024]{1,0:T(8,128)(2,1)S(1)}, u32[]{:S(2)}, u32[]{:S(2)}) collective-permute-start(bf16[192,1024]{1,0:T(8,128)(2,1)S(1)} %pad_maximum_fusion.4.rest_0_), channel_id=1, source_target_pairs={{0,16},{16,32},{32,48},{48,64},{64,80},{80,96},{96,112},{112,0},{1... | collective-permute-start | bytes 1179656 | tf_op jit(solution)/shard_map/ppermute | solution.py:66
  50.6 11.0 %collective-permute-start.5 = (bf16[192,1024]{1,0:T(8,128)(2,1)S(1)}, bf16[192,1024]{1,0:T(8,128)(2,1)}, u32[]{:S(2)}, u32[]{:S(2)}) collective-permute-start(bf16[192,1024]{1,0:T(8,128)(2,1)S(1)} %collective-permute-done.1.rest_1_), channel_id=1, source_target_pairs={{0,16},{16,32},{32,48},{48,64},{64,80},{80,96},{96,112},{112,0},{1... | collective-permute-start | bytes 1179656 | tf_op jit(solution)/shard_map/ppermute | solution.py:66
  52.5 13.3 %collective-permute-start.10 = (bf16[192,1024]{1,0:T(8,128)(2,1)S(1)}, bf16[192,1024]{1,0:T(8,128)(2,1)}, u32[]{:S(2)}, u32[]{:S(2)}) collective-permute-start(bf16[192,1024]{1,0:T(8,128)(2,1)S(1)} %collective-permute-done.4.rest_1_), channel_id=1, source_target_pairs={{0,16},{16,32},{32,48},{48,64},{64,80},{80,96},{96,112},{112,0},{1... | collective-permute-start | bytes 1179656 | tf_op jit(solution)/shard_map/ppermute | solution.py:66
  55.0 0.8 copy-start
  55.8 26.7 %collective-permute-start.8 = (bf16[8,192,256]{2,1,0:T(8,128)(2,1)S(1)}, bf16[8,192,256]{2,1,0:T(8,128)(2,1)S(1)}, u32[]{:S(2)}, u32[]{:S(2)}) collective-permute-start(bf16[8,192,256]{2,1,0:T(8,128)(2,1)S(1)} %all-to-all-done.acts), channel_id=1, source_target_pairs={{0,128},{128,0},{1,129},{129,1},{2,130},{130,2},{3,131},{131,3},{4... | collective-permute-start | bytes 2359304 | tf_op jit(solution)/shard_map/ppermute | solution.py:61
  61.6 11.1 %collective-permute-start.6 = (bf16[192,1024]{1,0:T(8,128)(2,1)}, bf16[192,1024]{1,0:T(8,128)(2,1)S(1)}, u32[]{:S(2)}, u32[]{:S(2)}) collective-permute-start(bf16[192,1024]{1,0:T(8,128)(2,1)} %collective-permute-done.5.rest_2_), channel_id=1, source_target_pairs={{0,16},{16,32},{32,48},{48,64},{64,80},{80,96},{96,112},{112,0},{1... | collective-permute-start | bytes 1179656 | tf_op jit(solution)/shard_map/ppermute | solution.py:66
  65.8 11.1 %collective-permute-start.11 = (bf16[192,1024]{1,0:T(8,128)(2,1)}, bf16[192,1024]{1,0:T(8,128)(2,1)S(1)}, u32[]{:S(2)}, u32[]{:S(2)}) collective-permute-start(bf16[192,1024]{1,0:T(8,128)(2,1)} %collective-permute-done.10.rest_2_), channel_id=1, source_target_pairs={{0,16},{16,32},{32,48},{48,64},{64,80},{80,96},{96,112},{112,0},{1... | collective-permute-start | bytes 1179656 | tf_op jit(solution)/shard_map/ppermute | solution.py:66
  73.4 9.1 %collective-permute-start.7 = (bf16[96,1024]{1,0:T(8,128)(2,1)}, bf16[96,1024]{1,0:T(8,128)(2,1)}, u32[]{:S(2)}, u32[]{:S(2)}) collective-permute-start(bf16[96,1024]{1,0:T(8,128)(2,1)} %slice.232), channel_id=1, source_target_pairs={{0,16},{16,32},{32,48},{48,64},{64,80},{80,96},{96,112},{112,0},{1... | collective-permute-start | bytes 589832 | tf_op jit(solution)/shard_map/ppermute | solution.py:66
  77.6 9.1 %collective-permute-start.12 = (bf16[96,1024]{1,0:T(8,128)(2,1)}, bf16[96,1024]{1,0:T(8,128)(2,1)}, u32[]{:S(2)}, u32[]{:S(2)}) collective-permute-start(bf16[96,1024]{1,0:T(8,128)(2,1)} %slice.233), channel_id=1, source_target_pairs={{0,16},{16,32},{32,48},{48,64},{64,80},{80,96},{96,112},{112,0},{1... | collective-permute-start | bytes 589832 | tf_op jit(solution)/shard_map/ppermute | solution.py:66
  79.7 7.0 %copy-start.1 = (bf16[192,1024]{1,0:T(8,128)(2,1)S(1)}, bf16[192,1024]{1,0:T(8,128)(2,1)}, u32[]{:S(2)}) copy-start(bf16[192,1024]{1,0:T(8,128)(2,1)} %copy-done) | copy-start | bytes 1179652
  84.4 6.3 %copy-start.8 = (s32[1,2]{1,0:T(1,128)S(1)}, s32[1,2]{1,0:T(1,128)}, u32[]{:S(2)}) copy-start(s32[1,2]{1,0:T(1,128)} %param.9) | copy-start | bytes 28
  84.4 10.4 %collective-permute-start.9 = (f32[256,1024]{1,0:T(8,128)S(1)}, f32[256,1024]{1,0:T(8,128)S(1)}, u32[]{:S(2)}, u32[]{:S(2)}) collective-permute-start(f32[256,1024]{1,0:T(8,128)S(1)} %token_half_product.5), channel_id=1, source_target_pairs={{0,128},{128,0},{1,129},{129,1},{2,130},{130,2},{3,131},{131,3},{4... | collective-permute-start | bytes 3145736 | tf_op jit(solution)/shard_map/ppermute | solution.py:61
  88.6 6.2 %collective-permute-start.13 = (f32[256,1024]{1,0:T(8,128)S(1)}, f32[256,1024]{1,0:T(8,128)S(1)}, u32[]{:S(2)}, u32[]{:S(2)}) collective-permute-start(f32[256,1024]{1,0:T(8,128)S(1)} %token_half_product.7), channel_id=1, source_target_pairs={{0,128},{128,0},{1,129},{129,1},{2,130},{130,2},{3,131},{131,3},{4... | collective-permute-start | bytes 3145736 | tf_op jit(solution)/shard_map/ppermute | solution.py:61
  92.7 2.1 %copy-start.3 = (f32[256,1024]{1,0:T(8,128)S(1)}, f32[256,1024]{1,0:T(8,128)}, u32[]{:S(2)}) copy-start(f32[256,1024]{1,0:T(8,128)} %pad_maximum_fusion) | copy-start | bytes 3145732
  92.7 2.1 %copy-start.4 = (f32[256,1024]{1,0:T(8,128)S(1)}, f32[256,1024]{1,0:T(8,128)}, u32[]{:S(2)}) copy-start(f32[256,1024]{1,0:T(8,128)} %pad_maximum_fusion.1) | copy-start | bytes 3145732
  95.9 32.9 %copy-start.6 = (f32[16,2,1024]{2,1,0:T(2,128)S(1)}, f32[16,2,1024]{2,1,0:T(2,128)}, u32[]{:S(2)}) copy-start(f32[16,2,1024]{2,1,0:T(2,128)} %param.10) | copy-start | bytes 393220
  95.9 32.9 %copy-start.7 = (f32[16,2,1024]{2,1,0:T(2,128)S(1)}, f32[16,2,1024]{2,1,0:T(2,128)}, u32[]{:S(2)}) copy-start(f32[16,2,1024]{2,1,0:T(2,128)} %param.11) | copy-start | bytes 393220

commit v7 on v5

--- a/solution.py
+++ b/solution.py
@@ -18,16 +18,15 @@
     blocks, out = rest[:n], rest[n]
     part = blocks[0].shape[0] // 2
     first, second = (pl.ds(pl.multiple_of(place[n + i], 32), part) for i in range(2))
+    tokens, values = [], []
     for i, block in enumerate(blocks):
-        tokens = acts[place[i], first, :]
+        tokens.append(acts[place[i], first, :])
+        values.append(block[...] if i > 0 else block[:part])
         if 0 < i < n - 1:
-            tokens = jnp.concatenate([tokens, acts[place[i], second, :]], axis=0)
-        value = block[...] if i > 0 else block[:part]
-        product = lax.dot_general(tokens, value, (((0,), (0,)), ((), ())), preferred_element_type=f32)
-        if i == 0:
-            out[...] = product
-        else:
-            out[...] += product
+            tokens.append(acts[place[i], second, :])
+    out[...] = lax.dot_general(
+        jnp.concatenate(tokens, axis=0), jnp.concatenate(values, axis=0), (((0,), (0,)), ((), ())), preferred_element_type=f32
+    )
 
 
 def product(place, acts, blocks):
@@ -120,8 +119,12 @@
     new_momentum = momentum_decay * outer_momentum + delta
     new_master = master_weights - outer_rate * (delta + momentum_decay * new_momentum)
 
-    fresh = jnp.broadcast_to(new_master.astype(bf16)[None], (replicas, own_rows, 2, kvw))
-    fresh_copy = lax.all_to_all(fresh, ("yl", "x"), 0, 0, tiled=True).reshape(rows, 2, kvw)
+    n_yl, n_x = lax.axis_size("yl"), lax.axis_size("x")
+    fresh = jnp.broadcast_to(new_master.astype(bf16)[None], (n_yl, own_rows, 2, kvw))
+    fresh = lax.all_to_all(fresh, "yl", 0, 0, tiled=True)
+    fresh = jnp.broadcast_to(fresh[None], (n_x, n_yl, own_rows, 2, kvw))
+    fresh = lax.all_to_all(fresh, "x", 0, 0, tiled=True)
+    fresh_copy = fresh.swapaxes(0, 1).reshape(rows, 2, kvw)
     return (new_master, new_momentum, fresh_copy)
 
 

time: 161 us -> 158 us (0.981)
  the two profiles are of different devices: /device:TPU:8 before, /device:TPU:24 now
where the time goes in v7:
time: 158 us; the launch traced here: 157 us
  blocking collectives  61.3 us (39%)
  starting transfers between devices  47.2 us (30%)
  waiting for transfers between devices  21 us (13%)
  local copies, waits for them, and re-layouts  13.1 us (8%)
  Pallas kernels  6.77 us (4%)
  other arithmetic  6.67 us (4%)
    all_to_all x1, blocking collectives, reduced(): lax.all_to_all(value.reshape(replicas, own_rows, -1), ('yl', 'x'), 0, 0,...  32.6 us
    ppermute x8, starting transfers between devices, step(): return lax.ppermute(value, ('core', 'z'), ways)  21.2 us
    ppermute x8, waiting for transfers between devices, step(): return lax.ppermute(value, ('core', 'z'), ways)  20 us
    all_to_all x1, blocking collectives, body(): fresh = lax.all_to_all(fresh, 'x', 0, 0, tiled=True)  17.3 us
    ppermute x6, starting transfers between devices, swap(): return lax.ppermute(value, axis, [(0, 1), (1, 0)])  15.8 us
    all_to_all x1, blocking collectives, body(): fresh = lax.all_to_all(fresh, 'yl', 0, 0, tiled=True)  11.4 us
    all_to_all x1, starting transfers between devices, body(): acts = lax.all_to_all(acts, 'z', 0, 0, tiled=True)  10.3 us
    unnamed x18, local copies, waits for them, and re-layouts  8.05 us
  transfers between devices with their start and end apart: 15, of which 6 were waited for; matrix products, arithmetic and copies ran while one was open for 8% of the time, Pallas kernels for 4%

profile of v7, /device:TPU:24, one launch (start us, length us, event | category | flops | bytes accessed | tf_op | source)
XLA Modules:
  0.0 157.3 jit_solution(363395762767423143)
XLA Ops:
  1.6 1.9 %collective-permute-start.1 = (bf16[2,192,256]{2,1,0:T(8,128)(2,1)S(1)}, bf16[2,192,256]{2,1,0:T(8,128)(2,1)S(1)}, u32[]{:S(2)}, u32[]{:S(2)}) collective-permute-start(bf16[2,192,256]{2,1,0:T(8,128)(2,1)S(1)} %bitcast.156), channel_id=1, source_target_pairs={{0,128},{128,0},{1,129},{129,1},{2,130},{130,2},{3,131},{131,3},{4... | collective-permute-start | bytes 589832 | tf_op jit(solution)/shard_map/ppermute | solution.py:60
  3.5 5.0 %collective-permute-start.7 = (bf16[2,192,256]{2,1,0:T(8,128)(2,1)S(1)}, bf16[2,192,256]{2,1,0:T(8,128)(2,1)S(1)}, u32[]{:S(2)}, u32[]{:S(2)}) collective-permute-start(bf16[2,192,256]{2,1,0:T(8,128)(2,1)S(1)} %bitcast.157), channel_id=1, source_target_pairs={{0,256},{256,0},{1,257},{257,1},{2,258},{258,2},{3,259},{259,3},{4... | collective-permute-start | bytes 589832 | tf_op jit(solution)/shard_map/ppermute | solution.py:60
  10.9 10.3 %all-to-all-start = ((bf16[8,192,256]{2,1,0:T(8,128)(2,1)}), bf16[8,192,256]{2,1,0:T(8,128)(2,1)S(1)}, u32[]{:S(2)}, u32[]{:S(2)}) async-start(bf16[8,192,256]{2,1,0:T(8,128)(2,1)} %bitcast.150), calls=%async_computation | async-start | bytes 1572864 | tf_op jit(solution)/shard_map/all_to_all | solution.py:84
  21.5 3.9 %collective-permute-start.2 = (bf16[192,1024]{1,0:T(8,128)(2,1)S(1)}, bf16[192,1024]{1,0:T(8,128)(2,1)S(1)}, u32[]{:S(2)}, u32[]{:S(2)}) collective-permute-start(bf16[192,1024]{1,0:T(8,128)(2,1)S(1)} %pad_maximum_fusion.3.rest_0_), channel_id=1, source_target_pairs={{0,16},{16,32},{32,48},{48,64},{64,80},{80,96},{96,112},{112,0},{1... | collective-permute-start | bytes 1179656 | tf_op jit(solution)/shard_map/ppermute | solution.py:65
  25.4 2.5 %collective-permute-start.8 = (bf16[2,192,256]{2,1,0:T(8,128)(2,1)S(1)}, bf16[2,192,256]{2,1,0:T(8,128)(2,1)S(1)}, u32[]{:S(2)}, u32[]{:S(2)}) collective-permute-start(bf16[2,192,256]{2,1,0:T(8,128)(2,1)S(1)} %collective-permute-done.7), channel_id=1, source_target_pairs={{0,128},{128,0},{1,129},{129,1},{2,130},{130,2},{3,131},{131,3},{4... | collective-permute-start | bytes 589832 | tf_op jit(solution)/shard_map/ppermute | solution.py:60
  29.2 3.2 %collective-permute-start.9 = (bf16[192,1024]{1,0:T(8,128)(2,1)S(1)}, bf16[192,1024]{1,0:T(8,128)(2,1)S(1)}, u32[]{:S(2)}, u32[]{:S(2)}) collective-permute-start(bf16[192,1024]{1,0:T(8,128)(2,1)S(1)} %pad_maximum_fusion.4.rest_0_), channel_id=1, source_target_pairs={{0,16},{16,32},{32,48},{48,64},{64,80},{80,96},{96,112},{112,0},{1... | collective-permute-start | bytes 1179656 | tf_op jit(solution)/shard_map/ppermute | solution.py:65
  32.3 13.9 %collective-permute-done.2.rest_1_ = bf16[192,1024]{1,0:T(8,128)(2,1)S(1)} collective-permute-done((bf16[192,1024]{1,0:T(8,128)(2,1)S(1)}, bf16[192,1024]{1,0:T(8,128)(2,1)S(1)}, u32[]{:S(2)}, u32[]{:S(2)}) %collective-permute-start.2) | collective-permute-done | bytes 393248 | tf_op jit(solution)/shard_map/ppermute | solution.py:65
  46.3 1.9 %collective-permute-start.3 = (bf16[192,1024]{1,0:T(8,128)(2,1)S(1)}, bf16[192,1024]{1,0:T(8,128)(2,1)}, u32[]{:S(2)}, u32[]{:S(2)}) collective-permute-start(bf16[192,1024]{1,0:T(8,128)(2,1)S(1)} %collective-permute-done.2.rest_1_), channel_id=1, source_target_pairs={{0,16},{16,32},{32,48},{48,64},{64,80},{80,96},{96,112},{112,0},{1... | collective-permute-start | bytes 1179656 | tf_op jit(solution)/shard_map/ppermute | solution.py:65
  48.2 2.3 %collective-permute-done.9.rest_1_ = bf16[192,1024]{1,0:T(8,128)(2,1)S(1)} collective-permute-done((bf16[192,1024]{1,0:T(8,128)(2,1)S(1)}, bf16[192,1024]{1,0:T(8,128)(2,1)S(1)}, u32[]{:S(2)}, u32[]{:S(2)}) %collective-permute-start.9) | collective-permute-done | bytes 393248 | tf_op jit(solution)/shard_map/ppermute | solution.py:65
  50.5 1.9 %collective-permute-start.10 = (bf16[192,1024]{1,0:T(8,128)(2,1)S(1)}, bf16[192,1024]{1,0:T(8,128)(2,1)}, u32[]{:S(2)}, u32[]{:S(2)}) collective-permute-start(bf16[192,1024]{1,0:T(8,128)(2,1)S(1)} %collective-permute-done.9.rest_1_), channel_id=1, source_target_pairs={{0,16},{16,32},{32,48},{48,64},{64,80},{80,96},{96,112},{112,0},{1... | collective-permute-start | bytes 1179656 | tf_op jit(solution)/shard_map/ppermute | solution.py:65
  52.4 3.6 %copy.40 = f32[1,256,2,1024]{3,1,2,0:T(8,128)} copy(f32[1,256,2,1024]{3,2,1,0:T(2,128)} %param.8) | data formatting | bytes 4194304 | tf_op args[2]
  57.2 1.9 %collective-permute-start.4 = (bf16[192,1024]{1,0:T(8,128)(2,1)}, bf16[192,1024]{1,0:T(8,128)(2,1)S(1)}, u32[]{:S(2)}, u32[]{:S(2)}) collective-permute-start(bf16[192,1024]{1,0:T(8,128)(2,1)} %collective-permute-done.3.rest_2_), channel_id=1, source_target_pairs={{0,16},{16,32},{32,48},{48,64},{64,80},{80,96},{96,112},{112,0},{1... | collective-permute-start | bytes 1179656 | tf_op jit(solution)/shard_map/ppermute | solution.py:65
  59.1 2.3 %collective-permute-done.10.rest_2_ = bf16[192,1024]{1,0:T(8,128)(2,1)} collective-permute-done((bf16[192,1024]{1,0:T(8,128)(2,1)S(1)}, bf16[192,1024]{1,0:T(8,128)(2,1)}, u32[]{:S(2)}, u32[]{:S(2)}) %collective-permute-start.10) | collective-permute-done | bytes 393248 | tf_op jit(solution)/shard_map/ppermute | solution.py:65
  61.4 1.9 %collective-permute-start.11 = (bf16[192,1024]{1,0:T(8,128)(2,1)}, bf16[192,1024]{1,0:T(8,128)(2,1)S(1)}, u32[]{:S(2)}, u32[]{:S(2)}) collective-permute-start(bf16[192,1024]{1,0:T(8,128)(2,1)} %collective-permute-done.10.rest_2_), channel_id=1, source_target_pairs={{0,16},{16,32},{32,48},{48,64},{64,80},{80,96},{96,112},{112,0},{1... | collective-permute-start | bytes 1179656 | tf_op jit(solution)/shard_map/ppermute | solution.py:65
  63.4 1.9 %collective-permute-start = (bf16[8,192,256]{2,1,0:T(8,128)(2,1)S(1)}, bf16[8,192,256]{2,1,0:T(8,128)(2,1)S(1)}, u32[]{:S(2)}, u32[]{:S(2)}) collective-permute-start(bf16[8,192,256]{2,1,0:T(8,128)(2,1)S(1)} %all-to-all-done.acts), channel_id=1, source_target_pairs={{0,128},{128,0},{1,129},{129,1},{2,130},{130,2},{3,131},{131,3},{4... | collective-permute-start | bytes 2359304 | tf_op jit(solution)/shard_map/ppermute | solution.py:60
  65.3 1.8 %slice_select_fusion = (f32[2,256,512]{2,1,0:T(8,128)S(1)}, f32[2,256,512]{2,1,0:T(8,128)S(1)}) fusion(f32[2,256,1024]{2,1,0:T(8,128)} %bitcast.152, pred[]{:T(512)S(6)} %not.3, pred[]{:T(512)S(6)} %eq.12), kind=kLoop, calls=%fused_computation.7 | loop fusion | flops 524288 | bytes 4194306 | tf_op jit(solution)/shard_map/jit(_where)/select_n | solution.py:99
  69.0 3.3 %collective-permute-start.5 = (bf16[96,1024]{1,0:T(8,128)(2,1)}, bf16[96,1024]{1,0:T(8,128)(2,1)}, u32[]{:S(2)}, u32[]{:S(2)}) collective-permute-start(bf16[96,1024]{1,0:T(8,128)(2,1)} %slice.220), channel_id=1, source_target_pairs={{0,16},{16,32},{32,48},{48,64},{64,80},{80,96},{96,112},{112,0},{1... | collective-permute-start | bytes 589832 | tf_op jit(solution)/shard_map/ppermute | solution.py:65
  73.2 3.1 %collective-permute-start.12 = (bf16[96,1024]{1,0:T(8,128)(2,1)}, bf16[96,1024]{1,0:T(8,128)(2,1)}, u32[]{:S(2)}, u32[]{:S(2)}) collective-permute-start(bf16[96,1024]{1,0:T(8,128)(2,1)} %slice.233), channel_id=1, source_target_pairs={{0,16},{16,32},{32,48},{48,64},{64,80},{80,96},{96,112},{112,0},{1... | collective-permute-start | bytes 589832 | tf_op jit(solution)/shard_map/ppermute | solution.py:65
  80.6 2.5 %collective-permute-start.6 = (f32[256,1024]{1,0:T(8,128)S(1)}, f32[256,1024]{1,0:T(8,128)S(1)}, u32[]{:S(2)}, u32[]{:S(2)}) collective-permute-start(f32[256,1024]{1,0:T(8,128)S(1)} %token_half_product.5), channel_id=1, source_target_pairs={{0,128},{128,0},{1,129},{129,1},{2,130},{130,2},{3,131},{131,3},{4... | collective-permute-start | bytes 3145736 | tf_op jit(solution)/shard_map/ppermute | solution.py:60
  84.7 1.9 %collective-permute-start.13 = (f32[256,1024]{1,0:T(8,128)S(1)}, f32[256,1024]{1,0:T(8,128)S(1)}, u32[]{:S(2)}, u32[]{:S(2)}) collective-permute-start(f32[256,1024]{1,0:T(8,128)S(1)} %token_half_product.7), channel_id=1, source_target_pairs={{0,128},{128,0},{1,129},{129,1},{2,130},{130,2},{3,131},{131,3},{4... | collective-permute-start | bytes 3145736 | tf_op jit(solution)/shard_map/ppermute | solution.py:60
  91.3 32.6 %all_to_all.20 = f16[16,16,2048]{2,1,0:T(8,128)(2,1)S(1)} all-to-all(f16[16,16,2048]{2,1,0:T(8,128)(2,1)S(1)} %bitcast.153), channel_id=1, replica_groups=mesh['yh'=2,'core'=2,'z'=8,'yl'=4,'x'=4] {'yl','x'}, dimensions={0} | all-to-all | bytes 2097152 | tf_op jit(solution)/shard_map/all_to_all | solution.py:109
  125.4 11.4 %all_to_all.21 = bf16[4,16,2,1024]{3,2,1,0:T(2,128)(2,1)S(1)} all-to-all(bf16[4,16,2,1024]{3,2,1,0:T(2,128)(2,1)S(1)} %broadcast_in_dim.7), channel_id=1, replica_groups=mesh['yh'=2,'core'=2,'z'=8,'yl'=4,'x'=4] {'yl'}, dimensions={0} | all-to-all | bytes 524288 | tf_op jit(solution)/shard_map/all_to_all | solution.py:124
  137.6 17.3 %all_to_all.22 = bf16[4,4,16,2,1024]{4,3,2,1,0:T(2,128)(2,1)S(1)} all-to-all(bf16[4,4,16,2,1024]{4,3,2,1,0:T(2,128)(2,1)S(1)} %broadcast_in_dim.8), channel_id=1, replica_groups=mesh['yh'=2,'core'=2,'z'=8,'yl'=4,'x'=4] {'x'}, dimensions={0} | all-to-all | bytes 2097152 | tf_op jit(solution)/shard_map/all_to_all | solution.py:126
  155.2 2.1 %copy.33 = bf16[256,2,1024]{2,1,0:T(2,128)(2,1)} copy(bf16[256,2,1024]{2,0,1:T(8,128)(2,1)S(1)} %bitcast.154) | data formatting | bytes 2097152
  (60 shorter events, 21.7 us)
Async XLA Ops:
  1.6 19.7 %collective-permute-start.1 = (bf16[2,192,256]{2,1,0:T(8,128)(2,1)S(1)}, bf16[2,192,256]{2,1,0:T(8,128)(2,1)S(1)}, u32[]{:S(2)}, u32[]{:S(2)}) collective-permute-start(bf16[2,192,256]{2,1,0:T(8,128)(2,1)S(1)} %bitcast.156), channel_id=1, source_target_pairs={{0,128},{128,0},{1,129},{129,1},{2,130},{130,2},{3,131},{131,3},{4... | collective-permute-start | bytes 589832 | tf_op jit(solution)/shard_map/ppermute | solution.py:60
  3.5 21.9 %collective-permute-start.7 = (bf16[2,192,256]{2,1,0:T(8,128)(2,1)S(1)}, bf16[2,192,256]{2,1,0:T(8,128)(2,1)S(1)}, u32[]{:S(2)}, u32[]{:S(2)}) collective-permute-start(bf16[2,192,256]{2,1,0:T(8,128)(2,1)S(1)} %bitcast.157), channel_id=1, source_target_pairs={{0,256},{256,0},{1,257},{257,1},{2,258},{258,2},{3,259},{259,3},{4... | collective-permute-start | bytes 589832 | tf_op jit(solution)/shard_map/ppermute | solution.py:60
  10.9 52.4 %all-to-all-start = ((bf16[8,192,256]{2,1,0:T(8,128)(2,1)}), bf16[8,192,256]{2,1,0:T(8,128)(2,1)S(1)}, u32[]{:S(2)}, u32[]{:S(2)}) async-start(bf16[8,192,256]{2,1,0:T(8,128)(2,1)} %bitcast.150), calls=%async_computation | async-start | bytes 1572864 | tf_op jit(solution)/shard_map/all_to_all | solution.py:84
  21.5 24.8 %collective-permute-start.2 = (bf16[192,1024]{1,0:T(8,128)(2,1)S(1)}, bf16[192,1024]{1,0:T(8,128)(2,1)S(1)}, u32[]{:S(2)}, u32[]{:S(2)}) collective-permute-start(bf16[192,1024]{1,0:T(8,128)(2,1)S(1)} %pad_maximum_fusion.3.rest_0_), channel_id=1, source_target_pairs={{0,16},{16,32},{32,48},{48,64},{64,80},{80,96},{96,112},{112,0},{1... | collective-permute-start | bytes 1179656 | tf_op jit(solution)/shard_map/ppermute | solution.py:65
  25.4 3.6 %collective-permute-start.8 = (bf16[2,192,256]{2,1,0:T(8,128)(2,1)S(1)}, bf16[2,192,256]{2,1,0:T(8,128)(2,1)S(1)}, u32[]{:S(2)}, u32[]{:S(2)}) collective-permute-start(bf16[2,192,256]{2,1,0:T(8,128)(2,1)S(1)} %collective-permute-done.7), channel_id=1, source_target_pairs={{0,128},{128,0},{1,129},{129,1},{2,130},{130,2},{3,131},{131,3},{4... | collective-permute-start | bytes 589832 | tf_op jit(solution)/shard_map/ppermute | solution.py:60
  29.2 21.3 %collective-permute-start.9 = (bf16[192,1024]{1,0:T(8,128)(2,1)S(1)}, bf16[192,1024]{1,0:T(8,128)(2,1)S(1)}, u32[]{:S(2)}, u32[]{:S(2)}) collective-permute-start(bf16[192,1024]{1,0:T(8,128)(2,1)S(1)} %pad_maximum_fusion.4.rest_0_), channel_id=1, source_target_pairs={{0,16},{16,32},{32,48},{48,64},{64,80},{80,96},{96,112},{112,0},{1... | collective-permute-start | bytes 1179656 | tf_op jit(solution)/shard_map/ppermute | solution.py:65
  46.3 11.0 %collective-permute-start.3 = (bf16[192,1024]{1,0:T(8,128)(2,1)S(1)}, bf16[192,1024]{1,0:T(8,128)(2,1)}, u32[]{:S(2)}, u32[]{:S(2)}) collective-permute-start(bf16[192,1024]{1,0:T(8,128)(2,1)S(1)} %collective-permute-done.2.rest_1_), channel_id=1, source_target_pairs={{0,16},{16,32},{32,48},{48,64},{64,80},{80,96},{96,112},{112,0},{1... | collective-permute-start | bytes 1179656 | tf_op jit(solution)/shard_map/ppermute | solution.py:65
  50.5 5.5 %copy-start = (bf16[192,1024]{1,0:T(8,128)(2,1)}, bf16[192,1024]{1,0:T(8,128)(2,1)S(1)}, u32[]{:S(2)}) copy-start(bf16[192,1024]{1,0:T(8,128)(2,1)S(1)} %collective-permute-done.9.rest_1_) | copy-start | bytes 1179652
  50.5 11.0 %collective-permute-start.10 = (bf16[192,1024]{1,0:T(8,128)(2,1)S(1)}, bf16[192,1024]{1,0:T(8,128)(2,1)}, u32[]{:S(2)}, u32[]{:S(2)}) collective-permute-start(bf16[192,1024]{1,0:T(8,128)(2,1)S(1)} %collective-permute-done.9.rest_1_), channel_id=1, source_target_pairs={{0,16},{16,32},{32,48},{48,64},{64,80},{80,96},{96,112},{112,0},{1... | collective-permute-start | bytes 1179656 | tf_op jit(solution)/shard_map/ppermute | solution.py:65
  57.2 11.1 %collective-permute-start.4 = (bf16[192,1024]{1,0:T(8,128)(2,1)}, bf16[192,1024]{1,0:T(8,128)(2,1)S(1)}, u32[]{:S(2)}, u32[]{:S(2)}) collective-permute-start(bf16[192,1024]{1,0:T(8,128)(2,1)} %collective-permute-done.3.rest_2_), channel_id=1, source_target_pairs={{0,16},{16,32},{32,48},{48,64},{64,80},{80,96},{96,112},{112,0},{1... | collective-permute-start | bytes 1179656 | tf_op jit(solution)/shard_map/ppermute | solution.py:65
  61.4 11.1 %collective-permute-start.11 = (bf16[192,1024]{1,0:T(8,128)(2,1)}, bf16[192,1024]{1,0:T(8,128)(2,1)S(1)}, u32[]{:S(2)}, u32[]{:S(2)}) collective-permute-start(bf16[192,1024]{1,0:T(8,128)(2,1)} %collective-permute-done.10.rest_2_), channel_id=1, source_target_pairs={{0,16},{16,32},{32,48},{48,64},{64,80},{80,96},{96,112},{112,0},{1... | collective-permute-start | bytes 1179656 | tf_op jit(solution)/shard_map/ppermute | solution.py:65
  63.4 15.5 %collective-permute-start = (bf16[8,192,256]{2,1,0:T(8,128)(2,1)S(1)}, bf16[8,192,256]{2,1,0:T(8,128)(2,1)S(1)}, u32[]{:S(2)}, u32[]{:S(2)}) collective-permute-start(bf16[8,192,256]{2,1,0:T(8,128)(2,1)S(1)} %all-to-all-done.acts), channel_id=1, source_target_pairs={{0,128},{128,0},{1,129},{129,1},{2,130},{130,2},{3,131},{131,3},{4... | collective-permute-start | bytes 2359304 | tf_op jit(solution)/shard_map/ppermute | solution.py:60
  69.0 9.8 %collective-permute-start.5 = (bf16[96,1024]{1,0:T(8,128)(2,1)}, bf16[96,1024]{1,0:T(8,128)(2,1)}, u32[]{:S(2)}, u32[]{:S(2)}) collective-permute-start(bf16[96,1024]{1,0:T(8,128)(2,1)} %slice.220), channel_id=1, source_target_pairs={{0,16},{16,32},{32,48},{48,64},{64,80},{80,96},{96,112},{112,0},{1... | collective-permute-start | bytes 589832 | tf_op jit(solution)/shard_map/ppermute | solution.py:65
  73.2 9.8 %collective-permute-start.12 = (bf16[96,1024]{1,0:T(8,128)(2,1)}, bf16[96,1024]{1,0:T(8,128)(2,1)}, u32[]{:S(2)}, u32[]{:S(2)}) collective-permute-start(bf16[96,1024]{1,0:T(8,128)(2,1)} %slice.233), channel_id=1, source_target_pairs={{0,16},{16,32},{32,48},{48,64},{64,80},{80,96},{96,112},{112,0},{1... | collective-permute-start | bytes 589832 | tf_op jit(solution)/shard_map/ppermute | solution.py:65
  78.8 4.2 %copy-start.1 = (bf16[192,1024]{1,0:T(8,128)(2,1)S(1)}, bf16[192,1024]{1,0:T(8,128)(2,1)}, u32[]{:S(2)}) copy-start(bf16[192,1024]{1,0:T(8,128)(2,1)} %copy-done) | copy-start | bytes 1179652
  80.6 6.1 %copy-start.5 = (s32[1,2]{1,0:T(1,128)S(1)}, s32[1,2]{1,0:T(1,128)}, u32[]{:S(2)}) copy-start(s32[1,2]{1,0:T(1,128)} %param.9) | copy-start | bytes 28
  80.6 9.6 %collective-permute-start.6 = (f32[256,1024]{1,0:T(8,128)S(1)}, f32[256,1024]{1,0:T(8,128)S(1)}, u32[]{:S(2)}, u32[]{:S(2)}) collective-permute-start(f32[256,1024]{1,0:T(8,128)S(1)} %token_half_product.5), channel_id=1, source_target_pairs={{0,128},{128,0},{1,129},{129,1},{2,130},{130,2},{3,131},{131,3},{4... | collective-permute-start | bytes 3145736 | tf_op jit(solution)/shard_map/ppermute | solution.py:60
  84.7 5.5 %collective-permute-start.13 = (f32[256,1024]{1,0:T(8,128)S(1)}, f32[256,1024]{1,0:T(8,128)S(1)}, u32[]{:S(2)}, u32[]{:S(2)}) collective-permute-start(f32[256,1024]{1,0:T(8,128)S(1)} %token_half_product.7), channel_id=1, source_target_pairs={{0,128},{128,0},{1,129},{129,1},{2,130},{130,2},{3,131},{131,3},{4... | collective-permute-start | bytes 3145736 | tf_op jit(solution)/shard_map/ppermute | solution.py:60
  88.4 1.8 %copy-start.2 = (f32[256,1024]{1,0:T(8,128)S(1)}, f32[256,1024]{1,0:T(8,128)}, u32[]{:S(2)}) copy-start(f32[256,1024]{1,0:T(8,128)} %pad_maximum_fusion) | copy-start | bytes 3145732
  91.3 33.0 %copy-start.3 = (f32[16,2,1024]{2,1,0:T(2,128)S(1)}, f32[16,2,1024]{2,1,0:T(2,128)}, u32[]{:S(2)}) copy-start(f32[16,2,1024]{2,1,0:T(2,128)} %param.10) | copy-start | bytes 393220
  91.3 33.0 %copy-start.4 = (f32[16,2,1024]{2,1,0:T(2,128)S(1)}, f32[16,2,1024]{2,1,0:T(2,128)}, u32[]{:S(2)}) copy-start(f32[16,2,1024]{2,1,0:T(2,128)} %param.11) | copy-start | bytes 393220
